TPU v7x, 32 devices: a whole 2x2x4 slice. The times are simulated.
32 devices in a mesh: dom: 16 (over z, x, core), feat: 2 (over y).
Axes of the slice: x: 2, y: 2, z: 4, core: 2. Of those that a mesh axis runs over, the one named last changes fastest.
Arguments:
- features: float32 [16384, 512], P('dom', 'feat'), may hold values from -6 to 6
- weight: float32 [512, 512], P(None, 'feat'), may hold values from -0.25 to 0.25
- cotangent: float32 [16384, 512], P('dom', 'feat'), may hold values from -6 to 6
- block_rows: int32 [16, 4, 24], P('dom'), may hold values from 0 to 7, as said below
- block_cols: int32 [16, 4, 24], P('dom'), may hold values from 0 to 7, as said below
- block_counts: int32 [16, 4], P('dom'), may hold values from 1 to 24, as said below
- block_values: float32 [16, 4, 24, 128, 128], P('dom'), may hold values from -0.25 to 0.25
Outputs:
- activated: float32 [16384, 512], P('dom', 'feat')
- feature_grad: float32 [16384, 512], P('dom', 'feat')
- weight_grad: float32 [512, 512], P(None, 'feat')
Inputs may be any that keep to these rules, and one draw needn't show every extreme that they name: `block_rows`: every entry is below 8; within one partition and slot the pairs (block_rows, block_cols) are all different. `block_cols`: every entry is below 8. `block_counts`: some partition has 24 blocks in every slot.
All inputs are finite; a program needn't handle non-finite values.
Results may differ from a plain program's by a relative error of at most 0.0003.
Values sent between devices are 32-bit elements; how exact they have to be, the bound alone decides.
No kernel may reach another device: no remote copies, remote signals or barrier semaphores. Data moves between devices by JAX's collectives and lax.ppermute only.
A program may use at most 128 MiB of HBM per device.

v0:
```python
import functools
import math

import jax
import jax.numpy as jnp
from jax import lax
from jax.experimental import pallas as pl
from jax.experimental.pallas import tpu as pltpu
from jax.sharding import PartitionSpec as P

F32 = jnp.float32
BF16 = jnp.bfloat16
TILE = 256
LIMIT = 8 * 1024 * 1024
IN_VMEM = pl.BlockSpec(memory_space=pltpu.VMEM)
IN_SMEM = pl.BlockSpec(memory_space=pltpu.SMEM)

SIDE, CORE, NEAR, FAR, TWO, OWN, CHIP, LAYER = range(8)


def split(value):
    high = value.astype(BF16)
    low = (value - high.astype(F32)).astype(BF16)
    return high, low


def mm(a, b, dims=((1,), (0,))):
    return lax.dot_general(a, b, (dims, ((), ())), preferred_element_type=F32)


def mm3(a, b, dims=((1,), (0,))):
    (ah, al), (bh, bl) = a, b
    return mm(ah, bh, dims) + (mm(ah, bl, dims) + mm(al, bh, dims))


def call(name, kernel, who, operands, shapes, scratch=(), flops=0, place=pltpu.VMEM):
    moved = sum(a.size * a.dtype.itemsize for a in operands)
    pinned = [pltpu.with_memory_space_constraint(a, pltpu.VMEM) for a in operands]
    return pl.pallas_call(
        kernel,
        in_specs=[IN_SMEM] + [IN_VMEM] * len(operands),
        out_specs=[IN_VMEM] * len(shapes),
        out_shape=[place(*shape) for shape in shapes],
        scratch_shapes=list(scratch),
        compiler_params=pltpu.CompilerParams(vmem_limit_bytes=LIMIT),
        cost_estimate=pl.CostEstimate(flops=int(flops), bytes_accessed=moved, transcendentals=0),
        name=name,
    )(who, *pinned)


def lay_out_kernel(rows, cols, counts, who, blocks, a, t):
    slot = pl.program_id(0)
    cap = blocks.shape[1]
    size = blocks.shape[2]
    for out in (a, t):
        for part in range(2):
            out[part, slot] = jnp.zeros(out.shape[2:], out.dtype)

    def one(k, carry):
        r = pl.multiple_of(rows[slot, k] * size, size)
        c = pl.multiple_of(cols[slot, k] * size, size)
        block = blocks[0, k]
        for part, value in enumerate(split(block)):
            a[part, slot, pl.ds(r, size), pl.ds(c, size)] = value
        for part, value in enumerate(split(block.T)):
            t[part, slot, pl.ds(c, size), pl.ds(r, size)] = value
        return carry

    lax.fori_loop(0, jnp.minimum(counts[0, slot], cap), one, 0)


def lay_out(rows, cols, counts, who, blocks, size_all):
    window, cap, size, _ = blocks.shape
    shape = pltpu.VMEM((2, window, size_all, size_all), BF16)
    return pl.pallas_call(
        lay_out_kernel,
        grid_spec=pltpu.PrefetchScalarGridSpec(
            num_scalar_prefetch=4,
            grid=(window,),
            in_specs=[pl.BlockSpec((1, cap, size, size), lambda s, *_: (s, 0, 0, 0))],
            out_specs=[IN_VMEM] * 2,
        ),
        out_shape=[shape] * 2,
        compiler_params=pltpu.CompilerParams(vmem_limit_bytes=LIMIT),
        cost_estimate=pl.CostEstimate(flops=0, bytes_accessed=20_000_000, transcendentals=0),
        name="lay_out",
    )(rows, cols, counts, who, pltpu.with_memory_space_constraint(blocks, pltpu.HBM))


def forward_kernel(slots, part, has_base, who, matrix, *refs):
    n = len(slots)
    sources, refs = refs[:n], refs[n:]
    base, refs = (refs[0], refs[1:]) if has_base else (None, refs)
    out, (highs, lows) = refs[0], refs[1:]
    rows = out.shape[0]
    from_row = 0 if part is None else (who[SIDE] ^ part) * rows
    for i, source in enumerate(sources):
        highs[i], lows[i] = split(source[...])

    def tile(k, carry):
        there = pl.ds(pl.multiple_of(k * TILE, TILE), TILE)
        here = pl.ds(pl.multiple_of(from_row + k * TILE, TILE), TILE)
        total = None
        if base is not None:
            total = base[here if base.shape[0] > rows else there, :]
        for i, slot in enumerate(slots):
            at = who[slot]
            term = mm3((matrix[0, at, here, :], matrix[1, at, here, :]), (highs[i], lows[i]))
            total = term if total is None else total + term
        out[there, :] = total
        return carry

    lax.fori_loop(0, rows // TILE, tile, 0)


def forward(name, who, matrix, terms, base=None, part=None):
    slots = [slot for slot, _ in terms]
    sources = [source for _, source in terms]
    depth, width = sources[0].shape
    rows = matrix.shape[2] // (1 if part is None else 2)
    extra = [] if base is None else [base]
    return call(
        name,
        functools.partial(forward_kernel, slots, part, base is not None),
        who,
        [matrix, *sources, *extra],
        [((rows, width), F32)],
        [pltpu.VMEM((len(terms), depth, width), BF16)] * 2,
        6 * len(terms) * rows * depth * width,
    )[0]


def backward_kernel(slots, part, n_add, first, pieces, who, matrix, source, *refs):
    addends, outs = refs[:n_add], refs[n_add:]
    depth = source.shape[0]
    parts = split(source[...])
    deep = pl.ds(pl.multiple_of((who[SIDE] ^ part) * depth, depth), depth)
    size = outs[0].shape[0]
    here = pl.ds(first, size * pieces)
    for i, slot in enumerate(slots):
        at = who[slot]
        total = mm3((matrix[0, at, here, deep], matrix[1, at, here, deep]), parts)
        for addend in addends:
            total = total + addend[here, :]
        for k in range(pieces):
            outs[i * pieces + k][...] = total[k * size : (k + 1) * size, :]


def backward(name, who, matrix, slots, source, addends, part, first=0, rows=None, pieces=1):
    depth, width = source.shape
    rows = rows or matrix.shape[2]
    return call(
        name,
        functools.partial(backward_kernel, slots, part, len(addends), first, pieces),
        who,
        [matrix, source, *addends],
        [((rows // pieces, width), F32)] * (len(slots) * pieces),
        flops=6 * len(slots) * rows * depth * width,
    )


def middle_kernel(who, own, far, w_here, w_there, cot, cot_there, *outs):
    act_here, act_there, grad_here, grad_there, g_there = outs
    half = own.shape[1]

    def rows_of(w, which):
        return split(w[pl.ds(pl.multiple_of((who[SIDE] ^ which) * half, half), half), :])

    rows = own.shape[0]
    cot_here = cot.at[pl.ds(pl.multiple_of(who[SIDE] * rows, rows), rows), :]
    source = split(own[...]), split(far[...])
    total = None
    for w, cot, act, grad in (
        (w_here, cot_here, act_here, grad_here),
        (w_there, cot_there, act_there, grad_there),
    ):
        pre = mm3(source[0], rows_of(w, 0)) + mm3(source[1], rows_of(w, 1))
        s = 1.0 / (1.0 + jnp.exp(-pre))
        act[...] = pre * s
        pg = cot[...] * (s + pre * s * (1.0 - s))
        grad[...] = pg
        term = mm3(split(pg), rows_of(w, 1), ((1,), (1,)))
        total = term if total is None else total + term
    g_there[...] = total


def middle(who, own, far, w_here, w_there, cot, cot_there):
    shape = (cot_there.shape, F32)
    flops = 36 * own.shape[0] * own.shape[1] * w_here.shape[1]
    operands = [own, far, w_here, w_there, cot, cot_there]
    return call("middle", middle_kernel, who, operands, [shape] * 5, flops=flops)


def keep_kernel(who, w_here, w_there, grad_here, grad_there, g_here):
    half = g_here.shape[1]
    at = pl.ds(pl.multiple_of(who[SIDE] * half, half), half)
    total = None
    for w, grad in ((w_here, grad_here), (w_there, grad_there)):
        term = mm3(split(grad[...]), split(w[at, :]), ((1,), (1,)))
        total = term if total is None else total + term
    g_here[...] = total


def weight_kernel(scale, which, who, own, far, grad_here, grad_there, here, there):
    mine = who[SIDE] == (who[CORE] ^ which)
    turned = split(jnp.where(mine, own[...], far[...]).T)
    for grad, out in ((grad_here, here), (grad_there, there)):
        out[...] = mm3(turned, split(grad[...])) * scale


def weight_term(name, who, scale, which, own, far, grad_here, grad_there):
    rows, half = own.shape
    hidden = grad_here.shape[1]
    return call(
        name,
        functools.partial(weight_kernel, scale, which),
        who,
        [own, far, grad_here, grad_there],
        [((half, hidden), F32)] * 2,
        flops=12 * rows * half * hidden,
    )


def half_kernel(which, who, whole, out):
    rows = out.shape[0]
    out[...] = whole[pl.ds(pl.multiple_of((who[SIDE] ^ which) * rows, rows), rows), :]


def join_kernel(place, who, *refs):
    parts, out = refs[:-1], refs[-1]
    rows = parts[0].shape[0]
    for k, part in enumerate(parts):
        out[pl.ds(pl.multiple_of((who[place] ^ k) * rows, rows), rows), :] = part[...]


def join(name, who, place, parts, kind=pltpu.VMEM):
    rows, cols = parts[0].shape
    shape = (rows * len(parts), cols)
    return call(
        name, functools.partial(join_kernel, place), who, parts, [(shape, F32)], place=kind
    )[0]


def pick_kernel(who, ready, later, ready_sent, later_sent, out):
    rows = ready.shape[0]
    odd = who[CHIP] == 1
    for which, one, other in ((0, ready, ready_sent), (1, later, later_sent)):
        at = pl.ds(pl.multiple_of((who[LAYER] ^ which) * rows, rows), rows)
        out[at, :] = jnp.where(odd, one[...], other[...])


def pick(name, who, *parts):
    rows, cols = parts[0].shape
    return call(name, pick_kernel, who, parts, [((2 * rows, cols), F32)])[0]


def hand_out(full, outs, place):
    rows = outs[0].shape[0]
    for k, out in enumerate(outs):
        out[...] = full[pl.ds(pl.multiple_of((place ^ k) * rows, rows), rows), :]


def side_kernel(who, one, two, three, keep, give, full):
    full[...] = one[...] + two[...] + three[...]
    hand_out(full, (keep, give), who[LAYER])


def side_sum(name, who, *parts):
    rows, cols = parts[0].shape
    shape = ((rows // 2, cols), F32)
    return call(name, side_kernel, who, parts, [shape] * 2, [pltpu.VMEM((rows, cols), F32)])


def add_kernel(who, *refs):
    total = refs[0][...]
    for ref in refs[1:-1]:
        total = total + ref[...]
    refs[-1][...] = total


def add(name, who, *parts):
    return call(name, add_kernel, who, parts, [(parts[0].shape, F32)])[0]


def moved(value, axis, even, odd):
    peers = lax.axis_size(axis)
    perm = [(i, (i + (odd if i % 2 else even)) % peers) for i in range(peers)]
    return lax.ppermute(value, axis, perm)


def chosen(value, axis, target):
    peers = lax.axis_size(axis)
    pairs = [(i, target(i)) for i in range(peers)]
    return lax.ppermute(value, axis, [pair for pair in pairs if pair[1] is not None])


def swapped(value, axis):
    return chosen(value, axis, lambda i: i ^ 1)


def after(value, *others):
    return lax.optimization_barrier((value, *others))[0]


def body(features, weight, cotangent, block_rows, block_cols, block_counts, block_values):
    rows, width = features.shape
    hidden = weight.shape[1]
    depth = weight.shape[0]
    parts = lax.axis_size("dom")
    side = lax.axis_index("feat").astype(jnp.int32)
    place = lax.axis_index("dom").astype(jnp.int32)
    odd = place & 1
    zero = place * 0
    who = jnp.stack([side, odd, 1 + 2 * odd, 3 - 2 * odd, zero + 2, zero, (place >> 1) & 1,
                     (place >> 2) & 1])

    near = moved(features, "dom", 3, 1)
    far = moved(features, "dom", 1, 3)
    w_there = swapped(weight, "feat")
    half_shape = ((rows // 2, hidden), F32)
    cot_give = call("cot_give", functools.partial(half_kernel, 1), who, [cotangent], [half_shape])[0]
    cot_there = swapped(cot_give, "feat")

    a, t = lay_out(
        block_rows[0], block_cols[0], block_counts, who, block_values[0], rows
    )
    total = forward("agg_own", who, a, [(OWN, features)])
    near = after(near, total, w_there, cot_there)
    two = swapped(near, "dom")
    total = forward("agg_near", who, a, [(NEAR, near)], total)
    far = after(far, total)
    give = forward("agg_give", who, a, [(FAR, far), (TWO, two)], total, 1)
    there = swapped(give, "feat")
    keep = forward("agg_keep", who, a, [(FAR, far), (TWO, after(two, give))], total, 0)

    act_here, act_there, grad_here, grad_there, g_give = middle(
        who, keep, there, weight, w_there, cotangent, cot_there
    )
    g_there = swapped(g_give, "feat")
    scale = 1.0 / math.sqrt(rows * parts)
    w_give = weight_term("weight_give", who, scale, 1, keep, there, grad_here, grad_there)
    w_keep = weight_term(
        "weight_keep", who, scale, 0, after(keep, w_give[0]), there, grad_here, grad_there
    )
    quick = parts == 16
    steps = weight_sum(who, w_keep, w_give, quick)

    last = next(steps)(grad_here)
    last = next(steps)(last)
    g_here = call(
        "keep",
        keep_kernel,
        who,
        [weight, w_there, after(grad_here, last), grad_there],
        [(keep.shape, F32)],
        flops=12 * rows // 2 * width * hidden,
    )[0]
    firsts = backward("back_here", who, t, [TWO, FAR, NEAR, OWN], after(g_here, last), [], 0)
    last = next(steps)(firsts[0])
    g_there = after(g_there, last)
    last = backward("back_two", who, t, [TWO], g_there, [firsts[0]], 1)[0]
    two = swapped(last, "dom")
    last = backward("back_far", who, t, [FAR], after(g_there, last), [firsts[1]], 1)[0]
    far = moved(last, "dom", -3, -1)
    last = backward("back_near", who, t, [NEAR], after(g_there, last), [firsts[2], two], 1)[0]
    near = moved(last, "dom", -1, -3)
    last = next(steps)(last)
    act_got = swapped(after(act_there, last), "feat")
    mine = backward("back_own", who, t, [OWN], after(g_there, last), [firsts[3]], 1)[0]
    last = next(steps)(mine, far)
    last = next(steps)(last)
    activated = join("activated", who, SIDE, [after(act_here, last), act_got], jax.ShapeDtypeStruct)
    last = next(steps)(activated)
    feature_grad = call(
        "feature_grad",
        add_kernel,
        who,
        [after(mine, last), far, near],
        [(features.shape, F32)],
        place=jax.ShapeDtypeStruct,
    )[0]
    weight_grad = next(steps)(feature_grad)
    return (activated, feature_grad, weight_grad)


def weight_sum(who, keep, give, quick):
    if not quick:
        here, there = (join("core_join", who, CORE, pair) for pair in zip(keep, give))
        total = lax.psum(here + swapped(there, "feat"), "dom")
        for _ in range(7):
            yield lambda *last: last[0]
        yield lambda *last: total
        return
    box = []

    def step(run):
        def go(*last):
            box.append(run(*last))
            return box[-1][0] if isinstance(box[-1], (list, tuple)) else box[-1]

        return go

    def up(value):
        return chosen(value, "dom", lambda i: i + 2 if i % 4 < 2 else None)

    gots = [swapped(value, "dom") for value in give]
    yield step(lambda *last: add("core_there", who, after(keep[1], *last), gots[1]))
    there = box[-1]
    yield step(lambda *last: add("core_here", who, after(keep[0], *last), gots[0]))
    here = box[-1]
    got = up(there)
    yield step(lambda *last: add("chip_there", who, after(there, *last), got))
    got = swapped(box[-1], "feat")
    also = up(here)
    yield step(lambda *last: side_sum("side_sum", who, after(here, *last), also, got)[::-1])
    give, keep = box[-1]
    for name, bit in (("layer_sum", 4), ("pair_sum", 8)):
        got = chosen(give, "dom", lambda i: i ^ bit if i % 4 >= 2 else None)
        yield step(lambda *last: add(name, who, after(keep, *last), got))
        keep = give = box[-1]
    later_sent = chosen(keep, "dom", lambda i: (i ^ 4) - 2 if i % 4 >= 2 else None)
    later = chosen(keep, "dom", lambda i: i ^ 4 if i % 4 >= 2 else None)
    ready_sent = chosen(keep, "dom", lambda i: i - 2 if i % 4 >= 2 else None)
    yield step(
        lambda *last: pick("chip_pick", who, after(keep, *last), later, ready_sent, later_sent)
    )
    got = swapped(box[-1], "dom")
    yield step(
        lambda *last: join("weight_grad", who, CORE, [after(box[-1], *last), got], jax.ShapeDtypeStruct)
    )


def solution(mesh):
    in_specs = (
        P("dom", "feat"),
        P(None, "feat"),
        P("dom", "feat"),
        P("dom", None, None),
        P("dom", None, None),
        P("dom", None),
        P("dom", None, None, None, None),
    )
    out_specs = (P("dom", "feat"), P("dom", "feat"), P(None, "feat"))
    return jax.shard_map(body, mesh=mesh, in_specs=in_specs, out_specs=out_specs, check_vma=False)
```

profile of v0, /device:TPU:0, one launch (start us, length us, event | category | flops | bytes accessed | tf_op | source)
XLA Modules:
  0.0 119.1 jit_solution(10257999754600625731)
XLA Ops:
  0.6 2.4 %collective-permute-start.1 = (f32[1024,256]{1,0:T(8,128)}, f32[1024,256]{1,0:T(8,128)S(1)}, u32[]{:S(2)}, u32[]{:S(2)}) collective-permute-start(f32[1024,256]{1,0:T(8,128)} %refs_0_.1), channel_id=1, source_target_pairs={{0,6},{2,4},{4,10},{6,8},{8,14},{10,12},{12,18},{14,16},{16,22},{1... | collective-permute-start | bytes 3145736 | tf_op jit(solution)/shard_map/ppermute | solution.py:288
  3.1 0.1 stack.27.who
  3.1 1.2 %copy-done = f32[1024,256]{1,0:T(8,128)S(1)} copy-done((f32[1024,256]{1,0:T(8,128)S(1)}, f32[1024,256]{1,0:T(8,128)}, u32[]{:S(2)}) %copy-start) | copy-done | bytes 1048600
  4.4 0.6 cot_give.1
  5.0 1.6 %collective-permute-start.3 = (f32[512,256]{1,0:T(8,128)S(1)}, f32[512,256]{1,0:T(8,128)S(1)}, u32[]{:S(2)}, u32[]{:S(2)}) collective-permute-start(f32[512,256]{1,0:T(8,128)S(1)} %cot_give.1), channel_id=1, source_target_pairs={{0,1},{1,0},{2,3},{3,2},{4,5},{5,4},{6,7},{7,6},{8,9},{9,8},{10,11... | collective-permute-start | bytes 1572872 | tf_op jit(solution)/shard_map/ppermute | solution.py:294
  6.5 0.5 collective-permute-start.2
  7.1 0.1 collective-permute-start
  7.2 0.7 copy-done.4
  7.9 0.7 copy-done.5
  8.6 0.7 copy-done.6
  9.2 7.2 %lay_out.1 = (bf16[2,4,1024,1024]{3,2,1,0:T(8,128)(2,1)S(1)}, bf16[2,4,1024,1024]{3,2,1,0:T(8,128)(2,1)S(1)}) custom-call(s32[4,24]{1,0:T(4,128)S(1)} %bitcast.9, s32[4,24]{1,0:T(4,128)S(1)} %bitcast.10, s32[1,4]{1,0:T(1,128)S(1)} %copy-done.6, s32[8]{0:T(128)S(1)} %stack.27.who, f32[4,24,128,128]{3,2,1,0:T(8,128)} %bitcast.11), custom_call_target="tpu_custom_call" | custom-call | bytes 20000000 | tf_op jit(solution)/shard_map/lay_out/pallas_call | solution.py:75
  16.4 0.0 copy-start.2
  16.4 1.2 %copy-done.2 = f32[1024,256]{1,0:T(8,128)S(1)} copy-done((f32[1024,256]{1,0:T(8,128)S(1)}, f32[1024,256]{1,0:T(8,128)}, u32[]{:S(2)}) %copy-start.2) | copy-done | bytes 1048600
  17.6 3.0 %agg_own.1.refs_1_ = f32[1024,256]{1,0:T(8,128)S(1)} custom-call(s32[8]{0:T(128)S(1)} %stack.27.who, bf16[2,4,1024,1024]{3,2,1,0:T(8,128)(2,1)S(1)} %get-tuple-element.41.matrix, f32[1024,256]{1,0:T(8,128)S(1)} %copy-done.2), custom_call_target="tpu_custom_call" | custom-call | flops 1610612736 | bytes 17825792 | tf_op jit(solution)/shard_map/agg_own/pallas_call | solution.py:39
  20.7 0.0 collective-permute-done.3.cot_there
  20.7 10.1 %collective-permute-done.2.w_there = f32[512,256]{1,0:T(8,128)S(1)} collective-permute-done((f32[512,256]{1,0:T(8,128)}, f32[512,256]{1,0:T(8,128)S(1)}, u32[]{:S(2)}, u32[]{:S(2)}) %collective-permute-start.2) | collective-permute-done | bytes 524320 | tf_op jit(solution)/shard_map/ppermute | solution.py:294
  30.8 3.0 %agg_near.1.refs_2_ = f32[1024,256]{1,0:T(8,128)S(1)} custom-call(s32[8]{0:T(128)S(1)} %stack.27.who, bf16[2,4,1024,1024]{3,2,1,0:T(8,128)(2,1)S(1)} %get-tuple-element.41.matrix, f32[1024,256]{1,0:T(8,128)S(1)} %collective-permute-done.1.refs_0_, f32[1024,256]{1,0:T(8,128)S(1)} %agg_own.1.refs_1_), custom_call_target="tpu_custom_call" | custom-call | flops 1610612736 | bytes 18874368 | tf_op jit(solution)/shard_map/agg_near/pallas_call | solution.py:39
  33.8 0.0 copy-start.1
  33.8 0.0 copy-start.3
  33.9 2.8 %agg_give.1 = f32[512,256]{1,0:T(8,128)S(1)} custom-call(s32[8]{0:T(128)S(1)} %stack.27.who, bf16[2,4,1024,1024]{3,2,1,0:T(8,128)(2,1)S(1)} %get-tuple-element.41.matrix, f32[1024,256]{1,0:T(8,128)S(1)} %collective-permute-done.refs_0_, f32[1024,256]{1,0:T(8,128)S(1)} %collective-permute-done.4.refs_1_, f32[1024,256]{1,0:T(8,128)S(1)} %agg_near.1.refs_2_), custom_call_target="tpu_custom_call" | custom-call | flops 1610612736 | bytes 19922944 | tf_op jit(solution)/shard_map/agg_give/pallas_call | solution.py:39
  36.7 1.6 %collective-permute-start.5 = (f32[512,256]{1,0:T(8,128)S(1)}, f32[512,256]{1,0:T(8,128)S(1)}, u32[]{:S(2)}, u32[]{:S(2)}) collective-permute-start(f32[512,256]{1,0:T(8,128)S(1)} %agg_give.1), channel_id=1, source_target_pairs={{0,1},{1,0},{2,3},{3,2},{4,5},{5,4},{6,7},{7,6},{8,9},{9,8},{10,11... | collective-permute-start | bytes 1572872 | tf_op jit(solution)/shard_map/ppermute | solution.py:294
  38.3 2.8 %agg_keep.1.own = f32[512,256]{1,0:T(8,128)S(1)} custom-call(s32[8]{0:T(128)S(1)} %stack.27.who, bf16[2,4,1024,1024]{3,2,1,0:T(8,128)(2,1)S(1)} %get-tuple-element.41.matrix, f32[1024,256]{1,0:T(8,128)S(1)} %collective-permute-done.refs_0_, f32[1024,256]{1,0:T(8,128)S(1)} %collective-permute-done.4.refs_1_, f32[1024,256]{1,0:T(8,128)S(1)} %agg_near.1.refs_2_), custom_call_target="tpu_custom_call" | custom-call | flops 1610612736 | bytes 19922944 | tf_op jit(solution)/shard_map/agg_keep/pallas_call | solution.py:39
  41.1 10.0 %collective-permute-done.5.far = f32[512,256]{1,0:T(8,128)S(1)} collective-permute-done((f32[512,256]{1,0:T(8,128)S(1)}, f32[512,256]{1,0:T(8,128)S(1)}, u32[]{:S(2)}, u32[]{:S(2)}) %collective-permute-start.5) | collective-permute-done | bytes 524320 | tf_op jit(solution)/shard_map/ppermute | solution.py:294
  51.1 2.3 %middle.1 = (f32[512,256]{1,0:T(8,128)S(1)}, f32[512,256]{1,0:T(8,128)S(1)}, f32[512,256]{1,0:T(8,128)S(1)}, f32[512,256]{1,0:T(8,128)S(1)}, f32[512,256]{1,0:T(8,128)S(1)}) custom-call(s32[8]{0:T(128)S(1)} %stack.27.who, f32[512,256]{1,0:T(8,128)S(1)} %agg_keep.1.own, f32[512,256]{1,0:T(8,128)S(1)} %collective-permute-done.5.far, f32[512,256]{1,0:T(8,128)S(1)} %copy-done.3, ...), custom_call_target="tpu_custom_call" | custom-call | flops 1207959552 | bytes 3670016 | tf_op jit(solution)/shard_map/middle/pallas_call | solution.py:39
  53.4 1.2 %weight_give.1 = (f32[256,256]{1,0:T(8,128)S(1)}, f32[256,256]{1,0:T(8,128)S(1)}) custom-call(s32[8]{0:T(128)S(1)} %stack.27.who, f32[512,256]{1,0:T(8,128)S(1)} %agg_keep.1.own, f32[512,256]{1,0:T(8,128)S(1)} %collective-permute-done.5.far, f32[512,256]{1,0:T(8,128)S(1)} %get-tuple-element.57.grad_here, f32[512,256]{1,0:T(8,128)S(1)} %get-tuple-element.47.grad_there), custom_call_target="tpu_custom_call" | custom-call | flops 402653184 | bytes 2097152 | tf_op jit(solution)/shard_map/weight_give/pallas_call | solution.py:39
  54.7 0.1 collective-permute-start.6
  54.7 0.5 collective-permute-start.7
  55.2 1.5 %collective-permute-start.8 = (f32[512,256]{1,0:T(8,128)S(1)}, f32[512,256]{1,0:T(8,128)S(1)}, u32[]{:S(2)}, u32[]{:S(2)}) collective-permute-start(f32[512,256]{1,0:T(8,128)S(1)} %get-tuple-element.56), channel_id=1, source_target_pairs={{0,1},{1,0},{2,3},{3,2},{4,5},{5,4},{6,7},{7,6},{8,9},{9,8},{10,11... | collective-permute-start | bytes 1572872 | tf_op jit(solution)/shard_map/ppermute | solution.py:294
  56.8 1.2 %weight_keep.1 = (f32[256,256]{1,0:T(8,128)S(1)}, f32[256,256]{1,0:T(8,128)S(1)}) custom-call(s32[8]{0:T(128)S(1)} %stack.27.who, f32[512,256]{1,0:T(8,128)S(1)} %agg_keep.1.own, f32[512,256]{1,0:T(8,128)S(1)} %collective-permute-done.5.far, f32[512,256]{1,0:T(8,128)S(1)} %get-tuple-element.57.grad_here, f32[512,256]{1,0:T(8,128)S(1)} %get-tuple-element.47.grad_there), custom_call_target="tpu_custom_call" | custom-call | flops 402653184 | bytes 2097152 | tf_op jit(solution)/shard_map/weight_keep/pallas_call | solution.py:39
  58.0 0.6 core_there.1.refs_0_
  58.6 7.4 %collective-permute-start.9 = (f32[256,256]{1,0:T(8,128)S(1)}, f32[256,256]{1,0:T(8,128)S(1)}, u32[]{:S(2)}, u32[]{:S(2)}) collective-permute-start(f32[256,256]{1,0:T(8,128)S(1)} %core_there.1.refs_0_), channel_id=1, source_target_pairs={{0,4},{2,6},{8,12},{10,14},{16,20},{18,22},{24,28},{26,30},{1,5},{... | collective-permute-start | bytes 786440 | tf_op jit(solution)/shard_map/ppermute | solution.py:294
  66.0 0.6 core_here.1.one
  66.5 1.2 keep.1.source
  67.7 3.9 %back_here.1 = (f32[1024,256]{1,0:T(8,128)S(1)}, f32[1024,256]{1,0:T(8,128)S(1)}, f32[1024,256]{1,0:T(8,128)S(1)}, f32[1024,256]{1,0:T(8,128)S(1)}) custom-call(s32[8]{0:T(128)S(1)} %stack.27.who, bf16[2,4,1024,1024]{3,2,1,0:T(8,128)(2,1)S(1)} %get-tuple-element.55.matrix, f32[512,256]{1,0:T(8,128)S(1)} %keep.1.source), custom_call_target="tpu_custom_call" | custom-call | flops 3221225472 | bytes 17301504 | tf_op jit(solution)/shard_map/back_here/pallas_call | solution.py:39
  71.7 0.6 chip_there.1
  72.3 1.5 %back_two.1 = f32[1024,256]{1,0:T(8,128)S(1)} custom-call(s32[8]{0:T(128)S(1)} %stack.27.who, bf16[2,4,1024,1024]{3,2,1,0:T(8,128)(2,1)S(1)} %get-tuple-element.55.matrix, f32[512,256]{1,0:T(8,128)S(1)} %collective-permute-done.8.source, f32[1024,256]{1,0:T(8,128)S(1)} %get-tuple-element.59.refs_0_), custom_call_target="tpu_custom_call" | custom-call | flops 805306368 | bytes 18350080 | tf_op jit(solution)/shard_map/back_two/pallas_call | solution.py:39
  73.8 0.1 collective-permute-start.10
  73.9 1.5 %back_far.1 = f32[1024,256]{1,0:T(8,128)S(1)} custom-call(s32[8]{0:T(128)S(1)} %stack.27.who, bf16[2,4,1024,1024]{3,2,1,0:T(8,128)(2,1)S(1)} %get-tuple-element.55.matrix, f32[512,256]{1,0:T(8,128)S(1)} %collective-permute-done.8.source, f32[1024,256]{1,0:T(8,128)S(1)} %get-tuple-element.63.refs_0_), custom_call_target="tpu_custom_call" | custom-call | flops 805306368 | bytes 18350080 | tf_op jit(solution)/shard_map/back_far/pallas_call | solution.py:39
  75.4 2.4 %collective-permute-start.13 = (f32[1024,256]{1,0:T(8,128)S(1)}, f32[1024,256]{1,0:T(8,128)S(1)}, u32[]{:S(2)}, u32[]{:S(2)}) collective-permute-start(f32[1024,256]{1,0:T(8,128)S(1)} %back_far.1), channel_id=1, source_target_pairs={{0,26},{2,0},{4,30},{6,4},{8,2},{10,8},{12,6},{14,12},{16,10},{18,... | collective-permute-start | bytes 3145736 | tf_op jit(solution)/shard_map/ppermute | solution.py:288
  77.8 4.3 %collective-permute-start.11 = (f32[256,256]{1,0:T(8,128)S(1)}, f32[256,256]{1,0:T(8,128)S(1)}, u32[]{:S(2)}, u32[]{:S(2)}) collective-permute-start(f32[256,256]{1,0:T(8,128)S(1)} %core_here.1.one), channel_id=1, source_target_pairs={{0,4},{2,6},{8,12},{10,14},{16,20},{18,22},{24,28},{26,30},{1,5},{... | collective-permute-start | bytes 786440 | tf_op jit(solution)/shard_map/ppermute | solution.py:294
  82.2 1.7 %collective-permute-start.12 = (f32[256,256]{1,0:T(8,128)S(1)}, f32[256,256]{1,0:T(8,128)S(1)}, u32[]{:S(2)}, u32[]{:S(2)}) collective-permute-start(f32[256,256]{1,0:T(8,128)S(1)} %chip_there.1), channel_id=1, source_target_pairs={{0,1},{1,0},{2,3},{3,2},{4,5},{5,4},{6,7},{7,6},{8,9},{9,8},{10,11... | collective-permute-start | bytes 786440 | tf_op jit(solution)/shard_map/ppermute | solution.py:294
  83.8 1.5 %back_near.1 = f32[1024,256]{1,0:T(8,128)S(1)} custom-call(s32[8]{0:T(128)S(1)} %stack.27.who, bf16[2,4,1024,1024]{3,2,1,0:T(8,128)(2,1)S(1)} %get-tuple-element.55.matrix, f32[512,256]{1,0:T(8,128)S(1)} %collective-permute-done.8.source, f32[1024,256]{1,0:T(8,128)S(1)} %get-tuple-element.65.refs_0_, f32[1024,256]{1,0:T(8,128)S(1)} %collective-permute-done.10.refs_1_), custom_call_target="tpu_custom_call" | custom-call | flops 805306368 | bytes 19398656 | tf_op jit(solution)/shard_map/back_near/pallas_call | solution.py:39
  85.4 0.1 collective-permute-start.20
  85.5 0.5 collective-permute-done.11.two
  85.9 2.7 %collective-permute-done.12.three = f32[256,256]{1,0:T(8,128)S(1)} collective-permute-done((f32[256,256]{1,0:T(8,128)S(1)}, f32[256,256]{1,0:T(8,128)S(1)}, u32[]{:S(2)}, u32[]{:S(2)}) %collective-permute-start.12) | collective-permute-done | bytes 262176 | tf_op jit(solution)/shard_map/ppermute | solution.py:294
  88.6 0.6 side_sum.1
  89.2 1.7 %collective-permute-start.16 = (f32[512,256]{1,0:T(8,128)S(1)}, f32[512,256]{1,0:T(8,128)S(1)}, u32[]{:S(2)}, u32[]{:S(2)}) collective-permute-start(f32[512,256]{1,0:T(8,128)S(1)} %get-tuple-element.75), channel_id=1, source_target_pairs={{0,1},{1,0},{2,3},{3,2},{4,5},{5,4},{6,7},{7,6},{8,9},{9,8},{10,11... | collective-permute-start | bytes 1572872 | tf_op jit(solution)/shard_map/ppermute | solution.py:294
  90.9 0.7 collective-permute-start.14
  91.6 1.5 %back_own.1.refs_0_ = f32[1024,256]{1,0:T(8,128)S(1)} custom-call(s32[8]{0:T(128)S(1)} %stack.27.who, bf16[2,4,1024,1024]{3,2,1,0:T(8,128)(2,1)S(1)} %get-tuple-element.55.matrix, f32[512,256]{1,0:T(8,128)S(1)} %collective-permute-done.8.source, f32[1024,256]{1,0:T(8,128)S(1)} %get-tuple-element.70.refs_0_), custom_call_target="tpu_custom_call" | custom-call | flops 805306368 | bytes 18350080 | tf_op jit(solution)/shard_map/back_own/pallas_call | solution.py:39
  93.1 0.6 collective-permute-done.13.refs_1_
  93.7 0.6 layer_sum.1.refs_0_
  94.2 0.7 collective-permute-start.15
  94.9 0.6 pair_sum.1.ready
  95.5 1.3 %collective-permute-start.19 = (f32[128,256]{1,0:T(8,128)S(1)}, f32[128,256]{1,0:T(8,128)S(1)}, u32[]{:S(2)}, u32[]{:S(2)}) collective-permute-start(f32[128,256]{1,0:T(8,128)S(1)} %pair_sum.1.ready), channel_id=1, source_target_pairs={{4,8},{6,10},{12,0},{14,2},{20,24},{22,26},{28,16},{30,18},{5,9},{... | collective-permute-start | bytes 393224 | tf_op jit(solution)/shard_map/ppermute | solution.py:294
  96.8 1.3 %collective-permute-start.18 = (f32[128,256]{1,0:T(8,128)S(1)}, f32[128,256]{1,0:T(8,128)S(1)}, u32[]{:S(2)}, u32[]{:S(2)}) collective-permute-start(f32[128,256]{1,0:T(8,128)S(1)} %pair_sum.1.ready), channel_id=1, source_target_pairs={{4,0},{6,2},{12,8},{14,10},{20,16},{22,18},{28,24},{30,26},{5,1},{... | collective-permute-start | bytes 393224 | tf_op jit(solution)/shard_map/ppermute | solution.py:294
  98.1 0.7 collective-permute-start.17
  98.8 1.9 %collective-permute-done.16.refs_1_ = f32[512,256]{1,0:T(8,128)S(1)} collective-permute-done((f32[512,256]{1,0:T(8,128)S(1)}, f32[512,256]{1,0:T(8,128)S(1)}, u32[]{:S(2)}, u32[]{:S(2)}) %collective-permute-start.16) | collective-permute-done | bytes 524320 | tf_op jit(solution)/shard_map/ppermute | solution.py:294
  100.7 1.6 %activated.1 = f32[1024,256]{1,0:T(8,128)} custom-call(s32[8]{0:T(128)S(1)} %stack.27.who, f32[512,256]{1,0:T(8,128)S(1)} %get-tuple-element.73.refs_0_, f32[512,256]{1,0:T(8,128)S(1)} %collective-permute-done.16.refs_1_), custom_call_target="tpu_custom_call" | custom-call | bytes 1048576 | tf_op jit(solution)/shard_map/activated/pallas_call | solution.py:39
  102.3 13.1 %collective-permute-done.19.later_sent = f32[128,256]{1,0:T(8,128)S(1)} collective-permute-done((f32[128,256]{1,0:T(8,128)S(1)}, f32[128,256]{1,0:T(8,128)S(1)}, u32[]{:S(2)}, u32[]{:S(2)}) %collective-permute-start.19) | collective-permute-done | bytes 131104 | tf_op jit(solution)/shard_map/ppermute | solution.py:294
  115.4 0.0 collective-permute-done.18.ready_sent
  115.4 0.6 chip_pick.1.refs_0_
  116.0 0.1 collective-permute-start.21
  116.1 1.7 %feature_grad.1 = f32[1024,256]{1,0:T(8,128)} custom-call(s32[8]{0:T(128)S(1)} %stack.27.who, f32[1024,256]{1,0:T(8,128)S(1)} %back_own.1.refs_0_, f32[1024,256]{1,0:T(8,128)S(1)} %collective-permute-done.13.refs_1_, f32[1024,256]{1,0:T(8,128)S(1)} %collective-permute-done.20.refs_2_), custom_call_target="tpu_custom_call" | custom-call | bytes 3145728 | tf_op jit(solution)/shard_map/feature_grad/pallas_call | solution.py:39
  117.8 1.4 %weight_grad.1 = f32[512,256]{1,0:T(8,128)} custom-call(s32[8]{0:T(128)S(1)} %stack.27.who, f32[256,256]{1,0:T(8,128)S(1)} %chip_pick.1.refs_0_, f32[256,256]{1,0:T(8,128)S(1)} %collective-permute-done.21.refs_1_), custom_call_target="tpu_custom_call" | custom-call | bytes 524288 | tf_op jit(solution)/shard_map/weight_grad/pallas_call | solution.py:39
  (20 shorter events, 0.0 us)
Async XLA Ops:
  0.6 30.1 %collective-permute-start.1 = (f32[1024,256]{1,0:T(8,128)}, f32[1024,256]{1,0:T(8,128)S(1)}, u32[]{:S(2)}, u32[]{:S(2)}) collective-permute-start(f32[1024,256]{1,0:T(8,128)} %refs_0_.1), channel_id=1, source_target_pairs={{0,6},{2,4},{4,10},{6,8},{8,14},{10,12},{12,18},{14,16},{16,22},{1... | collective-permute-start | bytes 3145736 | tf_op jit(solution)/shard_map/ppermute | solution.py:288
  3.1 1.2 %copy-start = (f32[1024,256]{1,0:T(8,128)S(1)}, f32[1024,256]{1,0:T(8,128)}, u32[]{:S(2)}) copy-start(f32[1024,256]{1,0:T(8,128)} %cot.1) | copy-start | bytes 3145732
  5.0 15.7 %collective-permute-start.3 = (f32[512,256]{1,0:T(8,128)S(1)}, f32[512,256]{1,0:T(8,128)S(1)}, u32[]{:S(2)}, u32[]{:S(2)}) collective-permute-start(f32[512,256]{1,0:T(8,128)S(1)} %cot_give.1), channel_id=1, source_target_pairs={{0,1},{1,0},{2,3},{3,2},{4,5},{5,4},{6,7},{7,6},{8,9},{9,8},{10,11... | collective-permute-start | bytes 1572872 | tf_op jit(solution)/shard_map/ppermute | solution.py:294
  6.5 24.2 %collective-permute-start.2 = (f32[512,256]{1,0:T(8,128)}, f32[512,256]{1,0:T(8,128)S(1)}, u32[]{:S(2)}, u32[]{:S(2)}) collective-permute-start(f32[512,256]{1,0:T(8,128)} %w_here.3), channel_id=1, source_target_pairs={{0,1},{1,0},{2,3},{3,2},{4,5},{5,4},{6,7},{7,6},{8,9},{9,8},{10,11... | collective-permute-start | bytes 1572872 | tf_op jit(solution)/shard_map/ppermute | solution.py:294
  7.1 26.8 %collective-permute-start = (f32[1024,256]{1,0:T(8,128)}, f32[1024,256]{1,0:T(8,128)S(1)}, u32[]{:S(2)}, u32[]{:S(2)}) collective-permute-start(f32[1024,256]{1,0:T(8,128)} %refs_0_.1), channel_id=1, source_target_pairs={{0,2},{2,8},{4,6},{6,12},{8,10},{10,16},{12,14},{14,20},{16,18},{1... | collective-permute-start | bytes 3145736 | tf_op jit(solution)/shard_map/ppermute | solution.py:288
  7.2 0.7 copy-start.4
  7.9 0.7 copy-start.5
  8.6 0.7 copy-start.6
  16.4 1.2 %copy-start.2 = (f32[1024,256]{1,0:T(8,128)S(1)}, f32[1024,256]{1,0:T(8,128)}, u32[]{:S(2)}) copy-start(f32[1024,256]{1,0:T(8,128)} %refs_0_.1) | copy-start | bytes 3145732
  30.8 3.1 %collective-permute-start.4 = (f32[1024,256]{1,0:T(8,128)S(1)}, f32[1024,256]{1,0:T(8,128)S(1)}, u32[]{:S(2)}, u32[]{:S(2)}) collective-permute-start(f32[1024,256]{1,0:T(8,128)S(1)} %collective-permute-done.1.refs_0_), channel_id=1, source_target_pairs={{0,2},{2,0},{4,6},{6,4},{8,10},{10,8},{12,14},{14,12},{16,18},{18,... | collective-permute-start | bytes 3145736 | tf_op jit(solution)/shard_map/ppermute | solution.py:294
  33.8 17.3 %copy-start.1 = (f32[1024,256]{1,0:T(8,128)S(1)}, f32[1024,256]{1,0:T(8,128)}, u32[]{:S(2)}) copy-start(f32[1024,256]{1,0:T(8,128)} %cot.1) | copy-start | bytes 3145732
  33.8 17.3 %copy-start.3 = (f32[512,256]{1,0:T(8,128)S(1)}, f32[512,256]{1,0:T(8,128)}, u32[]{:S(2)}) copy-start(f32[512,256]{1,0:T(8,128)} %w_here.3) | copy-start | bytes 1572868
  36.7 14.4 %collective-permute-start.5 = (f32[512,256]{1,0:T(8,128)S(1)}, f32[512,256]{1,0:T(8,128)S(1)}, u32[]{:S(2)}, u32[]{:S(2)}) collective-permute-start(f32[512,256]{1,0:T(8,128)S(1)} %agg_give.1), channel_id=1, source_target_pairs={{0,1},{1,0},{2,3},{3,2},{4,5},{5,4},{6,7},{7,6},{8,9},{9,8},{10,11... | collective-permute-start | bytes 1572872 | tf_op jit(solution)/shard_map/ppermute | solution.py:294
  54.7 3.3 %collective-permute-start.6 = (f32[256,256]{1,0:T(8,128)S(1)}, f32[256,256]{1,0:T(8,128)S(1)}, u32[]{:S(2)}, u32[]{:S(2)}) collective-permute-start(f32[256,256]{1,0:T(8,128)S(1)} %get-tuple-element.53), channel_id=1, source_target_pairs={{0,2},{2,0},{4,6},{6,4},{8,10},{10,8},{12,14},{14,12},{16,18},{18,... | collective-permute-start | bytes 786440 | tf_op jit(solution)/shard_map/ppermute | solution.py:294
  54.7 11.2 %collective-permute-start.7 = (f32[256,256]{1,0:T(8,128)S(1)}, f32[256,256]{1,0:T(8,128)S(1)}, u32[]{:S(2)}, u32[]{:S(2)}) collective-permute-start(f32[256,256]{1,0:T(8,128)S(1)} %get-tuple-element.48), channel_id=1, source_target_pairs={{0,2},{2,0},{4,6},{6,4},{8,10},{10,8},{12,14},{14,12},{16,18},{18,... | collective-permute-start | bytes 786440 | tf_op jit(solution)/shard_map/ppermute | solution.py:294
  55.2 17.0 %collective-permute-start.8 = (f32[512,256]{1,0:T(8,128)S(1)}, f32[512,256]{1,0:T(8,128)S(1)}, u32[]{:S(2)}, u32[]{:S(2)}) collective-permute-start(f32[512,256]{1,0:T(8,128)S(1)} %get-tuple-element.56), channel_id=1, source_target_pairs={{0,1},{1,0},{2,3},{3,2},{4,5},{5,4},{6,7},{7,6},{8,9},{9,8},{10,11... | collective-permute-start | bytes 1572872 | tf_op jit(solution)/shard_map/ppermute | solution.py:294
  58.6 13.1 %collective-permute-start.9 = (f32[256,256]{1,0:T(8,128)S(1)}, f32[256,256]{1,0:T(8,128)S(1)}, u32[]{:S(2)}, u32[]{:S(2)}) collective-permute-start(f32[256,256]{1,0:T(8,128)S(1)} %core_there.1.refs_0_), channel_id=1, source_target_pairs={{0,4},{2,6},{8,12},{10,14},{16,20},{18,22},{24,28},{26,30},{1,5},{... | collective-permute-start | bytes 786440 | tf_op jit(solution)/shard_map/ppermute | solution.py:294
  73.8 10.0 %collective-permute-start.10 = (f32[1024,256]{1,0:T(8,128)S(1)}, f32[1024,256]{1,0:T(8,128)S(1)}, u32[]{:S(2)}, u32[]{:S(2)}) collective-permute-start(f32[1024,256]{1,0:T(8,128)S(1)} %back_two.1), channel_id=1, source_target_pairs={{0,2},{2,0},{4,6},{6,4},{8,10},{10,8},{12,14},{14,12},{16,18},{18,... | collective-permute-start | bytes 3145736 | tf_op jit(solution)/shard_map/ppermute | solution.py:294
  75.4 18.2 %collective-permute-start.13 = (f32[1024,256]{1,0:T(8,128)S(1)}, f32[1024,256]{1,0:T(8,128)S(1)}, u32[]{:S(2)}, u32[]{:S(2)}) collective-permute-start(f32[1024,256]{1,0:T(8,128)S(1)} %back_far.1), channel_id=1, source_target_pairs={{0,26},{2,0},{4,30},{6,4},{8,2},{10,8},{12,6},{14,12},{16,10},{18,... | collective-permute-start | bytes 3145736 | tf_op jit(solution)/shard_map/ppermute | solution.py:288
  77.8 8.1 %collective-permute-start.11 = (f32[256,256]{1,0:T(8,128)S(1)}, f32[256,256]{1,0:T(8,128)S(1)}, u32[]{:S(2)}, u32[]{:S(2)}) collective-permute-start(f32[256,256]{1,0:T(8,128)S(1)} %core_here.1.one), channel_id=1, source_target_pairs={{0,4},{2,6},{8,12},{10,14},{16,20},{18,22},{24,28},{26,30},{1,5},{... | collective-permute-start | bytes 786440 | tf_op jit(solution)/shard_map/ppermute | solution.py:294
  82.2 6.4 %collective-permute-start.12 = (f32[256,256]{1,0:T(8,128)S(1)}, f32[256,256]{1,0:T(8,128)S(1)}, u32[]{:S(2)}, u32[]{:S(2)}) collective-permute-start(f32[256,256]{1,0:T(8,128)S(1)} %chip_there.1), channel_id=1, source_target_pairs={{0,1},{1,0},{2,3},{3,2},{4,5},{5,4},{6,7},{7,6},{8,9},{9,8},{10,11... | collective-permute-start | bytes 786440 | tf_op jit(solution)/shard_map/ppermute | solution.py:294
  85.4 30.7 %collective-permute-start.20 = (f32[1024,256]{1,0:T(8,128)S(1)}, f32[1024,256]{1,0:T(8,128)S(1)}, u32[]{:S(2)}, u32[]{:S(2)}) collective-permute-start(f32[1024,256]{1,0:T(8,128)S(1)} %back_near.1), channel_id=1, source_target_pairs={{0,30},{2,28},{4,2},{6,0},{8,6},{10,4},{12,10},{14,8},{16,14},{18,... | collective-permute-start | bytes 3145736 | tf_op jit(solution)/shard_map/ppermute | solution.py:288
  89.2 11.5 %collective-permute-start.16 = (f32[512,256]{1,0:T(8,128)S(1)}, f32[512,256]{1,0:T(8,128)S(1)}, u32[]{:S(2)}, u32[]{:S(2)}) collective-permute-start(f32[512,256]{1,0:T(8,128)S(1)} %get-tuple-element.75), channel_id=1, source_target_pairs={{0,1},{1,0},{2,3},{3,2},{4,5},{5,4},{6,7},{7,6},{8,9},{9,8},{10,11... | collective-permute-start | bytes 1572872 | tf_op jit(solution)/shard_map/ppermute | solution.py:294
  90.9 2.8 %collective-permute-start.14 = (f32[128,256]{1,0:T(8,128)S(1)}, f32[128,256]{1,0:T(8,128)S(1)}, u32[]{:S(2)}, u32[]{:S(2)}) collective-permute-start(f32[128,256]{1,0:T(8,128)S(1)} %get-tuple-element.68), channel_id=1, source_target_pairs={{4,12},{6,14},{12,4},{14,6},{20,28},{22,30},{28,20},{30,22},{5,13}... | collective-permute-start | bytes 393224 | tf_op jit(solution)/shard_map/ppermute | solution.py:294
  94.2 0.7 collective-permute-start.15
  95.5 19.9 %collective-permute-start.19 = (f32[128,256]{1,0:T(8,128)S(1)}, f32[128,256]{1,0:T(8,128)S(1)}, u32[]{:S(2)}, u32[]{:S(2)}) collective-permute-start(f32[128,256]{1,0:T(8,128)S(1)} %pair_sum.1.ready), channel_id=1, source_target_pairs={{4,8},{6,10},{12,0},{14,2},{20,24},{22,26},{28,16},{30,18},{5,9},{... | collective-permute-start | bytes 393224 | tf_op jit(solution)/shard_map/ppermute | solution.py:294
  96.8 18.6 %collective-permute-start.18 = (f32[128,256]{1,0:T(8,128)S(1)}, f32[128,256]{1,0:T(8,128)S(1)}, u32[]{:S(2)}, u32[]{:S(2)}) collective-permute-start(f32[128,256]{1,0:T(8,128)S(1)} %pair_sum.1.ready), channel_id=1, source_target_pairs={{4,0},{6,2},{12,8},{14,10},{20,16},{22,18},{28,24},{30,26},{5,1},{... | collective-permute-start | bytes 393224 | tf_op jit(solution)/shard_map/ppermute | solution.py:294
  98.1 17.3 %collective-permute-start.17 = (f32[128,256]{1,0:T(8,128)S(1)}, f32[128,256]{1,0:T(8,128)S(1)}, u32[]{:S(2)}, u32[]{:S(2)}) collective-permute-start(f32[128,256]{1,0:T(8,128)S(1)} %pair_sum.1.ready), channel_id=1, source_target_pairs={{4,12},{6,14},{12,4},{14,6},{20,28},{22,30},{28,20},{30,22},{5,13}... | collective-permute-start | bytes 393224 | tf_op jit(solution)/shard_map/ppermute | solution.py:294
  116.0 1.8 %collective-permute-start.21 = (f32[256,256]{1,0:T(8,128)S(1)}, f32[256,256]{1,0:T(8,128)S(1)}, u32[]{:S(2)}, u32[]{:S(2)}) collective-permute-start(f32[256,256]{1,0:T(8,128)S(1)} %chip_pick.1.refs_0_), channel_id=1, source_target_pairs={{0,2},{2,0},{4,6},{6,4},{8,10},{10,8},{12,14},{14,12},{16,18},{18,... | collective-permute-start | bytes 786440 | tf_op jit(solution)/shard_map/ppermute | solution.py:294
where the time goes:
time: 120 us; the launch traced here: 119 us
  Pallas kernels  44.1 us (37%)
  waiting for transfers between devices  38.9 us (32%)
  starting transfers between devices  30.6 us (26%)
  local copies, waits for them, and re-layouts  4.56 us (4%)
    ppermute x18, waiting for transfers between devices, chosen(): lax.ppermute(value, axis, [pair for pair in pairs if pair[1] is not None])  38.3 us
    pallas_call x24, Pallas kernels, call(): pl.pallas_call(kernel, in_specs=[IN_SMEM] + [IN_VMEM] * len(operands), ou...  37 us
    ppermute x18, starting transfers between devices, chosen(): lax.ppermute(value, axis, [pair for pair in pairs if pair[1] is not None])  25.5 us
    pallas_call x1, Pallas kernels, lay_out(): pl.pallas_call(lay_out_kernel, grid_spec=pltpu.PrefetchScalarGridSpec(num...  7.18 us
    ppermute x4, starting transfers between devices, moved(): return lax.ppermute(value, axis, perm)  5.04 us
    unnamed x14, local copies, waits for them, and re-layouts  4.48 us
  transfers between devices with their start and end apart: 22, of which 7 were waited for; matrix products, arithmetic and copies ran while one was open for 0% of the time, Pallas kernels for 29%

commit v1 on v0

--- a/solution.py
+++ b/solution.py
@@ -241,7 +241,7 @@
     )[0]
 
 
-def pick_kernel(who, ready, later, ready_sent, later_sent, out):
+def pick_kernel(who, ready, ready_sent, later, later_sent, out):
     rows = ready.shape[0]
     odd = who[CHIP] == 1
     for which, one, other in ((0, ready, ready_sent), (1, later, later_sent)):
@@ -269,6 +269,14 @@
     rows, cols = parts[0].shape
     shape = ((rows // 2, cols), F32)
     return call(name, side_kernel, who, parts, [shape] * 2, [pltpu.VMEM((rows, cols), F32)])
+
+
+def line_kernel(who, here, one, two, three, out):
+    out[...] = (here[...] + one[...]) + (two[...] + three[...])
+
+
+def line_sum(name, who, *parts):
+    return call(name, line_kernel, who, parts, [(parts[0].shape, F32)])[0]
 
 
 def add_kernel(who, *refs):
@@ -366,11 +374,10 @@
     near = moved(last, "dom", -1, -3)
     last = next(steps)(last)
     act_got = swapped(after(act_there, last), "feat")
+    last = next(steps)(last, far)
     mine = backward("back_own", who, t, [OWN], after(g_there, last), [firsts[3]], 1)[0]
-    last = next(steps)(mine, far)
-    last = next(steps)(last)
     activated = join("activated", who, SIDE, [after(act_here, last), act_got], jax.ShapeDtypeStruct)
-    last = next(steps)(activated)
+    last = next(steps)(activated, mine)
     feature_grad = call(
         "feature_grad",
         add_kernel,
@@ -387,7 +394,7 @@
     if not quick:
         here, there = (join("core_join", who, CORE, pair) for pair in zip(keep, give))
         total = lax.psum(here + swapped(there, "feat"), "dom")
-        for _ in range(7):
+        for _ in range(6):
             yield lambda *last: last[0]
         yield lambda *last: total
         return
@@ -414,15 +421,17 @@
     also = up(here)
     yield step(lambda *last: side_sum("side_sum", who, after(here, *last), also, got)[::-1])
     give, keep = box[-1]
-    for name, bit in (("layer_sum", 4), ("pair_sum", 8)):
-        got = chosen(give, "dom", lambda i: i ^ bit if i % 4 >= 2 else None)
-        yield step(lambda *last: add(name, who, after(keep, *last), got))
-        keep = give = box[-1]
+    gots = [
+        chosen(value, "dom", lambda i: i ^ bits if i % 4 >= 2 else None)
+        for value, bits in ((give, 4), (keep, 8), (give, 12))
+    ]
+    yield step(lambda *last: line_sum("line_sum", who, after(keep, *last), *gots))
+    keep = box[-1]
     later_sent = chosen(keep, "dom", lambda i: (i ^ 4) - 2 if i % 4 >= 2 else None)
     later = chosen(keep, "dom", lambda i: i ^ 4 if i % 4 >= 2 else None)
     ready_sent = chosen(keep, "dom", lambda i: i - 2 if i % 4 >= 2 else None)
     yield step(
-        lambda *last: pick("chip_pick", who, after(keep, *last), later, ready_sent, later_sent)
+        lambda *last: pick("chip_pick", who, after(keep, *last), ready_sent, later, later_sent)
     )
     got = swapped(box[-1], "dom")
     yield step(

time: 120 us -> 122 us (1.017)
  waiting for transfers between devices: 38.9 us -> 40.9 us
    ppermute x18 -> x19, waiting for transfers between devices: 38.3 us -> 39.5 us  [chosen(): lax.ppermute(value, axis, [pair for pair in pairs if pair[1] is not None])]
    ppermute x18 -> x19, starting transfers between devices: 25.5 us -> 26.2 us  [chosen(): lax.ppermute(value, axis, [pair for pair in pairs if pair[1] is not None])]
    pallas_call x24 -> x23, Pallas kernels: 37 us -> 36.4 us  [call(): pl.pallas_call(kernel, in_specs=[IN_SMEM] + [IN_VMEM] * len(operands), ou...]
  transfers between devices with their start and end apart: 22 -> 23, of which waited for: 7 -> 8; matrix products, arithmetic and copies ran while one was open for 0% -> 0% of each run, Pallas kernels for 29% -> 28%
where the time goes in v1:
time: 122 us; the launch traced here: 121 us
  Pallas kernels  43.4 us (36%)
  waiting for transfers between devices  40.9 us (34%)
  starting transfers between devices  31.2 us (26%)
  local copies, waits for them, and re-layouts  4.56 us (4%)
    ppermute x19, waiting for transfers between devices, chosen(): lax.ppermute(value, axis, [pair for pair in pairs if pair[1] is not None])  39.5 us
    pallas_call x23, Pallas kernels, call(): pl.pallas_call(kernel, in_specs=[IN_SMEM] + [IN_VMEM] * len(operands), ou...  36.4 us
    ppermute x19, starting transfers between devices, chosen(): lax.ppermute(value, axis, [pair for pair in pairs if pair[1] is not None])  26.2 us
    pallas_call x1, Pallas kernels, lay_out(): pl.pallas_call(lay_out_kernel, grid_spec=pltpu.PrefetchScalarGridSpec(num...  6.96 us
    ppermute x4, starting transfers between devices, moved(): return lax.ppermute(value, axis, perm)  5.04 us
    unnamed x14, local copies, waits for them, and re-layouts  4.48 us
  transfers between devices with their start and end apart: 23, of which 8 were waited for; matrix products, arithmetic and copies ran while one was open for 0% of the time, Pallas kernels for 28%

profile of v1, /device:TPU:0, one launch (start us, length us, event | category | flops | bytes accessed | tf_op | source)
XLA Modules:
  0.0 121.1 jit_solution(13528237823995246088)
XLA Ops:
  0.6 2.4 %collective-permute-start.1 = (f32[1024,256]{1,0:T(8,128)}, f32[1024,256]{1,0:T(8,128)S(1)}, u32[]{:S(2)}, u32[]{:S(2)}) collective-permute-start(f32[1024,256]{1,0:T(8,128)} %refs_0_.1), channel_id=1, source_target_pairs={{0,6},{2,4},{4,10},{6,8},{8,14},{10,12},{12,18},{14,16},{16,22},{1... | collective-permute-start | bytes 3145736 | tf_op jit(solution)/shard_map/ppermute | solution.py:296
  3.1 0.1 stack.27.who
  3.1 1.2 %copy-done = f32[1024,256]{1,0:T(8,128)S(1)} copy-done((f32[1024,256]{1,0:T(8,128)S(1)}, f32[1024,256]{1,0:T(8,128)}, u32[]{:S(2)}) %copy-start) | copy-done | bytes 1048600
  4.4 0.6 cot_give.1
  5.0 1.6 %collective-permute-start.3 = (f32[512,256]{1,0:T(8,128)S(1)}, f32[512,256]{1,0:T(8,128)S(1)}, u32[]{:S(2)}, u32[]{:S(2)}) collective-permute-start(f32[512,256]{1,0:T(8,128)S(1)} %cot_give.1), channel_id=1, source_target_pairs={{0,1},{1,0},{2,3},{3,2},{4,5},{5,4},{6,7},{7,6},{8,9},{9,8},{10,11... | collective-permute-start | bytes 1572872 | tf_op jit(solution)/shard_map/ppermute | solution.py:302
  6.5 0.5 collective-permute-start.2
  7.1 0.1 collective-permute-start
  7.2 0.7 copy-done.4
  7.9 0.7 copy-done.5
  8.6 0.7 copy-done.6
  9.2 7.0 %lay_out.1 = (bf16[2,4,1024,1024]{3,2,1,0:T(8,128)(2,1)S(1)}, bf16[2,4,1024,1024]{3,2,1,0:T(8,128)(2,1)S(1)}) custom-call(s32[4,24]{1,0:T(4,128)S(1)} %bitcast.9, s32[4,24]{1,0:T(4,128)S(1)} %bitcast.10, s32[1,4]{1,0:T(1,128)S(1)} %copy-done.6, s32[8]{0:T(128)S(1)} %stack.27.who, f32[4,24,128,128]{3,2,1,0:T(8,128)} %bitcast.11), custom_call_target="tpu_custom_call" | custom-call | bytes 20000000 | tf_op jit(solution)/shard_map/lay_out/pallas_call | solution.py:75
  16.2 0.0 copy-start.2
  16.2 1.2 %copy-done.2 = f32[1024,256]{1,0:T(8,128)S(1)} copy-done((f32[1024,256]{1,0:T(8,128)S(1)}, f32[1024,256]{1,0:T(8,128)}, u32[]{:S(2)}) %copy-start.2) | copy-done | bytes 1048600
  17.4 3.0 %agg_own.1.refs_1_ = f32[1024,256]{1,0:T(8,128)S(1)} custom-call(s32[8]{0:T(128)S(1)} %stack.27.who, bf16[2,4,1024,1024]{3,2,1,0:T(8,128)(2,1)S(1)} %get-tuple-element.40.matrix, f32[1024,256]{1,0:T(8,128)S(1)} %copy-done.2), custom_call_target="tpu_custom_call" | custom-call | flops 1610612736 | bytes 17825792 | tf_op jit(solution)/shard_map/agg_own/pallas_call | solution.py:39
  20.5 10.3 %collective-permute-done.2.w_there = f32[512,256]{1,0:T(8,128)S(1)} collective-permute-done((f32[512,256]{1,0:T(8,128)}, f32[512,256]{1,0:T(8,128)S(1)}, u32[]{:S(2)}, u32[]{:S(2)}) %collective-permute-start.2) | collective-permute-done | bytes 524320 | tf_op jit(solution)/shard_map/ppermute | solution.py:302
  30.8 0.0 collective-permute-done.1.refs_0_
  30.8 3.0 %agg_near.1.refs_2_ = f32[1024,256]{1,0:T(8,128)S(1)} custom-call(s32[8]{0:T(128)S(1)} %stack.27.who, bf16[2,4,1024,1024]{3,2,1,0:T(8,128)(2,1)S(1)} %get-tuple-element.40.matrix, f32[1024,256]{1,0:T(8,128)S(1)} %collective-permute-done.1.refs_0_, f32[1024,256]{1,0:T(8,128)S(1)} %agg_own.1.refs_1_), custom_call_target="tpu_custom_call" | custom-call | flops 1610612736 | bytes 18874368 | tf_op jit(solution)/shard_map/agg_near/pallas_call | solution.py:39
  33.8 0.0 copy-start.1
  33.8 0.0 copy-start.3
  33.9 2.8 %agg_give.1 = f32[512,256]{1,0:T(8,128)S(1)} custom-call(s32[8]{0:T(128)S(1)} %stack.27.who, bf16[2,4,1024,1024]{3,2,1,0:T(8,128)(2,1)S(1)} %get-tuple-element.40.matrix, f32[1024,256]{1,0:T(8,128)S(1)} %collective-permute-done.refs_0_, f32[1024,256]{1,0:T(8,128)S(1)} %collective-permute-done.4.refs_1_, f32[1024,256]{1,0:T(8,128)S(1)} %agg_near.1.refs_2_), custom_call_target="tpu_custom_call" | custom-call | flops 1610612736 | bytes 19922944 | tf_op jit(solution)/shard_map/agg_give/pallas_call | solution.py:39
  36.7 1.6 %collective-permute-start.5 = (f32[512,256]{1,0:T(8,128)S(1)}, f32[512,256]{1,0:T(8,128)S(1)}, u32[]{:S(2)}, u32[]{:S(2)}) collective-permute-start(f32[512,256]{1,0:T(8,128)S(1)} %agg_give.1), channel_id=1, source_target_pairs={{0,1},{1,0},{2,3},{3,2},{4,5},{5,4},{6,7},{7,6},{8,9},{9,8},{10,11... | collective-permute-start | bytes 1572872 | tf_op jit(solution)/shard_map/ppermute | solution.py:302
  38.3 2.8 %agg_keep.1.own = f32[512,256]{1,0:T(8,128)S(1)} custom-call(s32[8]{0:T(128)S(1)} %stack.27.who, bf16[2,4,1024,1024]{3,2,1,0:T(8,128)(2,1)S(1)} %get-tuple-element.40.matrix, f32[1024,256]{1,0:T(8,128)S(1)} %collective-permute-done.refs_0_, f32[1024,256]{1,0:T(8,128)S(1)} %collective-permute-done.4.refs_1_, f32[1024,256]{1,0:T(8,128)S(1)} %agg_near.1.refs_2_), custom_call_target="tpu_custom_call" | custom-call | flops 1610612736 | bytes 19922944 | tf_op jit(solution)/shard_map/agg_keep/pallas_call | solution.py:39
  41.1 10.0 %collective-permute-done.5.far = f32[512,256]{1,0:T(8,128)S(1)} collective-permute-done((f32[512,256]{1,0:T(8,128)S(1)}, f32[512,256]{1,0:T(8,128)S(1)}, u32[]{:S(2)}, u32[]{:S(2)}) %collective-permute-start.5) | collective-permute-done | bytes 524320 | tf_op jit(solution)/shard_map/ppermute | solution.py:302
  51.1 2.3 %middle.1 = (f32[512,256]{1,0:T(8,128)S(1)}, f32[512,256]{1,0:T(8,128)S(1)}, f32[512,256]{1,0:T(8,128)S(1)}, f32[512,256]{1,0:T(8,128)S(1)}, f32[512,256]{1,0:T(8,128)S(1)}) custom-call(s32[8]{0:T(128)S(1)} %stack.27.who, f32[512,256]{1,0:T(8,128)S(1)} %agg_keep.1.own, f32[512,256]{1,0:T(8,128)S(1)} %collective-permute-done.5.far, f32[512,256]{1,0:T(8,128)S(1)} %copy-done.3, ...), custom_call_target="tpu_custom_call" | custom-call | flops 1207959552 | bytes 3670016 | tf_op jit(solution)/shard_map/middle/pallas_call | solution.py:39
  53.4 1.2 weight_give.1
  54.7 0.1 collective-permute-start.6
  54.7 0.5 collective-permute-start.7
  55.2 1.5 %collective-permute-start.8 = (f32[512,256]{1,0:T(8,128)S(1)}, f32[512,256]{1,0:T(8,128)S(1)}, u32[]{:S(2)}, u32[]{:S(2)}) collective-permute-start(f32[512,256]{1,0:T(8,128)S(1)} %get-tuple-element.55), channel_id=1, source_target_pairs={{0,1},{1,0},{2,3},{3,2},{4,5},{5,4},{6,7},{7,6},{8,9},{9,8},{10,11... | collective-permute-start | bytes 1572872 | tf_op jit(solution)/shard_map/ppermute | solution.py:302
  56.8 1.2 weight_keep.1
  58.0 0.6 core_there.1.refs_0_
  58.6 7.4 %collective-permute-start.9 = (f32[256,256]{1,0:T(8,128)S(1)}, f32[256,256]{1,0:T(8,128)S(1)}, u32[]{:S(2)}, u32[]{:S(2)}) collective-permute-start(f32[256,256]{1,0:T(8,128)S(1)} %core_there.1.refs_0_), channel_id=1, source_target_pairs={{0,4},{2,6},{8,12},{10,14},{16,20},{18,22},{24,28},{26,30},{1,5},{... | collective-permute-start | bytes 786440 | tf_op jit(solution)/shard_map/ppermute | solution.py:302
  66.0 0.6 core_here.1.one
  66.5 1.2 keep.1.source
  67.7 3.9 %back_here.1 = (f32[1024,256]{1,0:T(8,128)S(1)}, f32[1024,256]{1,0:T(8,128)S(1)}, f32[1024,256]{1,0:T(8,128)S(1)}, f32[1024,256]{1,0:T(8,128)S(1)}) custom-call(s32[8]{0:T(128)S(1)} %stack.27.who, bf16[2,4,1024,1024]{3,2,1,0:T(8,128)(2,1)S(1)} %get-tuple-element.54.matrix, f32[512,256]{1,0:T(8,128)S(1)} %keep.1.source), custom_call_target="tpu_custom_call" | custom-call | flops 3221225472 | bytes 17301504 | tf_op jit(solution)/shard_map/back_here/pallas_call | solution.py:39
  71.7 0.6 chip_there.1
  72.3 1.5 %back_two.1 = f32[1024,256]{1,0:T(8,128)S(1)} custom-call(s32[8]{0:T(128)S(1)} %stack.27.who, bf16[2,4,1024,1024]{3,2,1,0:T(8,128)(2,1)S(1)} %get-tuple-element.54.matrix, f32[512,256]{1,0:T(8,128)S(1)} %collective-permute-done.8.source, f32[1024,256]{1,0:T(8,128)S(1)} %get-tuple-element.58.refs_0_), custom_call_target="tpu_custom_call" | custom-call | flops 805306368 | bytes 18350080 | tf_op jit(solution)/shard_map/back_two/pallas_call | solution.py:39
  73.8 0.1 collective-permute-start.10
  73.9 1.5 %back_far.1 = f32[1024,256]{1,0:T(8,128)S(1)} custom-call(s32[8]{0:T(128)S(1)} %stack.27.who, bf16[2,4,1024,1024]{3,2,1,0:T(8,128)(2,1)S(1)} %get-tuple-element.54.matrix, f32[512,256]{1,0:T(8,128)S(1)} %collective-permute-done.8.source, f32[1024,256]{1,0:T(8,128)S(1)} %get-tuple-element.62.refs_0_), custom_call_target="tpu_custom_call" | custom-call | flops 805306368 | bytes 18350080 | tf_op jit(solution)/shard_map/back_far/pallas_call | solution.py:39
  75.4 2.4 %collective-permute-start.13 = (f32[1024,256]{1,0:T(8,128)S(1)}, f32[1024,256]{1,0:T(8,128)S(1)}, u32[]{:S(2)}, u32[]{:S(2)}) collective-permute-start(f32[1024,256]{1,0:T(8,128)S(1)} %back_far.1), channel_id=1, source_target_pairs={{0,26},{2,0},{4,30},{6,4},{8,2},{10,8},{12,6},{14,12},{16,10},{18,... | collective-permute-start | bytes 3145736 | tf_op jit(solution)/shard_map/ppermute | solution.py:296
  77.8 4.3 %collective-permute-start.11 = (f32[256,256]{1,0:T(8,128)S(1)}, f32[256,256]{1,0:T(8,128)S(1)}, u32[]{:S(2)}, u32[]{:S(2)}) collective-permute-start(f32[256,256]{1,0:T(8,128)S(1)} %core_here.1.one), channel_id=1, source_target_pairs={{0,4},{2,6},{8,12},{10,14},{16,20},{18,22},{24,28},{26,30},{1,5},{... | collective-permute-start | bytes 786440 | tf_op jit(solution)/shard_map/ppermute | solution.py:302
  82.2 1.7 %collective-permute-start.12 = (f32[256,256]{1,0:T(8,128)S(1)}, f32[256,256]{1,0:T(8,128)S(1)}, u32[]{:S(2)}, u32[]{:S(2)}) collective-permute-start(f32[256,256]{1,0:T(8,128)S(1)} %chip_there.1), channel_id=1, source_target_pairs={{0,1},{1,0},{2,3},{3,2},{4,5},{5,4},{6,7},{7,6},{8,9},{9,8},{10,11... | collective-permute-start | bytes 786440 | tf_op jit(solution)/shard_map/ppermute | solution.py:302
  83.8 1.5 %back_near.1 = f32[1024,256]{1,0:T(8,128)S(1)} custom-call(s32[8]{0:T(128)S(1)} %stack.27.who, bf16[2,4,1024,1024]{3,2,1,0:T(8,128)(2,1)S(1)} %get-tuple-element.54.matrix, f32[512,256]{1,0:T(8,128)S(1)} %collective-permute-done.8.source, f32[1024,256]{1,0:T(8,128)S(1)} %get-tuple-element.64.refs_0_, f32[1024,256]{1,0:T(8,128)S(1)} %collective-permute-done.10.refs_1_), custom_call_target="tpu_custom_call" | custom-call | flops 805306368 | bytes 19398656 | tf_op jit(solution)/shard_map/back_near/pallas_call | solution.py:39
  85.4 0.1 collective-permute-start.21
  85.5 0.5 collective-permute-done.11.two
  85.9 2.7 %collective-permute-done.12.three = f32[256,256]{1,0:T(8,128)S(1)} collective-permute-done((f32[256,256]{1,0:T(8,128)S(1)}, f32[256,256]{1,0:T(8,128)S(1)}, u32[]{:S(2)}, u32[]{:S(2)}) %collective-permute-start.12) | collective-permute-done | bytes 262176 | tf_op jit(solution)/shard_map/ppermute | solution.py:302
  88.6 0.6 side_sum.1
  89.2 1.7 %collective-permute-start.17 = (f32[512,256]{1,0:T(8,128)S(1)}, f32[512,256]{1,0:T(8,128)S(1)}, u32[]{:S(2)}, u32[]{:S(2)}) collective-permute-start(f32[512,256]{1,0:T(8,128)S(1)} %get-tuple-element.71), channel_id=1, source_target_pairs={{0,1},{1,0},{2,3},{3,2},{4,5},{5,4},{6,7},{7,6},{8,9},{9,8},{10,11... | collective-permute-start | bytes 1572872 | tf_op jit(solution)/shard_map/ppermute | solution.py:302
  90.9 0.7 collective-permute-start.16
  91.6 0.7 collective-permute-start.15
  92.2 1.4 %collective-permute-done.13.refs_1_ = f32[1024,256]{1,0:T(8,128)S(1)} collective-permute-done((f32[1024,256]{1,0:T(8,128)S(1)}, f32[1024,256]{1,0:T(8,128)S(1)}, u32[]{:S(2)}, u32[]{:S(2)}) %collective-permute-start.13) | collective-permute-done | bytes 1048608 | tf_op jit(solution)/shard_map/ppermute | solution.py:296
  93.7 0.7 collective-permute-start.14
  94.4 0.6 line_sum.1.ready
  95.0 1.3 %collective-permute-start.20 = (f32[128,256]{1,0:T(8,128)S(1)}, f32[128,256]{1,0:T(8,128)S(1)}, u32[]{:S(2)}, u32[]{:S(2)}) collective-permute-start(f32[128,256]{1,0:T(8,128)S(1)} %line_sum.1.ready), channel_id=1, source_target_pairs={{4,8},{6,10},{12,0},{14,2},{20,24},{22,26},{28,16},{30,18},{5,9},{... | collective-permute-start | bytes 393224 | tf_op jit(solution)/shard_map/ppermute | solution.py:302
  96.3 0.7 collective-permute-start.19
  96.9 1.3 %collective-permute-start.18 = (f32[128,256]{1,0:T(8,128)S(1)}, f32[128,256]{1,0:T(8,128)S(1)}, u32[]{:S(2)}, u32[]{:S(2)}) collective-permute-start(f32[128,256]{1,0:T(8,128)S(1)} %line_sum.1.ready), channel_id=1, source_target_pairs={{4,0},{6,2},{12,8},{14,10},{20,16},{22,18},{28,24},{30,26},{5,1},{... | collective-permute-start | bytes 393224 | tf_op jit(solution)/shard_map/ppermute | solution.py:302
  98.2 1.5 %back_own.1.refs_0_ = f32[1024,256]{1,0:T(8,128)S(1)} custom-call(s32[8]{0:T(128)S(1)} %stack.27.who, bf16[2,4,1024,1024]{3,2,1,0:T(8,128)(2,1)S(1)} %get-tuple-element.54.matrix, f32[512,256]{1,0:T(8,128)S(1)} %collective-permute-done.8.source, f32[1024,256]{1,0:T(8,128)S(1)} %get-tuple-element.73.refs_0_), custom_call_target="tpu_custom_call" | custom-call | flops 805306368 | bytes 18350080 | tf_op jit(solution)/shard_map/back_own/pallas_call | solution.py:39
  99.8 0.9 collective-permute-done.17.refs_1_
  100.7 1.6 %activated.1 = f32[1024,256]{1,0:T(8,128)} custom-call(s32[8]{0:T(128)S(1)} %stack.27.who, f32[512,256]{1,0:T(8,128)S(1)} %get-tuple-element.69.refs_0_, f32[512,256]{1,0:T(8,128)S(1)} %collective-permute-done.17.refs_1_), custom_call_target="tpu_custom_call" | custom-call | bytes 1048576 | tf_op jit(solution)/shard_map/activated/pallas_call | solution.py:39
  102.3 10.9 %collective-permute-done.20.later_sent = f32[128,256]{1,0:T(8,128)S(1)} collective-permute-done((f32[128,256]{1,0:T(8,128)S(1)}, f32[128,256]{1,0:T(8,128)S(1)}, u32[]{:S(2)}, u32[]{:S(2)}) %collective-permute-start.20) | collective-permute-done | bytes 131104 | tf_op jit(solution)/shard_map/ppermute | solution.py:302
  113.1 4.2 %collective-permute-done.18.ready_sent = f32[128,256]{1,0:T(8,128)S(1)} collective-permute-done((f32[128,256]{1,0:T(8,128)S(1)}, f32[128,256]{1,0:T(8,128)S(1)}, u32[]{:S(2)}, u32[]{:S(2)}) %collective-permute-start.18) | collective-permute-done | bytes 131104 | tf_op jit(solution)/shard_map/ppermute | solution.py:302
  117.4 0.6 chip_pick.1.refs_0_
  118.0 0.1 collective-permute-start.22
  118.1 1.7 %feature_grad.1 = f32[1024,256]{1,0:T(8,128)} custom-call(s32[8]{0:T(128)S(1)} %stack.27.who, f32[1024,256]{1,0:T(8,128)S(1)} %back_own.1.refs_0_, f32[1024,256]{1,0:T(8,128)S(1)} %collective-permute-done.13.refs_1_, f32[1024,256]{1,0:T(8,128)S(1)} %collective-permute-done.21.refs_2_), custom_call_target="tpu_custom_call" | custom-call | bytes 3145728 | tf_op jit(solution)/shard_map/feature_grad/pallas_call | solution.py:39
  119.7 1.4 %weight_grad.1 = f32[512,256]{1,0:T(8,128)} custom-call(s32[8]{0:T(128)S(1)} %stack.27.who, f32[256,256]{1,0:T(8,128)S(1)} %chip_pick.1.refs_0_, f32[256,256]{1,0:T(8,128)S(1)} %collective-permute-done.22.refs_1_), custom_call_target="tpu_custom_call" | custom-call | bytes 524288 | tf_op jit(solution)/shard_map/weight_grad/pallas_call | solution.py:39
  (21 shorter events, 0.0 us)
Async XLA Ops:
  0.6 30.1 %collective-permute-start.1 = (f32[1024,256]{1,0:T(8,128)}, f32[1024,256]{1,0:T(8,128)S(1)}, u32[]{:S(2)}, u32[]{:S(2)}) collective-permute-start(f32[1024,256]{1,0:T(8,128)} %refs_0_.1), channel_id=1, source_target_pairs={{0,6},{2,4},{4,10},{6,8},{8,14},{10,12},{12,18},{14,16},{16,22},{1... | collective-permute-start | bytes 3145736 | tf_op jit(solution)/shard_map/ppermute | solution.py:296
  3.1 1.2 %copy-start = (f32[1024,256]{1,0:T(8,128)S(1)}, f32[1024,256]{1,0:T(8,128)}, u32[]{:S(2)}) copy-start(f32[1024,256]{1,0:T(8,128)} %cot.1) | copy-start | bytes 3145732
  5.0 15.5 %collective-permute-start.3 = (f32[512,256]{1,0:T(8,128)S(1)}, f32[512,256]{1,0:T(8,128)S(1)}, u32[]{:S(2)}, u32[]{:S(2)}) collective-permute-start(f32[512,256]{1,0:T(8,128)S(1)} %cot_give.1), channel_id=1, source_target_pairs={{0,1},{1,0},{2,3},{3,2},{4,5},{5,4},{6,7},{7,6},{8,9},{9,8},{10,11... | collective-permute-start | bytes 1572872 | tf_op jit(solution)/shard_map/ppermute | solution.py:302
  6.5 24.2 %collective-permute-start.2 = (f32[512,256]{1,0:T(8,128)}, f32[512,256]{1,0:T(8,128)S(1)}, u32[]{:S(2)}, u32[]{:S(2)}) collective-permute-start(f32[512,256]{1,0:T(8,128)} %w_here.3), channel_id=1, source_target_pairs={{0,1},{1,0},{2,3},{3,2},{4,5},{5,4},{6,7},{7,6},{8,9},{9,8},{10,11... | collective-permute-start | bytes 1572872 | tf_op jit(solution)/shard_map/ppermute | solution.py:302
  7.1 26.8 %collective-permute-start = (f32[1024,256]{1,0:T(8,128)}, f32[1024,256]{1,0:T(8,128)S(1)}, u32[]{:S(2)}, u32[]{:S(2)}) collective-permute-start(f32[1024,256]{1,0:T(8,128)} %refs_0_.1), channel_id=1, source_target_pairs={{0,2},{2,8},{4,6},{6,12},{8,10},{10,16},{12,14},{14,20},{16,18},{1... | collective-permute-start | bytes 3145736 | tf_op jit(solution)/shard_map/ppermute | solution.py:296
  7.2 0.7 copy-start.4
  7.9 0.7 copy-start.5
  8.6 0.7 copy-start.6
  16.2 1.2 %copy-start.2 = (f32[1024,256]{1,0:T(8,128)S(1)}, f32[1024,256]{1,0:T(8,128)}, u32[]{:S(2)}) copy-start(f32[1024,256]{1,0:T(8,128)} %refs_0_.1) | copy-start | bytes 3145732
  30.8 3.1 %collective-permute-start.4 = (f32[1024,256]{1,0:T(8,128)S(1)}, f32[1024,256]{1,0:T(8,128)S(1)}, u32[]{:S(2)}, u32[]{:S(2)}) collective-permute-start(f32[1024,256]{1,0:T(8,128)S(1)} %collective-permute-done.1.refs_0_), channel_id=1, source_target_pairs={{0,2},{2,0},{4,6},{6,4},{8,10},{10,8},{12,14},{14,12},{16,18},{18,... | collective-permute-start | bytes 3145736 | tf_op jit(solution)/shard_map/ppermute | solution.py:302
  33.8 17.3 %copy-start.1 = (f32[1024,256]{1,0:T(8,128)S(1)}, f32[1024,256]{1,0:T(8,128)}, u32[]{:S(2)}) copy-start(f32[1024,256]{1,0:T(8,128)} %cot.1) | copy-start | bytes 3145732
  33.8 17.3 %copy-start.3 = (f32[512,256]{1,0:T(8,128)S(1)}, f32[512,256]{1,0:T(8,128)}, u32[]{:S(2)}) copy-start(f32[512,256]{1,0:T(8,128)} %w_here.3) | copy-start | bytes 1572868
  36.7 14.4 %collective-permute-start.5 = (f32[512,256]{1,0:T(8,128)S(1)}, f32[512,256]{1,0:T(8,128)S(1)}, u32[]{:S(2)}, u32[]{:S(2)}) collective-permute-start(f32[512,256]{1,0:T(8,128)S(1)} %agg_give.1), channel_id=1, source_target_pairs={{0,1},{1,0},{2,3},{3,2},{4,5},{5,4},{6,7},{7,6},{8,9},{9,8},{10,11... | collective-permute-start | bytes 1572872 | tf_op jit(solution)/shard_map/ppermute | solution.py:302
  54.7 3.3 %collective-permute-start.6 = (f32[256,256]{1,0:T(8,128)S(1)}, f32[256,256]{1,0:T(8,128)S(1)}, u32[]{:S(2)}, u32[]{:S(2)}) collective-permute-start(f32[256,256]{1,0:T(8,128)S(1)} %get-tuple-element.52), channel_id=1, source_target_pairs={{0,2},{2,0},{4,6},{6,4},{8,10},{10,8},{12,14},{14,12},{16,18},{18,... | collective-permute-start | bytes 786440 | tf_op jit(solution)/shard_map/ppermute | solution.py:302
  54.7 11.2 %collective-permute-start.7 = (f32[256,256]{1,0:T(8,128)S(1)}, f32[256,256]{1,0:T(8,128)S(1)}, u32[]{:S(2)}, u32[]{:S(2)}) collective-permute-start(f32[256,256]{1,0:T(8,128)S(1)} %get-tuple-element.47), channel_id=1, source_target_pairs={{0,2},{2,0},{4,6},{6,4},{8,10},{10,8},{12,14},{14,12},{16,18},{18,... | collective-permute-start | bytes 786440 | tf_op jit(solution)/shard_map/ppermute | solution.py:302
  55.2 17.0 %collective-permute-start.8 = (f32[512,256]{1,0:T(8,128)S(1)}, f32[512,256]{1,0:T(8,128)S(1)}, u32[]{:S(2)}, u32[]{:S(2)}) collective-permute-start(f32[512,256]{1,0:T(8,128)S(1)} %get-tuple-element.55), channel_id=1, source_target_pairs={{0,1},{1,0},{2,3},{3,2},{4,5},{5,4},{6,7},{7,6},{8,9},{9,8},{10,11... | collective-permute-start | bytes 1572872 | tf_op jit(solution)/shard_map/ppermute | solution.py:302
  58.6 13.1 %collective-permute-start.9 = (f32[256,256]{1,0:T(8,128)S(1)}, f32[256,256]{1,0:T(8,128)S(1)}, u32[]{:S(2)}, u32[]{:S(2)}) collective-permute-start(f32[256,256]{1,0:T(8,128)S(1)} %core_there.1.refs_0_), channel_id=1, source_target_pairs={{0,4},{2,6},{8,12},{10,14},{16,20},{18,22},{24,28},{26,30},{1,5},{... | collective-permute-start | bytes 786440 | tf_op jit(solution)/shard_map/ppermute | solution.py:302
  73.8 10.0 %collective-permute-start.10 = (f32[1024,256]{1,0:T(8,128)S(1)}, f32[1024,256]{1,0:T(8,128)S(1)}, u32[]{:S(2)}, u32[]{:S(2)}) collective-permute-start(f32[1024,256]{1,0:T(8,128)S(1)} %back_two.1), channel_id=1, source_target_pairs={{0,2},{2,0},{4,6},{6,4},{8,10},{10,8},{12,14},{14,12},{16,18},{18,... | collective-permute-start | bytes 3145736 | tf_op jit(solution)/shard_map/ppermute | solution.py:302
  75.4 18.2 %collective-permute-start.13 = (f32[1024,256]{1,0:T(8,128)S(1)}, f32[1024,256]{1,0:T(8,128)S(1)}, u32[]{:S(2)}, u32[]{:S(2)}) collective-permute-start(f32[1024,256]{1,0:T(8,128)S(1)} %back_far.1), channel_id=1, source_target_pairs={{0,26},{2,0},{4,30},{6,4},{8,2},{10,8},{12,6},{14,12},{16,10},{18,... | collective-permute-start | bytes 3145736 | tf_op jit(solution)/shard_map/ppermute | solution.py:296
  77.8 8.1 %collective-permute-start.11 = (f32[256,256]{1,0:T(8,128)S(1)}, f32[256,256]{1,0:T(8,128)S(1)}, u32[]{:S(2)}, u32[]{:S(2)}) collective-permute-start(f32[256,256]{1,0:T(8,128)S(1)} %core_here.1.one), channel_id=1, source_target_pairs={{0,4},{2,6},{8,12},{10,14},{16,20},{18,22},{24,28},{26,30},{1,5},{... | collective-permute-start | bytes 786440 | tf_op jit(solution)/shard_map/ppermute | solution.py:302
  82.2 6.4 %collective-permute-start.12 = (f32[256,256]{1,0:T(8,128)S(1)}, f32[256,256]{1,0:T(8,128)S(1)}, u32[]{:S(2)}, u32[]{:S(2)}) collective-permute-start(f32[256,256]{1,0:T(8,128)S(1)} %chip_there.1), channel_id=1, source_target_pairs={{0,1},{1,0},{2,3},{3,2},{4,5},{5,4},{6,7},{7,6},{8,9},{9,8},{10,11... | collective-permute-start | bytes 786440 | tf_op jit(solution)/shard_map/ppermute | solution.py:302
  85.4 32.6 %collective-permute-start.21 = (f32[1024,256]{1,0:T(8,128)S(1)}, f32[1024,256]{1,0:T(8,128)S(1)}, u32[]{:S(2)}, u32[]{:S(2)}) collective-permute-start(f32[1024,256]{1,0:T(8,128)S(1)} %back_near.1), channel_id=1, source_target_pairs={{0,30},{2,28},{4,2},{6,0},{8,6},{10,4},{12,10},{14,8},{16,14},{18,... | collective-permute-start | bytes 3145736 | tf_op jit(solution)/shard_map/ppermute | solution.py:296
  89.2 11.5 %collective-permute-start.17 = (f32[512,256]{1,0:T(8,128)S(1)}, f32[512,256]{1,0:T(8,128)S(1)}, u32[]{:S(2)}, u32[]{:S(2)}) collective-permute-start(f32[512,256]{1,0:T(8,128)S(1)} %get-tuple-element.71), channel_id=1, source_target_pairs={{0,1},{1,0},{2,3},{3,2},{4,5},{5,4},{6,7},{7,6},{8,9},{9,8},{10,11... | collective-permute-start | bytes 1572872 | tf_op jit(solution)/shard_map/ppermute | solution.py:302
  90.9 3.5 %collective-permute-start.16 = (f32[128,256]{1,0:T(8,128)S(1)}, f32[128,256]{1,0:T(8,128)S(1)}, u32[]{:S(2)}, u32[]{:S(2)}) collective-permute-start(f32[128,256]{1,0:T(8,128)S(1)} %get-tuple-element.67), channel_id=1, source_target_pairs={{4,28},{6,30},{12,20},{14,22},{20,12},{22,14},{28,4},{30,6},{5,29}... | collective-permute-start | bytes 393224 | tf_op jit(solution)/shard_map/ppermute | solution.py:302
  91.6 2.8 %collective-permute-start.15 = (f32[128,256]{1,0:T(8,128)S(1)}, f32[128,256]{1,0:T(8,128)S(1)}, u32[]{:S(2)}, u32[]{:S(2)}) collective-permute-start(f32[128,256]{1,0:T(8,128)S(1)} %get-tuple-element.68.here), channel_id=1, source_target_pairs={{4,20},{6,22},{12,28},{14,30},{20,4},{22,6},{28,12},{30,14},{5,21}... | collective-permute-start | bytes 393224 | tf_op jit(solution)/shard_map/ppermute | solution.py:302
  93.7 0.7 collective-permute-start.14
  95.0 18.2 %collective-permute-start.20 = (f32[128,256]{1,0:T(8,128)S(1)}, f32[128,256]{1,0:T(8,128)S(1)}, u32[]{:S(2)}, u32[]{:S(2)}) collective-permute-start(f32[128,256]{1,0:T(8,128)S(1)} %line_sum.1.ready), channel_id=1, source_target_pairs={{4,8},{6,10},{12,0},{14,2},{20,24},{22,26},{28,16},{30,18},{5,9},{... | collective-permute-start | bytes 393224 | tf_op jit(solution)/shard_map/ppermute | solution.py:302
  96.3 16.9 %collective-permute-start.19 = (f32[128,256]{1,0:T(8,128)S(1)}, f32[128,256]{1,0:T(8,128)S(1)}, u32[]{:S(2)}, u32[]{:S(2)}) collective-permute-start(f32[128,256]{1,0:T(8,128)S(1)} %line_sum.1.ready), channel_id=1, source_target_pairs={{4,12},{6,14},{12,4},{14,6},{20,28},{22,30},{28,20},{30,22},{5,13}... | collective-permute-start | bytes 393224 | tf_op jit(solution)/shard_map/ppermute | solution.py:302
  96.9 20.5 %collective-permute-start.18 = (f32[128,256]{1,0:T(8,128)S(1)}, f32[128,256]{1,0:T(8,128)S(1)}, u32[]{:S(2)}, u32[]{:S(2)}) collective-permute-start(f32[128,256]{1,0:T(8,128)S(1)} %line_sum.1.ready), channel_id=1, source_target_pairs={{4,0},{6,2},{12,8},{14,10},{20,16},{22,18},{28,24},{30,26},{5,1},{... | collective-permute-start | bytes 393224 | tf_op jit(solution)/shard_map/ppermute | solution.py:302
  118.0 1.8 %collective-permute-start.22 = (f32[256,256]{1,0:T(8,128)S(1)}, f32[256,256]{1,0:T(8,128)S(1)}, u32[]{:S(2)}, u32[]{:S(2)}) collective-permute-start(f32[256,256]{1,0:T(8,128)S(1)} %chip_pick.1.refs_0_), channel_id=1, source_target_pairs={{0,2},{2,0},{4,6},{6,4},{8,10},{10,8},{12,14},{14,12},{16,18},{18,... | collective-permute-start | bytes 786440 | tf_op jit(solution)/shard_map/ppermute | solution.py:302

commit v2 on v1

--- a/solution.py
+++ b/solution.py
@@ -241,7 +241,7 @@
     )[0]
 
 
-def pick_kernel(who, ready, ready_sent, later, later_sent, out):
+def pick_kernel(who, ready, later, ready_sent, later_sent, out):
     rows = ready.shape[0]
     odd = who[CHIP] == 1
     for which, one, other in ((0, ready, ready_sent), (1, later, later_sent)):
@@ -374,10 +374,10 @@
     near = moved(last, "dom", -1, -3)
     last = next(steps)(last)
     act_got = swapped(after(act_there, last), "feat")
-    last = next(steps)(last, far)
     mine = backward("back_own", who, t, [OWN], after(g_there, last), [firsts[3]], 1)[0]
+    last = next(steps)(mine, far)
     activated = join("activated", who, SIDE, [after(act_here, last), act_got], jax.ShapeDtypeStruct)
-    last = next(steps)(activated, mine)
+    last = next(steps)(activated)
     feature_grad = call(
         "feature_grad",
         add_kernel,
@@ -431,7 +431,7 @@
     later = chosen(keep, "dom", lambda i: i ^ 4 if i % 4 >= 2 else None)
     ready_sent = chosen(keep, "dom", lambda i: i - 2 if i % 4 >= 2 else None)
     yield step(
-        lambda *last: pick("chip_pick", who, after(keep, *last), ready_sent, later, later_sent)
+        lambda *last: pick("chip_pick", who, after(keep, *last), later, ready_sent, later_sent)
     )
     got = swapped(box[-1], "dom")
     yield step(

time: 122 us -> 121 us (level)
  waiting for transfers between devices: 40.9 us -> 38.9 us
    ppermute x19, waiting for transfers between devices: 39.5 us -> 37.4 us  [chosen(): lax.ppermute(value, axis, [pair for pair in pairs if pair[1] is not None])]
  transfers between devices with their start and end apart: 23 -> 23, of which waited for: 8 -> 8; matrix products, arithmetic and copies ran while one was open for 0% -> 0% of each run, Pallas kernels for 28% -> 29%
where the time goes in v2:
time: 121 us; the launch traced here: 119 us
  Pallas kernels  43.5 us (36%)
  waiting for transfers between devices  38.9 us (32%)
  starting transfers between devices  31.2 us (26%)
  local copies, waits for them, and re-layouts  4.56 us (4%)
    ppermute x19, waiting for transfers between devices, chosen(): lax.ppermute(value, axis, [pair for pair in pairs if pair[1] is not None])  37.4 us
    pallas_call x23, Pallas kernels, call(): pl.pallas_call(kernel, in_specs=[IN_SMEM] + [IN_VMEM] * len(operands), ou...  36.4 us
    ppermute x19, starting transfers between devices, chosen(): lax.ppermute(value, axis, [pair for pair in pairs if pair[1] is not None])  26.2 us
    pallas_call x1, Pallas kernels, lay_out(): pl.pallas_call(lay_out_kernel, grid_spec=pltpu.PrefetchScalarGridSpec(num...  7.11 us
    ppermute x4, starting transfers between devices, moved(): return lax.ppermute(value, axis, perm)  5.04 us
    unnamed x14, local copies, waits for them, and re-layouts  4.48 us
  transfers between devices with their start and end apart: 23, of which 8 were waited for; matrix products, arithmetic and copies ran while one was open for 0% of the time, Pallas kernels for 29%

profile of v2, /device:TPU:0, one launch (start us, length us, event | category | flops | bytes accessed | tf_op | source)
XLA Modules:
  0.0 119.2 jit_solution(15602468865328368597)
XLA Ops:
  0.6 2.4 %collective-permute-start.1 = (f32[1024,256]{1,0:T(8,128)}, f32[1024,256]{1,0:T(8,128)S(1)}, u32[]{:S(2)}, u32[]{:S(2)}) collective-permute-start(f32[1024,256]{1,0:T(8,128)} %refs_0_.1), channel_id=1, source_target_pairs={{0,6},{2,4},{4,10},{6,8},{8,14},{10,12},{12,18},{14,16},{16,22},{1... | collective-permute-start | bytes 3145736 | tf_op jit(solution)/shard_map/ppermute | solution.py:296
  3.1 0.1 stack.27.who
  3.1 1.2 %copy-done = f32[1024,256]{1,0:T(8,128)S(1)} copy-done((f32[1024,256]{1,0:T(8,128)S(1)}, f32[1024,256]{1,0:T(8,128)}, u32[]{:S(2)}) %copy-start) | copy-done | bytes 1048600
  4.4 0.6 cot_give.1
  5.0 1.6 %collective-permute-start.3 = (f32[512,256]{1,0:T(8,128)S(1)}, f32[512,256]{1,0:T(8,128)S(1)}, u32[]{:S(2)}, u32[]{:S(2)}) collective-permute-start(f32[512,256]{1,0:T(8,128)S(1)} %cot_give.1), channel_id=1, source_target_pairs={{0,1},{1,0},{2,3},{3,2},{4,5},{5,4},{6,7},{7,6},{8,9},{9,8},{10,11... | collective-permute-start | bytes 1572872 | tf_op jit(solution)/shard_map/ppermute | solution.py:302
  6.5 0.5 collective-permute-start.2
  7.1 0.1 collective-permute-start
  7.2 0.7 copy-done.4
  7.9 0.7 copy-done.5
  8.6 0.7 copy-done.6
  9.2 7.1 %lay_out.1 = (bf16[2,4,1024,1024]{3,2,1,0:T(8,128)(2,1)S(1)}, bf16[2,4,1024,1024]{3,2,1,0:T(8,128)(2,1)S(1)}) custom-call(s32[4,24]{1,0:T(4,128)S(1)} %bitcast.9, s32[4,24]{1,0:T(4,128)S(1)} %bitcast.10, s32[1,4]{1,0:T(1,128)S(1)} %copy-done.6, s32[8]{0:T(128)S(1)} %stack.27.who, f32[4,24,128,128]{3,2,1,0:T(8,128)} %bitcast.11), custom_call_target="tpu_custom_call" | custom-call | bytes 20000000 | tf_op jit(solution)/shard_map/lay_out/pallas_call | solution.py:75
  16.3 0.0 copy-start.2
  16.3 1.2 %copy-done.2 = f32[1024,256]{1,0:T(8,128)S(1)} copy-done((f32[1024,256]{1,0:T(8,128)S(1)}, f32[1024,256]{1,0:T(8,128)}, u32[]{:S(2)}) %copy-start.2) | copy-done | bytes 1048600
  17.6 3.0 %agg_own.1.refs_1_ = f32[1024,256]{1,0:T(8,128)S(1)} custom-call(s32[8]{0:T(128)S(1)} %stack.27.who, bf16[2,4,1024,1024]{3,2,1,0:T(8,128)(2,1)S(1)} %get-tuple-element.40.matrix, f32[1024,256]{1,0:T(8,128)S(1)} %copy-done.2), custom_call_target="tpu_custom_call" | custom-call | flops 1610612736 | bytes 17825792 | tf_op jit(solution)/shard_map/agg_own/pallas_call | solution.py:39
  20.6 0.0 collective-permute-done.3.cot_there
  20.6 10.1 %collective-permute-done.2.w_there = f32[512,256]{1,0:T(8,128)S(1)} collective-permute-done((f32[512,256]{1,0:T(8,128)}, f32[512,256]{1,0:T(8,128)S(1)}, u32[]{:S(2)}, u32[]{:S(2)}) %collective-permute-start.2) | collective-permute-done | bytes 524320 | tf_op jit(solution)/shard_map/ppermute | solution.py:302
  30.8 3.0 %agg_near.1.refs_2_ = f32[1024,256]{1,0:T(8,128)S(1)} custom-call(s32[8]{0:T(128)S(1)} %stack.27.who, bf16[2,4,1024,1024]{3,2,1,0:T(8,128)(2,1)S(1)} %get-tuple-element.40.matrix, f32[1024,256]{1,0:T(8,128)S(1)} %collective-permute-done.1.refs_0_, f32[1024,256]{1,0:T(8,128)S(1)} %agg_own.1.refs_1_), custom_call_target="tpu_custom_call" | custom-call | flops 1610612736 | bytes 18874368 | tf_op jit(solution)/shard_map/agg_near/pallas_call | solution.py:39
  33.8 0.0 copy-start.1
  33.8 0.0 copy-start.3
  33.9 2.8 %agg_give.1 = f32[512,256]{1,0:T(8,128)S(1)} custom-call(s32[8]{0:T(128)S(1)} %stack.27.who, bf16[2,4,1024,1024]{3,2,1,0:T(8,128)(2,1)S(1)} %get-tuple-element.40.matrix, f32[1024,256]{1,0:T(8,128)S(1)} %collective-permute-done.refs_0_, f32[1024,256]{1,0:T(8,128)S(1)} %collective-permute-done.4.refs_1_, f32[1024,256]{1,0:T(8,128)S(1)} %agg_near.1.refs_2_), custom_call_target="tpu_custom_call" | custom-call | flops 1610612736 | bytes 19922944 | tf_op jit(solution)/shard_map/agg_give/pallas_call | solution.py:39
  36.7 1.6 %collective-permute-start.5 = (f32[512,256]{1,0:T(8,128)S(1)}, f32[512,256]{1,0:T(8,128)S(1)}, u32[]{:S(2)}, u32[]{:S(2)}) collective-permute-start(f32[512,256]{1,0:T(8,128)S(1)} %agg_give.1), channel_id=1, source_target_pairs={{0,1},{1,0},{2,3},{3,2},{4,5},{5,4},{6,7},{7,6},{8,9},{9,8},{10,11... | collective-permute-start | bytes 1572872 | tf_op jit(solution)/shard_map/ppermute | solution.py:302
  38.3 2.8 %agg_keep.1.own = f32[512,256]{1,0:T(8,128)S(1)} custom-call(s32[8]{0:T(128)S(1)} %stack.27.who, bf16[2,4,1024,1024]{3,2,1,0:T(8,128)(2,1)S(1)} %get-tuple-element.40.matrix, f32[1024,256]{1,0:T(8,128)S(1)} %collective-permute-done.refs_0_, f32[1024,256]{1,0:T(8,128)S(1)} %collective-permute-done.4.refs_1_, f32[1024,256]{1,0:T(8,128)S(1)} %agg_near.1.refs_2_), custom_call_target="tpu_custom_call" | custom-call | flops 1610612736 | bytes 19922944 | tf_op jit(solution)/shard_map/agg_keep/pallas_call | solution.py:39
  41.1 10.0 %collective-permute-done.5.far = f32[512,256]{1,0:T(8,128)S(1)} collective-permute-done((f32[512,256]{1,0:T(8,128)S(1)}, f32[512,256]{1,0:T(8,128)S(1)}, u32[]{:S(2)}, u32[]{:S(2)}) %collective-permute-start.5) | collective-permute-done | bytes 524320 | tf_op jit(solution)/shard_map/ppermute | solution.py:302
  51.1 2.3 %middle.1 = (f32[512,256]{1,0:T(8,128)S(1)}, f32[512,256]{1,0:T(8,128)S(1)}, f32[512,256]{1,0:T(8,128)S(1)}, f32[512,256]{1,0:T(8,128)S(1)}, f32[512,256]{1,0:T(8,128)S(1)}) custom-call(s32[8]{0:T(128)S(1)} %stack.27.who, f32[512,256]{1,0:T(8,128)S(1)} %agg_keep.1.own, f32[512,256]{1,0:T(8,128)S(1)} %collective-permute-done.5.far, f32[512,256]{1,0:T(8,128)S(1)} %copy-done.3, ...), custom_call_target="tpu_custom_call" | custom-call | flops 1207959552 | bytes 3670016 | tf_op jit(solution)/shard_map/middle/pallas_call | solution.py:39
  53.4 1.2 %weight_give.1 = (f32[256,256]{1,0:T(8,128)S(1)}, f32[256,256]{1,0:T(8,128)S(1)}) custom-call(s32[8]{0:T(128)S(1)} %stack.27.who, f32[512,256]{1,0:T(8,128)S(1)} %agg_keep.1.own, f32[512,256]{1,0:T(8,128)S(1)} %collective-permute-done.5.far, f32[512,256]{1,0:T(8,128)S(1)} %get-tuple-element.56.grad_here, f32[512,256]{1,0:T(8,128)S(1)} %get-tuple-element.46.grad_there), custom_call_target="tpu_custom_call" | custom-call | flops 402653184 | bytes 2097152 | tf_op jit(solution)/shard_map/weight_give/pallas_call | solution.py:39
  54.7 0.1 collective-permute-start.6
  54.7 0.5 collective-permute-start.7
  55.2 1.5 %collective-permute-start.8 = (f32[512,256]{1,0:T(8,128)S(1)}, f32[512,256]{1,0:T(8,128)S(1)}, u32[]{:S(2)}, u32[]{:S(2)}) collective-permute-start(f32[512,256]{1,0:T(8,128)S(1)} %get-tuple-element.55), channel_id=1, source_target_pairs={{0,1},{1,0},{2,3},{3,2},{4,5},{5,4},{6,7},{7,6},{8,9},{9,8},{10,11... | collective-permute-start | bytes 1572872 | tf_op jit(solution)/shard_map/ppermute | solution.py:302
  56.8 1.2 %weight_keep.1 = (f32[256,256]{1,0:T(8,128)S(1)}, f32[256,256]{1,0:T(8,128)S(1)}) custom-call(s32[8]{0:T(128)S(1)} %stack.27.who, f32[512,256]{1,0:T(8,128)S(1)} %agg_keep.1.own, f32[512,256]{1,0:T(8,128)S(1)} %collective-permute-done.5.far, f32[512,256]{1,0:T(8,128)S(1)} %get-tuple-element.56.grad_here, f32[512,256]{1,0:T(8,128)S(1)} %get-tuple-element.46.grad_there), custom_call_target="tpu_custom_call" | custom-call | flops 402653184 | bytes 2097152 | tf_op jit(solution)/shard_map/weight_keep/pallas_call | solution.py:39
  58.0 0.6 core_there.1.refs_0_
  58.6 7.4 %collective-permute-start.9 = (f32[256,256]{1,0:T(8,128)S(1)}, f32[256,256]{1,0:T(8,128)S(1)}, u32[]{:S(2)}, u32[]{:S(2)}) collective-permute-start(f32[256,256]{1,0:T(8,128)S(1)} %core_there.1.refs_0_), channel_id=1, source_target_pairs={{0,4},{2,6},{8,12},{10,14},{16,20},{18,22},{24,28},{26,30},{1,5},{... | collective-permute-start | bytes 786440 | tf_op jit(solution)/shard_map/ppermute | solution.py:302
  66.0 0.6 core_here.1.one
  66.5 1.2 keep.1.source
  67.7 3.9 %back_here.1 = (f32[1024,256]{1,0:T(8,128)S(1)}, f32[1024,256]{1,0:T(8,128)S(1)}, f32[1024,256]{1,0:T(8,128)S(1)}, f32[1024,256]{1,0:T(8,128)S(1)}) custom-call(s32[8]{0:T(128)S(1)} %stack.27.who, bf16[2,4,1024,1024]{3,2,1,0:T(8,128)(2,1)S(1)} %get-tuple-element.54.matrix, f32[512,256]{1,0:T(8,128)S(1)} %keep.1.source), custom_call_target="tpu_custom_call" | custom-call | flops 3221225472 | bytes 17301504 | tf_op jit(solution)/shard_map/back_here/pallas_call | solution.py:39
  71.7 0.6 chip_there.1
  72.3 1.5 %back_two.1 = f32[1024,256]{1,0:T(8,128)S(1)} custom-call(s32[8]{0:T(128)S(1)} %stack.27.who, bf16[2,4,1024,1024]{3,2,1,0:T(8,128)(2,1)S(1)} %get-tuple-element.54.matrix, f32[512,256]{1,0:T(8,128)S(1)} %collective-permute-done.8.source, f32[1024,256]{1,0:T(8,128)S(1)} %get-tuple-element.58.refs_0_), custom_call_target="tpu_custom_call" | custom-call | flops 805306368 | bytes 18350080 | tf_op jit(solution)/shard_map/back_two/pallas_call | solution.py:39
  73.8 0.1 collective-permute-start.10
  73.9 1.5 %back_far.1 = f32[1024,256]{1,0:T(8,128)S(1)} custom-call(s32[8]{0:T(128)S(1)} %stack.27.who, bf16[2,4,1024,1024]{3,2,1,0:T(8,128)(2,1)S(1)} %get-tuple-element.54.matrix, f32[512,256]{1,0:T(8,128)S(1)} %collective-permute-done.8.source, f32[1024,256]{1,0:T(8,128)S(1)} %get-tuple-element.62.refs_0_), custom_call_target="tpu_custom_call" | custom-call | flops 805306368 | bytes 18350080 | tf_op jit(solution)/shard_map/back_far/pallas_call | solution.py:39
  75.4 2.4 %collective-permute-start.13 = (f32[1024,256]{1,0:T(8,128)S(1)}, f32[1024,256]{1,0:T(8,128)S(1)}, u32[]{:S(2)}, u32[]{:S(2)}) collective-permute-start(f32[1024,256]{1,0:T(8,128)S(1)} %back_far.1), channel_id=1, source_target_pairs={{0,26},{2,0},{4,30},{6,4},{8,2},{10,8},{12,6},{14,12},{16,10},{18,... | collective-permute-start | bytes 3145736 | tf_op jit(solution)/shard_map/ppermute | solution.py:296
  77.8 4.3 %collective-permute-start.11 = (f32[256,256]{1,0:T(8,128)S(1)}, f32[256,256]{1,0:T(8,128)S(1)}, u32[]{:S(2)}, u32[]{:S(2)}) collective-permute-start(f32[256,256]{1,0:T(8,128)S(1)} %core_here.1.one), channel_id=1, source_target_pairs={{0,4},{2,6},{8,12},{10,14},{16,20},{18,22},{24,28},{26,30},{1,5},{... | collective-permute-start | bytes 786440 | tf_op jit(solution)/shard_map/ppermute | solution.py:302
  82.2 1.7 %collective-permute-start.12 = (f32[256,256]{1,0:T(8,128)S(1)}, f32[256,256]{1,0:T(8,128)S(1)}, u32[]{:S(2)}, u32[]{:S(2)}) collective-permute-start(f32[256,256]{1,0:T(8,128)S(1)} %chip_there.1), channel_id=1, source_target_pairs={{0,1},{1,0},{2,3},{3,2},{4,5},{5,4},{6,7},{7,6},{8,9},{9,8},{10,11... | collective-permute-start | bytes 786440 | tf_op jit(solution)/shard_map/ppermute | solution.py:302
  83.8 1.5 %back_near.1 = f32[1024,256]{1,0:T(8,128)S(1)} custom-call(s32[8]{0:T(128)S(1)} %stack.27.who, bf16[2,4,1024,1024]{3,2,1,0:T(8,128)(2,1)S(1)} %get-tuple-element.54.matrix, f32[512,256]{1,0:T(8,128)S(1)} %collective-permute-done.8.source, f32[1024,256]{1,0:T(8,128)S(1)} %get-tuple-element.64.refs_0_, f32[1024,256]{1,0:T(8,128)S(1)} %collective-permute-done.10.refs_1_), custom_call_target="tpu_custom_call" | custom-call | flops 805306368 | bytes 19398656 | tf_op jit(solution)/shard_map/back_near/pallas_call | solution.py:39
  85.4 0.1 collective-permute-start.21
  85.5 0.5 collective-permute-done.11.two
  85.9 2.7 %collective-permute-done.12.three = f32[256,256]{1,0:T(8,128)S(1)} collective-permute-done((f32[256,256]{1,0:T(8,128)S(1)}, f32[256,256]{1,0:T(8,128)S(1)}, u32[]{:S(2)}, u32[]{:S(2)}) %collective-permute-start.12) | collective-permute-done | bytes 262176 | tf_op jit(solution)/shard_map/ppermute | solution.py:302
  88.6 0.6 side_sum.1
  89.2 1.7 %collective-permute-start.17 = (f32[512,256]{1,0:T(8,128)S(1)}, f32[512,256]{1,0:T(8,128)S(1)}, u32[]{:S(2)}, u32[]{:S(2)}) collective-permute-start(f32[512,256]{1,0:T(8,128)S(1)} %get-tuple-element.73), channel_id=1, source_target_pairs={{0,1},{1,0},{2,3},{3,2},{4,5},{5,4},{6,7},{7,6},{8,9},{9,8},{10,11... | collective-permute-start | bytes 1572872 | tf_op jit(solution)/shard_map/ppermute | solution.py:302
  90.9 0.7 collective-permute-start.16
  91.6 0.7 collective-permute-start.15
  92.2 1.4 %collective-permute-done.13.refs_1_ = f32[1024,256]{1,0:T(8,128)S(1)} collective-permute-done((f32[1024,256]{1,0:T(8,128)S(1)}, f32[1024,256]{1,0:T(8,128)S(1)}, u32[]{:S(2)}, u32[]{:S(2)}) %collective-permute-start.13) | collective-permute-done | bytes 1048608 | tf_op jit(solution)/shard_map/ppermute | solution.py:296
  93.7 0.7 collective-permute-start.14
  94.3 1.5 %back_own.1.refs_0_ = f32[1024,256]{1,0:T(8,128)S(1)} custom-call(s32[8]{0:T(128)S(1)} %stack.27.who, bf16[2,4,1024,1024]{3,2,1,0:T(8,128)(2,1)S(1)} %get-tuple-element.54.matrix, f32[512,256]{1,0:T(8,128)S(1)} %collective-permute-done.8.source, f32[1024,256]{1,0:T(8,128)S(1)} %get-tuple-element.69.refs_0_), custom_call_target="tpu_custom_call" | custom-call | flops 805306368 | bytes 18350080 | tf_op jit(solution)/shard_map/back_own/pallas_call | solution.py:39
  95.9 0.6 line_sum.1.ready
  96.5 1.3 %collective-permute-start.20 = (f32[128,256]{1,0:T(8,128)S(1)}, f32[128,256]{1,0:T(8,128)S(1)}, u32[]{:S(2)}, u32[]{:S(2)}) collective-permute-start(f32[128,256]{1,0:T(8,128)S(1)} %line_sum.1.ready), channel_id=1, source_target_pairs={{4,8},{6,10},{12,0},{14,2},{20,24},{22,26},{28,16},{30,18},{5,9},{... | collective-permute-start | bytes 393224 | tf_op jit(solution)/shard_map/ppermute | solution.py:302
  97.8 1.3 %collective-permute-start.19 = (f32[128,256]{1,0:T(8,128)S(1)}, f32[128,256]{1,0:T(8,128)S(1)}, u32[]{:S(2)}, u32[]{:S(2)}) collective-permute-start(f32[128,256]{1,0:T(8,128)S(1)} %line_sum.1.ready), channel_id=1, source_target_pairs={{4,0},{6,2},{12,8},{14,10},{20,16},{22,18},{28,24},{30,26},{5,1},{... | collective-permute-start | bytes 393224 | tf_op jit(solution)/shard_map/ppermute | solution.py:302
  99.1 0.7 collective-permute-start.18
  99.8 0.9 collective-permute-done.17.refs_1_
  100.7 1.6 %activated.1 = f32[1024,256]{1,0:T(8,128)} custom-call(s32[8]{0:T(128)S(1)} %stack.27.who, f32[512,256]{1,0:T(8,128)S(1)} %get-tuple-element.71.refs_0_, f32[512,256]{1,0:T(8,128)S(1)} %collective-permute-done.17.refs_1_), custom_call_target="tpu_custom_call" | custom-call | bytes 1048576 | tf_op jit(solution)/shard_map/activated/pallas_call | solution.py:39
  102.3 11.7 %collective-permute-done.20.later_sent = f32[128,256]{1,0:T(8,128)S(1)} collective-permute-done((f32[128,256]{1,0:T(8,128)S(1)}, f32[128,256]{1,0:T(8,128)S(1)}, u32[]{:S(2)}, u32[]{:S(2)}) %collective-permute-start.20) | collective-permute-done | bytes 131104 | tf_op jit(solution)/shard_map/ppermute | solution.py:302
  113.9 1.5 %collective-permute-done.19.ready_sent = f32[128,256]{1,0:T(8,128)S(1)} collective-permute-done((f32[128,256]{1,0:T(8,128)S(1)}, f32[128,256]{1,0:T(8,128)S(1)}, u32[]{:S(2)}, u32[]{:S(2)}) %collective-permute-start.19) | collective-permute-done | bytes 131104 | tf_op jit(solution)/shard_map/ppermute | solution.py:302
  115.5 0.6 chip_pick.1.refs_0_
  116.0 0.1 collective-permute-start.22
  116.1 1.7 %feature_grad.1 = f32[1024,256]{1,0:T(8,128)} custom-call(s32[8]{0:T(128)S(1)} %stack.27.who, f32[1024,256]{1,0:T(8,128)S(1)} %back_own.1.refs_0_, f32[1024,256]{1,0:T(8,128)S(1)} %collective-permute-done.13.refs_1_, f32[1024,256]{1,0:T(8,128)S(1)} %collective-permute-done.21.refs_2_), custom_call_target="tpu_custom_call" | custom-call | bytes 3145728 | tf_op jit(solution)/shard_map/feature_grad/pallas_call | solution.py:39
  117.8 1.4 %weight_grad.1 = f32[512,256]{1,0:T(8,128)} custom-call(s32[8]{0:T(128)S(1)} %stack.27.who, f32[256,256]{1,0:T(8,128)S(1)} %chip_pick.1.refs_0_, f32[256,256]{1,0:T(8,128)S(1)} %collective-permute-done.22.refs_1_), custom_call_target="tpu_custom_call" | custom-call | bytes 524288 | tf_op jit(solution)/shard_map/weight_grad/pallas_call | solution.py:39
  (21 shorter events, 0.1 us)
Async XLA Ops:
  0.6 30.1 %collective-permute-start.1 = (f32[1024,256]{1,0:T(8,128)}, f32[1024,256]{1,0:T(8,128)S(1)}, u32[]{:S(2)}, u32[]{:S(2)}) collective-permute-start(f32[1024,256]{1,0:T(8,128)} %refs_0_.1), channel_id=1, source_target_pairs={{0,6},{2,4},{4,10},{6,8},{8,14},{10,12},{12,18},{14,16},{16,22},{1... | collective-permute-start | bytes 3145736 | tf_op jit(solution)/shard_map/ppermute | solution.py:296
  3.1 1.2 %copy-start = (f32[1024,256]{1,0:T(8,128)S(1)}, f32[1024,256]{1,0:T(8,128)}, u32[]{:S(2)}) copy-start(f32[1024,256]{1,0:T(8,128)} %cot.1) | copy-start | bytes 3145732
  5.0 15.6 %collective-permute-start.3 = (f32[512,256]{1,0:T(8,128)S(1)}, f32[512,256]{1,0:T(8,128)S(1)}, u32[]{:S(2)}, u32[]{:S(2)}) collective-permute-start(f32[512,256]{1,0:T(8,128)S(1)} %cot_give.1), channel_id=1, source_target_pairs={{0,1},{1,0},{2,3},{3,2},{4,5},{5,4},{6,7},{7,6},{8,9},{9,8},{10,11... | collective-permute-start | bytes 1572872 | tf_op jit(solution)/shard_map/ppermute | solution.py:302
  6.5 24.2 %collective-permute-start.2 = (f32[512,256]{1,0:T(8,128)}, f32[512,256]{1,0:T(8,128)S(1)}, u32[]{:S(2)}, u32[]{:S(2)}) collective-permute-start(f32[512,256]{1,0:T(8,128)} %w_here.3), channel_id=1, source_target_pairs={{0,1},{1,0},{2,3},{3,2},{4,5},{5,4},{6,7},{7,6},{8,9},{9,8},{10,11... | collective-permute-start | bytes 1572872 | tf_op jit(solution)/shard_map/ppermute | solution.py:302
  7.1 26.8 %collective-permute-start = (f32[1024,256]{1,0:T(8,128)}, f32[1024,256]{1,0:T(8,128)S(1)}, u32[]{:S(2)}, u32[]{:S(2)}) collective-permute-start(f32[1024,256]{1,0:T(8,128)} %refs_0_.1), channel_id=1, source_target_pairs={{0,2},{2,8},{4,6},{6,12},{8,10},{10,16},{12,14},{14,20},{16,18},{1... | collective-permute-start | bytes 3145736 | tf_op jit(solution)/shard_map/ppermute | solution.py:296
  7.2 0.7 copy-start.4
  7.9 0.7 copy-start.5
  8.6 0.7 copy-start.6
  16.3 1.2 %copy-start.2 = (f32[1024,256]{1,0:T(8,128)S(1)}, f32[1024,256]{1,0:T(8,128)}, u32[]{:S(2)}) copy-start(f32[1024,256]{1,0:T(8,128)} %refs_0_.1) | copy-start | bytes 3145732
  30.8 3.1 %collective-permute-start.4 = (f32[1024,256]{1,0:T(8,128)S(1)}, f32[1024,256]{1,0:T(8,128)S(1)}, u32[]{:S(2)}, u32[]{:S(2)}) collective-permute-start(f32[1024,256]{1,0:T(8,128)S(1)} %collective-permute-done.1.refs_0_), channel_id=1, source_target_pairs={{0,2},{2,0},{4,6},{6,4},{8,10},{10,8},{12,14},{14,12},{16,18},{18,... | collective-permute-start | bytes 3145736 | tf_op jit(solution)/shard_map/ppermute | solution.py:302
  33.8 17.3 %copy-start.1 = (f32[1024,256]{1,0:T(8,128)S(1)}, f32[1024,256]{1,0:T(8,128)}, u32[]{:S(2)}) copy-start(f32[1024,256]{1,0:T(8,128)} %cot.1) | copy-start | bytes 3145732
  33.8 17.3 %copy-start.3 = (f32[512,256]{1,0:T(8,128)S(1)}, f32[512,256]{1,0:T(8,128)}, u32[]{:S(2)}) copy-start(f32[512,256]{1,0:T(8,128)} %w_here.3) | copy-start | bytes 1572868
  36.7 14.4 %collective-permute-start.5 = (f32[512,256]{1,0:T(8,128)S(1)}, f32[512,256]{1,0:T(8,128)S(1)}, u32[]{:S(2)}, u32[]{:S(2)}) collective-permute-start(f32[512,256]{1,0:T(8,128)S(1)} %agg_give.1), channel_id=1, source_target_pairs={{0,1},{1,0},{2,3},{3,2},{4,5},{5,4},{6,7},{7,6},{8,9},{9,8},{10,11... | collective-permute-start | bytes 1572872 | tf_op jit(solution)/shard_map/ppermute | solution.py:302
  54.7 3.3 %collective-permute-start.6 = (f32[256,256]{1,0:T(8,128)S(1)}, f32[256,256]{1,0:T(8,128)S(1)}, u32[]{:S(2)}, u32[]{:S(2)}) collective-permute-start(f32[256,256]{1,0:T(8,128)S(1)} %get-tuple-element.52), channel_id=1, source_target_pairs={{0,2},{2,0},{4,6},{6,4},{8,10},{10,8},{12,14},{14,12},{16,18},{18,... | collective-permute-start | bytes 786440 | tf_op jit(solution)/shard_map/ppermute | solution.py:302
  54.7 11.2 %collective-permute-start.7 = (f32[256,256]{1,0:T(8,128)S(1)}, f32[256,256]{1,0:T(8,128)S(1)}, u32[]{:S(2)}, u32[]{:S(2)}) collective-permute-start(f32[256,256]{1,0:T(8,128)S(1)} %get-tuple-element.47), channel_id=1, source_target_pairs={{0,2},{2,0},{4,6},{6,4},{8,10},{10,8},{12,14},{14,12},{16,18},{18,... | collective-permute-start | bytes 786440 | tf_op jit(solution)/shard_map/ppermute | solution.py:302
  55.2 17.0 %collective-permute-start.8 = (f32[512,256]{1,0:T(8,128)S(1)}, f32[512,256]{1,0:T(8,128)S(1)}, u32[]{:S(2)}, u32[]{:S(2)}) collective-permute-start(f32[512,256]{1,0:T(8,128)S(1)} %get-tuple-element.55), channel_id=1, source_target_pairs={{0,1},{1,0},{2,3},{3,2},{4,5},{5,4},{6,7},{7,6},{8,9},{9,8},{10,11... | collective-permute-start | bytes 1572872 | tf_op jit(solution)/shard_map/ppermute | solution.py:302
  58.6 13.1 %collective-permute-start.9 = (f32[256,256]{1,0:T(8,128)S(1)}, f32[256,256]{1,0:T(8,128)S(1)}, u32[]{:S(2)}, u32[]{:S(2)}) collective-permute-start(f32[256,256]{1,0:T(8,128)S(1)} %core_there.1.refs_0_), channel_id=1, source_target_pairs={{0,4},{2,6},{8,12},{10,14},{16,20},{18,22},{24,28},{26,30},{1,5},{... | collective-permute-start | bytes 786440 | tf_op jit(solution)/shard_map/ppermute | solution.py:302
  73.8 10.0 %collective-permute-start.10 = (f32[1024,256]{1,0:T(8,128)S(1)}, f32[1024,256]{1,0:T(8,128)S(1)}, u32[]{:S(2)}, u32[]{:S(2)}) collective-permute-start(f32[1024,256]{1,0:T(8,128)S(1)} %back_two.1), channel_id=1, source_target_pairs={{0,2},{2,0},{4,6},{6,4},{8,10},{10,8},{12,14},{14,12},{16,18},{18,... | collective-permute-start | bytes 3145736 | tf_op jit(solution)/shard_map/ppermute | solution.py:302
  75.4 18.2 %collective-permute-start.13 = (f32[1024,256]{1,0:T(8,128)S(1)}, f32[1024,256]{1,0:T(8,128)S(1)}, u32[]{:S(2)}, u32[]{:S(2)}) collective-permute-start(f32[1024,256]{1,0:T(8,128)S(1)} %back_far.1), channel_id=1, source_target_pairs={{0,26},{2,0},{4,30},{6,4},{8,2},{10,8},{12,6},{14,12},{16,10},{18,... | collective-permute-start | bytes 3145736 | tf_op jit(solution)/shard_map/ppermute | solution.py:296
  77.8 8.1 %collective-permute-start.11 = (f32[256,256]{1,0:T(8,128)S(1)}, f32[256,256]{1,0:T(8,128)S(1)}, u32[]{:S(2)}, u32[]{:S(2)}) collective-permute-start(f32[256,256]{1,0:T(8,128)S(1)} %core_here.1.one), channel_id=1, source_target_pairs={{0,4},{2,6},{8,12},{10,14},{16,20},{18,22},{24,28},{26,30},{1,5},{... | collective-permute-start | bytes 786440 | tf_op jit(solution)/shard_map/ppermute | solution.py:302
  82.2 6.4 %collective-permute-start.12 = (f32[256,256]{1,0:T(8,128)S(1)}, f32[256,256]{1,0:T(8,128)S(1)}, u32[]{:S(2)}, u32[]{:S(2)}) collective-permute-start(f32[256,256]{1,0:T(8,128)S(1)} %chip_there.1), channel_id=1, source_target_pairs={{0,1},{1,0},{2,3},{3,2},{4,5},{5,4},{6,7},{7,6},{8,9},{9,8},{10,11... | collective-permute-start | bytes 786440 | tf_op jit(solution)/shard_map/ppermute | solution.py:302
  85.4 30.7 %collective-permute-start.21 = (f32[1024,256]{1,0:T(8,128)S(1)}, f32[1024,256]{1,0:T(8,128)S(1)}, u32[]{:S(2)}, u32[]{:S(2)}) collective-permute-start(f32[1024,256]{1,0:T(8,128)S(1)} %back_near.1), channel_id=1, source_target_pairs={{0,30},{2,28},{4,2},{6,0},{8,6},{10,4},{12,10},{14,8},{16,14},{18,... | collective-permute-start | bytes 3145736 | tf_op jit(solution)/shard_map/ppermute | solution.py:296
  89.2 11.5 %collective-permute-start.17 = (f32[512,256]{1,0:T(8,128)S(1)}, f32[512,256]{1,0:T(8,128)S(1)}, u32[]{:S(2)}, u32[]{:S(2)}) collective-permute-start(f32[512,256]{1,0:T(8,128)S(1)} %get-tuple-element.73), channel_id=1, source_target_pairs={{0,1},{1,0},{2,3},{3,2},{4,5},{5,4},{6,7},{7,6},{8,9},{9,8},{10,11... | collective-permute-start | bytes 1572872 | tf_op jit(solution)/shard_map/ppermute | solution.py:302
  90.9 5.0 %collective-permute-start.16 = (f32[128,256]{1,0:T(8,128)S(1)}, f32[128,256]{1,0:T(8,128)S(1)}, u32[]{:S(2)}, u32[]{:S(2)}) collective-permute-start(f32[128,256]{1,0:T(8,128)S(1)} %get-tuple-element.67), channel_id=1, source_target_pairs={{4,28},{6,30},{12,20},{14,22},{20,12},{22,14},{28,4},{30,6},{5,29}... | collective-permute-start | bytes 393224 | tf_op jit(solution)/shard_map/ppermute | solution.py:302
  91.6 4.3 %collective-permute-start.15 = (f32[128,256]{1,0:T(8,128)S(1)}, f32[128,256]{1,0:T(8,128)S(1)}, u32[]{:S(2)}, u32[]{:S(2)}) collective-permute-start(f32[128,256]{1,0:T(8,128)S(1)} %get-tuple-element.70.here), channel_id=1, source_target_pairs={{4,20},{6,22},{12,28},{14,30},{20,4},{22,6},{28,12},{30,14},{5,21}... | collective-permute-start | bytes 393224 | tf_op jit(solution)/shard_map/ppermute | solution.py:302
  93.7 2.2 %collective-permute-start.14 = (f32[128,256]{1,0:T(8,128)S(1)}, f32[128,256]{1,0:T(8,128)S(1)}, u32[]{:S(2)}, u32[]{:S(2)}) collective-permute-start(f32[128,256]{1,0:T(8,128)S(1)} %get-tuple-element.67), channel_id=1, source_target_pairs={{4,12},{6,14},{12,4},{14,6},{20,28},{22,30},{28,20},{30,22},{5,13}... | collective-permute-start | bytes 393224 | tf_op jit(solution)/shard_map/ppermute | solution.py:302
  96.5 17.4 %collective-permute-start.20 = (f32[128,256]{1,0:T(8,128)S(1)}, f32[128,256]{1,0:T(8,128)S(1)}, u32[]{:S(2)}, u32[]{:S(2)}) collective-permute-start(f32[128,256]{1,0:T(8,128)S(1)} %line_sum.1.ready), channel_id=1, source_target_pairs={{4,8},{6,10},{12,0},{14,2},{20,24},{22,26},{28,16},{30,18},{5,9},{... | collective-permute-start | bytes 393224 | tf_op jit(solution)/shard_map/ppermute | solution.py:302
  97.8 17.7 %collective-permute-start.19 = (f32[128,256]{1,0:T(8,128)S(1)}, f32[128,256]{1,0:T(8,128)S(1)}, u32[]{:S(2)}, u32[]{:S(2)}) collective-permute-start(f32[128,256]{1,0:T(8,128)S(1)} %line_sum.1.ready), channel_id=1, source_target_pairs={{4,0},{6,2},{12,8},{14,10},{20,16},{22,18},{28,24},{30,26},{5,1},{... | collective-permute-start | bytes 393224 | tf_op jit(solution)/shard_map/ppermute | solution.py:302
  99.1 16.4 %collective-permute-start.18 = (f32[128,256]{1,0:T(8,128)S(1)}, f32[128,256]{1,0:T(8,128)S(1)}, u32[]{:S(2)}, u32[]{:S(2)}) collective-permute-start(f32[128,256]{1,0:T(8,128)S(1)} %line_sum.1.ready), channel_id=1, source_target_pairs={{4,12},{6,14},{12,4},{14,6},{20,28},{22,30},{28,20},{30,22},{5,13}... | collective-permute-start | bytes 393224 | tf_op jit(solution)/shard_map/ppermute | solution.py:302
  116.0 1.8 %collective-permute-start.22 = (f32[256,256]{1,0:T(8,128)S(1)}, f32[256,256]{1,0:T(8,128)S(1)}, u32[]{:S(2)}, u32[]{:S(2)}) collective-permute-start(f32[256,256]{1,0:T(8,128)S(1)} %chip_pick.1.refs_0_), channel_id=1, source_target_pairs={{0,2},{2,0},{4,6},{6,4},{8,10},{10,8},{12,14},{14,12},{16,18},{18,... | collective-permute-start | bytes 786440 | tf_op jit(solution)/shard_map/ppermute | solution.py:302

commit v3 on v0

--- a/solution.py
+++ b/solution.py
@@ -87,15 +87,18 @@
     )(rows, cols, counts, who, pltpu.with_memory_space_constraint(blocks, pltpu.HBM))
 
 
-def forward_kernel(slots, part, has_base, who, matrix, *refs):
+def forward_kernel(slots, halves, part, has_base, who, matrix, *refs):
     n = len(slots)
-    sources, refs = refs[:n], refs[n:]
+    sources, refs = list(refs[: sum(halves)]), refs[sum(halves) :]
     base, refs = (refs[0], refs[1:]) if has_base else (None, refs)
     out, (highs, lows) = refs[0], refs[1:]
     rows = out.shape[0]
     from_row = 0 if part is None else (who[SIDE] ^ part) * rows
-    for i, source in enumerate(sources):
-        highs[i], lows[i] = split(source[...])
+    for i in range(n):
+        depth = highs.shape[1] // halves[i]
+        for k in range(halves[i]):
+            at = pl.ds(k * depth, depth)
+            highs[i, at, :], lows[i, at, :] = split(sources.pop(0)[...])
 
     def tile(k, carry):
         there = pl.ds(pl.multiple_of(k * TILE, TILE), TILE)
@@ -115,13 +118,17 @@
 
 def forward(name, who, matrix, terms, base=None, part=None):
     slots = [slot for slot, _ in terms]
-    sources = [source for _, source in terms]
-    depth, width = sources[0].shape
+    groups = [group if isinstance(group, tuple) else (group,) for _, group in terms]
+    sources = [source for group in groups for source in group]
+    width = sources[0].shape[1]
+    depth = matrix.shape[3]
     rows = matrix.shape[2] // (1 if part is None else 2)
     extra = [] if base is None else [base]
     return call(
         name,
-        functools.partial(forward_kernel, slots, part, base is not None),
+        functools.partial(
+            forward_kernel, slots, [len(group) for group in groups], part, base is not None
+        ),
         who,
         [matrix, *sources, *extra],
         [((rows, width), F32)],
@@ -201,11 +208,12 @@
     g_here[...] = total
 
 
-def weight_kernel(scale, which, who, own, far, grad_here, grad_there, here, there):
+def weight_kernel(scale, which, who, own, far, grad_here, grad_there, out):
     mine = who[SIDE] == (who[CORE] ^ which)
     turned = split(jnp.where(mine, own[...], far[...]).T)
-    for grad, out in ((grad_here, here), (grad_there, there)):
-        out[...] = mm3(turned, split(grad[...])) * scale
+    hidden = grad_here.shape[1]
+    for k, grad in enumerate((grad_here, grad_there)):
+        out[:, k * hidden : (k + 1) * hidden] = mm3(turned, split(grad[...])) * scale
 
 
 def weight_term(name, who, scale, which, own, far, grad_here, grad_there):
@@ -216,9 +224,9 @@
         functools.partial(weight_kernel, scale, which),
         who,
         [own, far, grad_here, grad_there],
-        [((half, hidden), F32)] * 2,
+        [((half, 2 * hidden), F32)],
         flops=12 * rows * half * hidden,
-    )
+    )[0]
 
 
 def half_kernel(which, who, whole, out):
@@ -269,6 +277,17 @@
     rows, cols = parts[0].shape
     shape = ((rows // 2, cols), F32)
     return call(name, side_kernel, who, parts, [shape] * 2, [pltpu.VMEM((rows, cols), F32)])
+
+
+def core_kernel(who, one, other, here, there):
+    cols = here.shape[1]
+    here[...] = one[:, :cols] + other[:, :cols]
+    there[...] = one[:, cols:] + other[:, cols:]
+
+
+def core_sum(name, who, one, other):
+    rows, cols = one.shape
+    return call(name, core_kernel, who, [one, other], [((rows, cols // 2), F32)] * 2)
 
 
 def add_kernel(who, *refs):
@@ -326,12 +345,13 @@
     )
     total = forward("agg_own", who, a, [(OWN, features)])
     near = after(near, total, w_there, cot_there)
-    two = swapped(near, "dom")
+    two = tuple(swapped(near[k * rows // 2 : (k + 1) * rows // 2], "dom") for k in range(2))
     total = forward("agg_near", who, a, [(NEAR, near)], total)
-    far = after(far, total)
-    give = forward("agg_give", who, a, [(FAR, far), (TWO, two)], total, 1)
+    give = forward("agg_two", who, a, [(TWO, two)], total, 1)
+    far = after(far, give)
+    give = forward("agg_give", who, a, [(FAR, far)], give, 1)
     there = swapped(give, "feat")
-    keep = forward("agg_keep", who, a, [(FAR, far), (TWO, after(two, give))], total, 0)
+    keep = forward("agg_keep", who, a, [(FAR, far), (TWO, (after(two[0], give), two[1]))], total, 0)
 
     act_here, act_there, grad_here, grad_there, g_give = middle(
         who, keep, there, weight, w_there, cotangent, cot_there
@@ -340,13 +360,12 @@
     scale = 1.0 / math.sqrt(rows * parts)
     w_give = weight_term("weight_give", who, scale, 1, keep, there, grad_here, grad_there)
     w_keep = weight_term(
-        "weight_keep", who, scale, 0, after(keep, w_give[0]), there, grad_here, grad_there
+        "weight_keep", who, scale, 0, after(keep, w_give), there, grad_here, grad_there
     )
     quick = parts == 16
     steps = weight_sum(who, w_keep, w_give, quick)
 
     last = next(steps)(grad_here)
-    last = next(steps)(last)
     g_here = call(
         "keep",
         keep_kernel,
@@ -385,9 +404,9 @@
 
 def weight_sum(who, keep, give, quick):
     if not quick:
-        here, there = (join("core_join", who, CORE, pair) for pair in zip(keep, give))
+        here, there = jnp.split(join("core_join", who, CORE, (keep, give)), 2, axis=1)
         total = lax.psum(here + swapped(there, "feat"), "dom")
-        for _ in range(7):
+        for _ in range(6):
             yield lambda *last: last[0]
         yield lambda *last: total
         return
@@ -403,11 +422,9 @@
     def up(value):
         return chosen(value, "dom", lambda i: i + 2 if i % 4 < 2 else None)
 
-    gots = [swapped(value, "dom") for value in give]
-    yield step(lambda *last: add("core_there", who, after(keep[1], *last), gots[1]))
-    there = box[-1]
-    yield step(lambda *last: add("core_here", who, after(keep[0], *last), gots[0]))
-    here = box[-1]
+    got = swapped(give, "dom")
+    yield step(lambda *last: core_sum("core_sum", who, after(keep, *last), got)[::-1])
+    there, here = box[-1]
     got = up(there)
     yield step(lambda *last: add("chip_there", who, after(there, *last), got))
     got = swapped(box[-1], "feat")

time: 120 us -> 120 us (level)
  Pallas kernels: 44.1 us -> 46.3 us
  starting transfers between devices: 30.6 us -> 28.7 us
    ppermute x18, starting transfers between devices: 25.5 us -> 23.1 us  [chosen(): lax.ppermute(value, axis, [pair for pair in pairs if pair[1] is not None])]
    pallas_call x1, Pallas kernels: 7.18 us -> 8.84 us  [lay_out(): pl.pallas_call(lay_out_kernel, grid_spec=pltpu.PrefetchScalarGridSpec(num...]
    ppermute x18, waiting for transfers between devices: 38.3 us -> 36.7 us  [chosen(): lax.ppermute(value, axis, [pair for pair in pairs if pair[1] is not None])]
  transfers between devices with their start and end apart: 22 -> 22, of which waited for: 7 -> 9; matrix products, arithmetic and copies ran while one was open for 0% -> 0% of each run, Pallas kernels for 29% -> 32%
where the time goes in v3:
time: 120 us; the launch traced here: 119 us
  Pallas kernels  46.3 us (39%)
  waiting for transfers between devices  38.4 us (32%)
  starting transfers between devices  28.7 us (24%)
  local copies, waits for them, and re-layouts  4.63 us (4%)
    pallas_call x24, Pallas kernels, call(): pl.pallas_call(kernel, in_specs=[IN_SMEM] + [IN_VMEM] * len(operands), ou...  37.5 us
    ppermute x18, waiting for transfers between devices, chosen(): lax.ppermute(value, axis, [pair for pair in pairs if pair[1] is not None])  36.7 us
    ppermute x18, starting transfers between devices, chosen(): lax.ppermute(value, axis, [pair for pair in pairs if pair[1] is not None])  23.1 us
    pallas_call x1, Pallas kernels, lay_out(): pl.pallas_call(lay_out_kernel, grid_spec=pltpu.PrefetchScalarGridSpec(num...  8.84 us
    ppermute x4, starting transfers between devices, moved(): return lax.ppermute(value, axis, perm)  5.59 us
    unnamed x14, local copies, waits for them, and re-layouts  4.48 us
  transfers between devices with their start and end apart: 22, of which 9 were waited for; matrix products, arithmetic and copies ran while one was open for 0% of the time, Pallas kernels for 32%

profile of v3, /device:TPU:0, one launch (start us, length us, event | category | flops | bytes accessed | tf_op | source)
XLA Modules:
  0.0 119.0 jit_solution(9523902773062223780)
XLA Ops:
  0.6 2.4 %collective-permute-start.1 = (f32[1024,256]{1,0:T(8,128)}, f32[1024,256]{1,0:T(8,128)S(1)}, u32[]{:S(2)}, u32[]{:S(2)}) collective-permute-start(f32[1024,256]{1,0:T(8,128)} %refs_0_.1), channel_id=1, source_target_pairs={{0,6},{2,4},{4,10},{6,8},{8,14},{10,12},{12,18},{14,16},{16,22},{1... | collective-permute-start | bytes 3145736 | tf_op jit(solution)/shard_map/ppermute | solution.py:307
  3.1 0.1 stack.27.who
  3.1 1.2 %copy-done = f32[1024,256]{1,0:T(8,128)S(1)} copy-done((f32[1024,256]{1,0:T(8,128)S(1)}, f32[1024,256]{1,0:T(8,128)}, u32[]{:S(2)}) %copy-start) | copy-done | bytes 1048600
  4.4 0.6 cot_give.1
  5.0 1.6 %collective-permute-start.3 = (f32[512,256]{1,0:T(8,128)S(1)}, f32[512,256]{1,0:T(8,128)S(1)}, u32[]{:S(2)}, u32[]{:S(2)}) collective-permute-start(f32[512,256]{1,0:T(8,128)S(1)} %cot_give.1), channel_id=1, source_target_pairs={{0,1},{1,0},{2,3},{3,2},{4,5},{5,4},{6,7},{7,6},{8,9},{9,8},{10,11... | collective-permute-start | bytes 1572872 | tf_op jit(solution)/shard_map/ppermute | solution.py:313
  6.5 0.5 collective-permute-start.2
  7.1 0.1 collective-permute-start
  7.2 0.7 copy-done.4
  7.9 0.7 copy-done.5
  8.6 0.7 copy-done.6
  9.2 8.8 %lay_out.1 = (bf16[2,4,1024,1024]{3,2,1,0:T(8,128)(2,1)S(1)}, bf16[2,4,1024,1024]{3,2,1,0:T(8,128)(2,1)S(1)}) custom-call(s32[4,24]{1,0:T(4,128)S(1)} %bitcast.9, s32[4,24]{1,0:T(4,128)S(1)} %bitcast.10, s32[1,4]{1,0:T(1,128)S(1)} %copy-done.6, s32[8]{0:T(128)S(1)} %stack.27.who, f32[4,24,128,128]{3,2,1,0:T(8,128)} %bitcast.11), custom_call_target="tpu_custom_call" | custom-call | bytes 20000000 | tf_op jit(solution)/shard_map/lay_out/pallas_call | solution.py:75
  18.1 1.2 %copy-done.2 = f32[1024,256]{1,0:T(8,128)S(1)} copy-done((f32[1024,256]{1,0:T(8,128)S(1)}, f32[1024,256]{1,0:T(8,128)}, u32[]{:S(2)}) %copy-start.2) | copy-done | bytes 1048600
  19.3 3.0 %agg_own.1.refs_1_ = f32[1024,256]{1,0:T(8,128)S(1)} custom-call(s32[8]{0:T(128)S(1)} %stack.27.who, bf16[2,4,1024,1024]{3,2,1,0:T(8,128)(2,1)S(1)} %get-tuple-element.38.matrix, f32[1024,256]{1,0:T(8,128)S(1)} %copy-done.2), custom_call_target="tpu_custom_call" | custom-call | flops 1610612736 | bytes 17825792 | tf_op jit(solution)/shard_map/agg_own/pallas_call | solution.py:39
  22.3 8.4 %collective-permute-done.2.w_there = f32[512,256]{1,0:T(8,128)S(1)} collective-permute-done((f32[512,256]{1,0:T(8,128)}, f32[512,256]{1,0:T(8,128)S(1)}, u32[]{:S(2)}, u32[]{:S(2)}) %collective-permute-start.2) | collective-permute-done | bytes 524320 | tf_op jit(solution)/shard_map/ppermute | solution.py:313
  30.8 0.1 fusion
  30.8 0.1 collective-permute-start.5
  30.9 0.5 collective-permute-start.4
  31.4 3.0 %agg_near.1.refs_2_.refs_3_ = f32[1024,256]{1,0:T(8,128)S(1)} custom-call(s32[8]{0:T(128)S(1)} %stack.27.who, bf16[2,4,1024,1024]{3,2,1,0:T(8,128)(2,1)S(1)} %get-tuple-element.38.matrix, f32[1024,256]{1,0:T(8,128)S(1)} %collective-permute-done.1.refs_0_, f32[1024,256]{1,0:T(8,128)S(1)} %agg_own.1.refs_1_), custom_call_target="tpu_custom_call" | custom-call | flops 1610612736 | bytes 18874368 | tf_op jit(solution)/shard_map/agg_near/pallas_call | solution.py:39
  34.5 1.9 %agg_two.1.refs_1_ = f32[512,256]{1,0:T(8,128)S(1)} custom-call(s32[8]{0:T(128)S(1)} %stack.27.who, bf16[2,4,1024,1024]{3,2,1,0:T(8,128)(2,1)S(1)} %get-tuple-element.38.matrix, f32[512,256]{1,0:T(8,128)S(1)} %collective-permute-done.4.refs_0_.refs_1_, f32[512,256]{1,0:T(8,128)S(1)} %collective-permute-done.5.refs_1_.refs_2_, ...), custom_call_target="tpu_custom_call" | custom-call | flops 805306368 | bytes 18874368 | tf_op jit(solution)/shard_map/agg_two/pallas_call | solution.py:39
  36.4 0.0 copy-start.3
  36.4 1.9 %agg_give.1 = f32[512,256]{1,0:T(8,128)S(1)} custom-call(s32[8]{0:T(128)S(1)} %stack.27.who, bf16[2,4,1024,1024]{3,2,1,0:T(8,128)(2,1)S(1)} %get-tuple-element.38.matrix, f32[1024,256]{1,0:T(8,128)S(1)} %collective-permute-done.refs_0_, f32[512,256]{1,0:T(8,128)S(1)} %agg_two.1.refs_1_), custom_call_target="tpu_custom_call" | custom-call | flops 805306368 | bytes 18350080 | tf_op jit(solution)/shard_map/agg_give/pallas_call | solution.py:39
  38.3 1.6 %collective-permute-start.6 = (f32[512,256]{1,0:T(8,128)S(1)}, f32[512,256]{1,0:T(8,128)S(1)}, u32[]{:S(2)}, u32[]{:S(2)}) collective-permute-start(f32[512,256]{1,0:T(8,128)S(1)} %agg_give.1), channel_id=1, source_target_pairs={{0,1},{1,0},{2,3},{3,2},{4,5},{5,4},{6,7},{7,6},{8,9},{9,8},{10,11... | collective-permute-start | bytes 1572872 | tf_op jit(solution)/shard_map/ppermute | solution.py:313
  39.9 2.9 %agg_keep.1.own = f32[512,256]{1,0:T(8,128)S(1)} custom-call(s32[8]{0:T(128)S(1)} %stack.27.who, bf16[2,4,1024,1024]{3,2,1,0:T(8,128)(2,1)S(1)} %get-tuple-element.38.matrix, f32[1024,256]{1,0:T(8,128)S(1)} %collective-permute-done.refs_0_, f32[512,256]{1,0:T(8,128)S(1)} %collective-permute-done.4.refs_0_.refs_1_, ...), custom_call_target="tpu_custom_call" | custom-call | flops 1610612736 | bytes 19922944 | tf_op jit(solution)/shard_map/agg_keep/pallas_call | solution.py:39
  42.8 9.5 %collective-permute-done.6.far = f32[512,256]{1,0:T(8,128)S(1)} collective-permute-done((f32[512,256]{1,0:T(8,128)S(1)}, f32[512,256]{1,0:T(8,128)S(1)}, u32[]{:S(2)}, u32[]{:S(2)}) %collective-permute-start.6) | collective-permute-done | bytes 524320 | tf_op jit(solution)/shard_map/ppermute | solution.py:313
  52.3 2.3 %middle.1 = (f32[512,256]{1,0:T(8,128)S(1)}, f32[512,256]{1,0:T(8,128)S(1)}, f32[512,256]{1,0:T(8,128)S(1)}, f32[512,256]{1,0:T(8,128)S(1)}, f32[512,256]{1,0:T(8,128)S(1)}) custom-call(s32[8]{0:T(128)S(1)} %stack.27.who, f32[512,256]{1,0:T(8,128)S(1)} %agg_keep.1.own, f32[512,256]{1,0:T(8,128)S(1)} %collective-permute-done.6.far, f32[512,256]{1,0:T(8,128)S(1)} %copy-done.3, ...), custom_call_target="tpu_custom_call" | custom-call | flops 1207959552 | bytes 3670016 | tf_op jit(solution)/shard_map/middle/pallas_call | solution.py:39
  54.6 1.2 %weight_give.1 = f32[256,512]{1,0:T(8,128)S(1)} custom-call(s32[8]{0:T(128)S(1)} %stack.27.who, f32[512,256]{1,0:T(8,128)S(1)} %agg_keep.1.own, f32[512,256]{1,0:T(8,128)S(1)} %collective-permute-done.6.far, f32[512,256]{1,0:T(8,128)S(1)} %get-tuple-element.51.grad_here, f32[512,256]{1,0:T(8,128)S(1)} %get-tuple-element.44.grad_there), custom_call_target="tpu_custom_call" | custom-call | flops 402653184 | bytes 2097152 | tf_op jit(solution)/shard_map/weight_give/pallas_call | solution.py:39
  55.8 0.1 collective-permute-start.7
  55.9 1.6 %collective-permute-start.8 = (f32[512,256]{1,0:T(8,128)S(1)}, f32[512,256]{1,0:T(8,128)S(1)}, u32[]{:S(2)}, u32[]{:S(2)}) collective-permute-start(f32[512,256]{1,0:T(8,128)S(1)} %get-tuple-element.49), channel_id=1, source_target_pairs={{0,1},{1,0},{2,3},{3,2},{4,5},{5,4},{6,7},{7,6},{8,9},{9,8},{10,11... | collective-permute-start | bytes 1572872 | tf_op jit(solution)/shard_map/ppermute | solution.py:313
  57.5 1.2 %weight_keep.1.one = f32[256,512]{1,0:T(8,128)S(1)} custom-call(s32[8]{0:T(128)S(1)} %stack.27.who, f32[512,256]{1,0:T(8,128)S(1)} %agg_keep.1.own, f32[512,256]{1,0:T(8,128)S(1)} %collective-permute-done.6.far, f32[512,256]{1,0:T(8,128)S(1)} %get-tuple-element.51.grad_here, f32[512,256]{1,0:T(8,128)S(1)} %get-tuple-element.44.grad_there), custom_call_target="tpu_custom_call" | custom-call | flops 402653184 | bytes 2097152 | tf_op jit(solution)/shard_map/weight_keep/pallas_call | solution.py:39
  58.8 0.6 core_sum.1
  59.4 5.4 %collective-permute-start.9 = (f32[256,256]{1,0:T(8,128)S(1)}, f32[256,256]{1,0:T(8,128)S(1)}, u32[]{:S(2)}, u32[]{:S(2)}) collective-permute-start(f32[256,256]{1,0:T(8,128)S(1)} %get-tuple-element.54.refs_0_), channel_id=1, source_target_pairs={{0,4},{2,6},{8,12},{10,14},{16,20},{18,22},{24,28},{26,30},{1,5},{... | collective-permute-start | bytes 786440 | tf_op jit(solution)/shard_map/ppermute | solution.py:313
  64.8 1.2 %keep.1.source = f32[512,256]{1,0:T(8,128)S(1)} custom-call(s32[8]{0:T(128)S(1)} %stack.27.who, f32[512,256]{1,0:T(8,128)S(1)} %copy-done.3, f32[512,256]{1,0:T(8,128)S(1)} %collective-permute-done.2.w_there, f32[512,256]{1,0:T(8,128)S(1)} %get-tuple-element.51.grad_here, f32[512,256]{1,0:T(8,128)S(1)} %get-tuple-element.44.grad_there), custom_call_target="tpu_custom_call" | custom-call | flops 402653184 | bytes 2097152 | tf_op jit(solution)/shard_map/keep/pallas_call | solution.py:39
  66.0 3.9 %back_here.1 = (f32[1024,256]{1,0:T(8,128)S(1)}, f32[1024,256]{1,0:T(8,128)S(1)}, f32[1024,256]{1,0:T(8,128)S(1)}, f32[1024,256]{1,0:T(8,128)S(1)}) custom-call(s32[8]{0:T(128)S(1)} %stack.27.who, bf16[2,4,1024,1024]{3,2,1,0:T(8,128)(2,1)S(1)} %get-tuple-element.48.matrix, f32[512,256]{1,0:T(8,128)S(1)} %keep.1.source), custom_call_target="tpu_custom_call" | custom-call | flops 3221225472 | bytes 17301504 | tf_op jit(solution)/shard_map/back_here/pallas_call | solution.py:39
  69.9 0.5 collective-permute-done.9.refs_1_
  70.5 0.6 chip_there.1
  71.0 1.5 %back_two.1 = f32[1024,256]{1,0:T(8,128)S(1)} custom-call(s32[8]{0:T(128)S(1)} %stack.27.who, bf16[2,4,1024,1024]{3,2,1,0:T(8,128)(2,1)S(1)} %get-tuple-element.48.matrix, f32[512,256]{1,0:T(8,128)S(1)} %collective-permute-done.8.source, f32[1024,256]{1,0:T(8,128)S(1)} %get-tuple-element.53.refs_0_), custom_call_target="tpu_custom_call" | custom-call | flops 805306368 | bytes 18350080 | tf_op jit(solution)/shard_map/back_two/pallas_call | solution.py:39
  72.6 0.1 collective-permute-start.10
  72.7 1.5 %back_far.1 = f32[1024,256]{1,0:T(8,128)S(1)} custom-call(s32[8]{0:T(128)S(1)} %stack.27.who, bf16[2,4,1024,1024]{3,2,1,0:T(8,128)(2,1)S(1)} %get-tuple-element.48.matrix, f32[512,256]{1,0:T(8,128)S(1)} %collective-permute-done.8.source, f32[1024,256]{1,0:T(8,128)S(1)} %get-tuple-element.57.refs_0_), custom_call_target="tpu_custom_call" | custom-call | flops 805306368 | bytes 18350080 | tf_op jit(solution)/shard_map/back_far/pallas_call | solution.py:39
  74.2 3.0 %collective-permute-start.13 = (f32[1024,256]{1,0:T(8,128)S(1)}, f32[1024,256]{1,0:T(8,128)S(1)}, u32[]{:S(2)}, u32[]{:S(2)}) collective-permute-start(f32[1024,256]{1,0:T(8,128)S(1)} %back_far.1), channel_id=1, source_target_pairs={{0,26},{2,0},{4,30},{6,4},{8,2},{10,8},{12,6},{14,12},{16,10},{18,... | collective-permute-start | bytes 3145736 | tf_op jit(solution)/shard_map/ppermute | solution.py:307
  77.2 3.8 %collective-permute-start.11 = (f32[256,256]{1,0:T(8,128)S(1)}, f32[256,256]{1,0:T(8,128)S(1)}, u32[]{:S(2)}, u32[]{:S(2)}) collective-permute-start(f32[256,256]{1,0:T(8,128)S(1)} %get-tuple-element.60.one), channel_id=1, source_target_pairs={{0,4},{2,6},{8,12},{10,14},{16,20},{18,22},{24,28},{26,30},{1,5},{... | collective-permute-start | bytes 786440 | tf_op jit(solution)/shard_map/ppermute | solution.py:313
  81.0 1.6 %collective-permute-start.12 = (f32[256,256]{1,0:T(8,128)S(1)}, f32[256,256]{1,0:T(8,128)S(1)}, u32[]{:S(2)}, u32[]{:S(2)}) collective-permute-start(f32[256,256]{1,0:T(8,128)S(1)} %chip_there.1), channel_id=1, source_target_pairs={{0,1},{1,0},{2,3},{3,2},{4,5},{5,4},{6,7},{7,6},{8,9},{9,8},{10,11... | collective-permute-start | bytes 786440 | tf_op jit(solution)/shard_map/ppermute | solution.py:313
  82.6 1.5 %back_near.1 = f32[1024,256]{1,0:T(8,128)S(1)} custom-call(s32[8]{0:T(128)S(1)} %stack.27.who, bf16[2,4,1024,1024]{3,2,1,0:T(8,128)(2,1)S(1)} %get-tuple-element.48.matrix, f32[512,256]{1,0:T(8,128)S(1)} %collective-permute-done.8.source, f32[1024,256]{1,0:T(8,128)S(1)} %get-tuple-element.59.refs_0_, f32[1024,256]{1,0:T(8,128)S(1)} %collective-permute-done.10.refs_1_), custom_call_target="tpu_custom_call" | custom-call | flops 805306368 | bytes 19398656 | tf_op jit(solution)/shard_map/back_near/pallas_call | solution.py:39
  84.2 0.1 collective-permute-start.20
  84.2 0.7 collective-permute-done.11.two
  84.9 2.5 %collective-permute-done.12.three = f32[256,256]{1,0:T(8,128)S(1)} collective-permute-done((f32[256,256]{1,0:T(8,128)S(1)}, f32[256,256]{1,0:T(8,128)S(1)}, u32[]{:S(2)}, u32[]{:S(2)}) %collective-permute-start.12) | collective-permute-done | bytes 262176 | tf_op jit(solution)/shard_map/ppermute | solution.py:313
  87.5 0.6 side_sum.1
  88.1 1.6 %collective-permute-start.16 = (f32[512,256]{1,0:T(8,128)S(1)}, f32[512,256]{1,0:T(8,128)S(1)}, u32[]{:S(2)}, u32[]{:S(2)}) collective-permute-start(f32[512,256]{1,0:T(8,128)S(1)} %get-tuple-element.69), channel_id=1, source_target_pairs={{0,1},{1,0},{2,3},{3,2},{4,5},{5,4},{6,7},{7,6},{8,9},{9,8},{10,11... | collective-permute-start | bytes 1572872 | tf_op jit(solution)/shard_map/ppermute | solution.py:313
  89.7 0.7 collective-permute-start.14
  90.3 1.5 %back_own.1.refs_0_ = f32[1024,256]{1,0:T(8,128)S(1)} custom-call(s32[8]{0:T(128)S(1)} %stack.27.who, bf16[2,4,1024,1024]{3,2,1,0:T(8,128)(2,1)S(1)} %get-tuple-element.48.matrix, f32[512,256]{1,0:T(8,128)S(1)} %collective-permute-done.8.source, f32[1024,256]{1,0:T(8,128)S(1)} %get-tuple-element.64.refs_0_), custom_call_target="tpu_custom_call" | custom-call | flops 805306368 | bytes 18350080 | tf_op jit(solution)/shard_map/back_own/pallas_call | solution.py:39
  91.9 1.7 %collective-permute-done.13.refs_1_ = f32[1024,256]{1,0:T(8,128)S(1)} collective-permute-done((f32[1024,256]{1,0:T(8,128)S(1)}, f32[1024,256]{1,0:T(8,128)S(1)}, u32[]{:S(2)}, u32[]{:S(2)}) %collective-permute-start.13) | collective-permute-done | bytes 1048608 | tf_op jit(solution)/shard_map/ppermute | solution.py:307
  93.6 0.6 layer_sum.1.refs_0_
  94.1 0.7 collective-permute-start.15
  94.8 0.6 pair_sum.1.ready
  95.4 1.3 %collective-permute-start.19 = (f32[128,256]{1,0:T(8,128)S(1)}, f32[128,256]{1,0:T(8,128)S(1)}, u32[]{:S(2)}, u32[]{:S(2)}) collective-permute-start(f32[128,256]{1,0:T(8,128)S(1)} %pair_sum.1.ready), channel_id=1, source_target_pairs={{4,8},{6,10},{12,0},{14,2},{20,24},{22,26},{28,16},{30,18},{5,9},{... | collective-permute-start | bytes 393224 | tf_op jit(solution)/shard_map/ppermute | solution.py:313
  96.7 1.3 %collective-permute-start.18 = (f32[128,256]{1,0:T(8,128)S(1)}, f32[128,256]{1,0:T(8,128)S(1)}, u32[]{:S(2)}, u32[]{:S(2)}) collective-permute-start(f32[128,256]{1,0:T(8,128)S(1)} %pair_sum.1.ready), channel_id=1, source_target_pairs={{4,0},{6,2},{12,8},{14,10},{20,16},{22,18},{28,24},{30,26},{5,1},{... | collective-permute-start | bytes 393224 | tf_op jit(solution)/shard_map/ppermute | solution.py:313
  98.0 0.7 collective-permute-start.17
  98.7 0.8 collective-permute-done.16.refs_1_
  99.5 1.6 %activated.1 = f32[1024,256]{1,0:T(8,128)} custom-call(s32[8]{0:T(128)S(1)} %stack.27.who, f32[512,256]{1,0:T(8,128)S(1)} %get-tuple-element.67.refs_0_, f32[512,256]{1,0:T(8,128)S(1)} %collective-permute-done.16.refs_1_), custom_call_target="tpu_custom_call" | custom-call | bytes 1048576 | tf_op jit(solution)/shard_map/activated/pallas_call | solution.py:39
  101.1 13.5 %collective-permute-done.19.later_sent = f32[128,256]{1,0:T(8,128)S(1)} collective-permute-done((f32[128,256]{1,0:T(8,128)S(1)}, f32[128,256]{1,0:T(8,128)S(1)}, u32[]{:S(2)}, u32[]{:S(2)}) %collective-permute-start.19) | collective-permute-done | bytes 131104 | tf_op jit(solution)/shard_map/ppermute | solution.py:313
  114.5 0.7 collective-permute-done.18.ready_sent
  115.2 0.6 chip_pick.1.refs_0_
  115.8 0.1 collective-permute-start.21
  115.9 1.7 %feature_grad.1 = f32[1024,256]{1,0:T(8,128)} custom-call(s32[8]{0:T(128)S(1)} %stack.27.who, f32[1024,256]{1,0:T(8,128)S(1)} %back_own.1.refs_0_, f32[1024,256]{1,0:T(8,128)S(1)} %collective-permute-done.13.refs_1_, f32[1024,256]{1,0:T(8,128)S(1)} %collective-permute-done.20.refs_2_), custom_call_target="tpu_custom_call" | custom-call | bytes 3145728 | tf_op jit(solution)/shard_map/feature_grad/pallas_call | solution.py:39
  117.6 1.4 %weight_grad.1 = f32[512,256]{1,0:T(8,128)} custom-call(s32[8]{0:T(128)S(1)} %stack.27.who, f32[256,256]{1,0:T(8,128)S(1)} %chip_pick.1.refs_0_, f32[256,256]{1,0:T(8,128)S(1)} %collective-permute-done.21.refs_1_), custom_call_target="tpu_custom_call" | custom-call | bytes 524288 | tf_op jit(solution)/shard_map/weight_grad/pallas_call | solution.py:39
  (21 shorter events, 0.1 us)
Async XLA Ops:
  0.6 30.1 %collective-permute-start.1 = (f32[1024,256]{1,0:T(8,128)}, f32[1024,256]{1,0:T(8,128)S(1)}, u32[]{:S(2)}, u32[]{:S(2)}) collective-permute-start(f32[1024,256]{1,0:T(8,128)} %refs_0_.1), channel_id=1, source_target_pairs={{0,6},{2,4},{4,10},{6,8},{8,14},{10,12},{12,18},{14,16},{16,22},{1... | collective-permute-start | bytes 3145736 | tf_op jit(solution)/shard_map/ppermute | solution.py:307
  3.1 1.2 %copy-start = (f32[1024,256]{1,0:T(8,128)S(1)}, f32[1024,256]{1,0:T(8,128)}, u32[]{:S(2)}) copy-start(f32[1024,256]{1,0:T(8,128)} %cot.1) | copy-start | bytes 3145732
  5.0 17.4 %collective-permute-start.3 = (f32[512,256]{1,0:T(8,128)S(1)}, f32[512,256]{1,0:T(8,128)S(1)}, u32[]{:S(2)}, u32[]{:S(2)}) collective-permute-start(f32[512,256]{1,0:T(8,128)S(1)} %cot_give.1), channel_id=1, source_target_pairs={{0,1},{1,0},{2,3},{3,2},{4,5},{5,4},{6,7},{7,6},{8,9},{9,8},{10,11... | collective-permute-start | bytes 1572872 | tf_op jit(solution)/shard_map/ppermute | solution.py:313
  6.5 24.2 %collective-permute-start.2 = (f32[512,256]{1,0:T(8,128)}, f32[512,256]{1,0:T(8,128)S(1)}, u32[]{:S(2)}, u32[]{:S(2)}) collective-permute-start(f32[512,256]{1,0:T(8,128)} %w_here.3), channel_id=1, source_target_pairs={{0,1},{1,0},{2,3},{3,2},{4,5},{5,4},{6,7},{7,6},{8,9},{9,8},{10,11... | collective-permute-start | bytes 1572872 | tf_op jit(solution)/shard_map/ppermute | solution.py:313
  7.1 29.4 %collective-permute-start = (f32[1024,256]{1,0:T(8,128)}, f32[1024,256]{1,0:T(8,128)S(1)}, u32[]{:S(2)}, u32[]{:S(2)}) collective-permute-start(f32[1024,256]{1,0:T(8,128)} %refs_0_.1), channel_id=1, source_target_pairs={{0,2},{2,8},{4,6},{6,12},{8,10},{10,16},{12,14},{14,20},{16,18},{1... | collective-permute-start | bytes 3145736 | tf_op jit(solution)/shard_map/ppermute | solution.py:307
  7.2 0.7 copy-start.4
  7.9 0.7 copy-start.5
  8.6 0.7 copy-start.6
  18.1 1.2 %copy-start.2 = (f32[1024,256]{1,0:T(8,128)S(1)}, f32[1024,256]{1,0:T(8,128)}, u32[]{:S(2)}) copy-start(f32[1024,256]{1,0:T(8,128)} %refs_0_.1) | copy-start | bytes 3145732
  30.8 3.6 %collective-permute-start.5 = (f32[512,256]{1,0:T(8,128)S(1)}, f32[512,256]{1,0:T(8,128)S(1)}, u32[]{:S(2)}, u32[]{:S(2)}) collective-permute-start(f32[512,256]{1,0:T(8,128)S(1)} %get-tuple-element.73), channel_id=1, source_target_pairs={{0,2},{2,0},{4,6},{6,4},{8,10},{10,8},{12,14},{14,12},{16,18},{18,... | collective-permute-start | bytes 1572872 | tf_op jit(solution)/shard_map/ppermute | solution.py:313
  30.9 3.5 %collective-permute-start.4 = (f32[512,256]{1,0:T(8,128)S(1)}, f32[512,256]{1,0:T(8,128)S(1)}, u32[]{:S(2)}, u32[]{:S(2)}) collective-permute-start(f32[512,256]{1,0:T(8,128)S(1)} %get-tuple-element.74), channel_id=1, source_target_pairs={{0,2},{2,0},{4,6},{6,4},{8,10},{10,8},{12,14},{14,12},{16,18},{18,... | collective-permute-start | bytes 1572872 | tf_op jit(solution)/shard_map/ppermute | solution.py:313
  36.4 15.9 %copy-start.1 = (f32[1024,256]{1,0:T(8,128)S(1)}, f32[1024,256]{1,0:T(8,128)}, u32[]{:S(2)}) copy-start(f32[1024,256]{1,0:T(8,128)} %cot.1) | copy-start | bytes 3145732
  36.4 15.9 %copy-start.3 = (f32[512,256]{1,0:T(8,128)S(1)}, f32[512,256]{1,0:T(8,128)}, u32[]{:S(2)}) copy-start(f32[512,256]{1,0:T(8,128)} %w_here.3) | copy-start | bytes 1572868
  38.3 14.0 %collective-permute-start.6 = (f32[512,256]{1,0:T(8,128)S(1)}, f32[512,256]{1,0:T(8,128)S(1)}, u32[]{:S(2)}, u32[]{:S(2)}) collective-permute-start(f32[512,256]{1,0:T(8,128)S(1)} %agg_give.1), channel_id=1, source_target_pairs={{0,1},{1,0},{2,3},{3,2},{4,5},{5,4},{6,7},{7,6},{8,9},{9,8},{10,11... | collective-permute-start | bytes 1572872 | tf_op jit(solution)/shard_map/ppermute | solution.py:313
  55.8 2.9 %collective-permute-start.7 = (f32[256,512]{1,0:T(8,128)S(1)}, f32[256,512]{1,0:T(8,128)S(1)}, u32[]{:S(2)}, u32[]{:S(2)}) collective-permute-start(f32[256,512]{1,0:T(8,128)S(1)} %weight_give.1), channel_id=1, source_target_pairs={{0,2},{2,0},{4,6},{6,4},{8,10},{10,8},{12,14},{14,12},{16,18},{18,... | collective-permute-start | bytes 1572872 | tf_op jit(solution)/shard_map/ppermute | solution.py:313
  55.9 15.1 %collective-permute-start.8 = (f32[512,256]{1,0:T(8,128)S(1)}, f32[512,256]{1,0:T(8,128)S(1)}, u32[]{:S(2)}, u32[]{:S(2)}) collective-permute-start(f32[512,256]{1,0:T(8,128)S(1)} %get-tuple-element.49), channel_id=1, source_target_pairs={{0,1},{1,0},{2,3},{3,2},{4,5},{5,4},{6,7},{7,6},{8,9},{9,8},{10,11... | collective-permute-start | bytes 1572872 | tf_op jit(solution)/shard_map/ppermute | solution.py:313
  59.4 11.1 %collective-permute-start.9 = (f32[256,256]{1,0:T(8,128)S(1)}, f32[256,256]{1,0:T(8,128)S(1)}, u32[]{:S(2)}, u32[]{:S(2)}) collective-permute-start(f32[256,256]{1,0:T(8,128)S(1)} %get-tuple-element.54.refs_0_), channel_id=1, source_target_pairs={{0,4},{2,6},{8,12},{10,14},{16,20},{18,22},{24,28},{26,30},{1,5},{... | collective-permute-start | bytes 786440 | tf_op jit(solution)/shard_map/ppermute | solution.py:313
  72.6 10.0 %collective-permute-start.10 = (f32[1024,256]{1,0:T(8,128)S(1)}, f32[1024,256]{1,0:T(8,128)S(1)}, u32[]{:S(2)}, u32[]{:S(2)}) collective-permute-start(f32[1024,256]{1,0:T(8,128)S(1)} %back_two.1), channel_id=1, source_target_pairs={{0,2},{2,0},{4,6},{6,4},{8,10},{10,8},{12,14},{14,12},{16,18},{18,... | collective-permute-start | bytes 3145736 | tf_op jit(solution)/shard_map/ppermute | solution.py:313
  74.2 19.3 %collective-permute-start.13 = (f32[1024,256]{1,0:T(8,128)S(1)}, f32[1024,256]{1,0:T(8,128)S(1)}, u32[]{:S(2)}, u32[]{:S(2)}) collective-permute-start(f32[1024,256]{1,0:T(8,128)S(1)} %back_far.1), channel_id=1, source_target_pairs={{0,26},{2,0},{4,30},{6,4},{8,2},{10,8},{12,6},{14,12},{16,10},{18,... | collective-permute-start | bytes 3145736 | tf_op jit(solution)/shard_map/ppermute | solution.py:307
  77.2 7.7 %collective-permute-start.11 = (f32[256,256]{1,0:T(8,128)S(1)}, f32[256,256]{1,0:T(8,128)S(1)}, u32[]{:S(2)}, u32[]{:S(2)}) collective-permute-start(f32[256,256]{1,0:T(8,128)S(1)} %get-tuple-element.60.one), channel_id=1, source_target_pairs={{0,4},{2,6},{8,12},{10,14},{16,20},{18,22},{24,28},{26,30},{1,5},{... | collective-permute-start | bytes 786440 | tf_op jit(solution)/shard_map/ppermute | solution.py:313
  81.0 6.4 %collective-permute-start.12 = (f32[256,256]{1,0:T(8,128)S(1)}, f32[256,256]{1,0:T(8,128)S(1)}, u32[]{:S(2)}, u32[]{:S(2)}) collective-permute-start(f32[256,256]{1,0:T(8,128)S(1)} %chip_there.1), channel_id=1, source_target_pairs={{0,1},{1,0},{2,3},{3,2},{4,5},{5,4},{6,7},{7,6},{8,9},{9,8},{10,11... | collective-permute-start | bytes 786440 | tf_op jit(solution)/shard_map/ppermute | solution.py:313
  84.2 31.7 %collective-permute-start.20 = (f32[1024,256]{1,0:T(8,128)S(1)}, f32[1024,256]{1,0:T(8,128)S(1)}, u32[]{:S(2)}, u32[]{:S(2)}) collective-permute-start(f32[1024,256]{1,0:T(8,128)S(1)} %back_near.1), channel_id=1, source_target_pairs={{0,30},{2,28},{4,2},{6,0},{8,6},{10,4},{12,10},{14,8},{16,14},{18,... | collective-permute-start | bytes 3145736 | tf_op jit(solution)/shard_map/ppermute | solution.py:307
  88.1 11.4 %collective-permute-start.16 = (f32[512,256]{1,0:T(8,128)S(1)}, f32[512,256]{1,0:T(8,128)S(1)}, u32[]{:S(2)}, u32[]{:S(2)}) collective-permute-start(f32[512,256]{1,0:T(8,128)S(1)} %get-tuple-element.69), channel_id=1, source_target_pairs={{0,1},{1,0},{2,3},{3,2},{4,5},{5,4},{6,7},{7,6},{8,9},{9,8},{10,11... | collective-permute-start | bytes 1572872 | tf_op jit(solution)/shard_map/ppermute | solution.py:313
  89.7 3.9 %collective-permute-start.14 = (f32[128,256]{1,0:T(8,128)S(1)}, f32[128,256]{1,0:T(8,128)S(1)}, u32[]{:S(2)}, u32[]{:S(2)}) collective-permute-start(f32[128,256]{1,0:T(8,128)S(1)} %get-tuple-element.62), channel_id=1, source_target_pairs={{4,12},{6,14},{12,4},{14,6},{20,28},{22,30},{28,20},{30,22},{5,13}... | collective-permute-start | bytes 393224 | tf_op jit(solution)/shard_map/ppermute | solution.py:313
  94.1 0.7 collective-permute-start.15
  95.4 19.1 %collective-permute-start.19 = (f32[128,256]{1,0:T(8,128)S(1)}, f32[128,256]{1,0:T(8,128)S(1)}, u32[]{:S(2)}, u32[]{:S(2)}) collective-permute-start(f32[128,256]{1,0:T(8,128)S(1)} %pair_sum.1.ready), channel_id=1, source_target_pairs={{4,8},{6,10},{12,0},{14,2},{20,24},{22,26},{28,16},{30,18},{5,9},{... | collective-permute-start | bytes 393224 | tf_op jit(solution)/shard_map/ppermute | solution.py:313
  96.7 18.6 %collective-permute-start.18 = (f32[128,256]{1,0:T(8,128)S(1)}, f32[128,256]{1,0:T(8,128)S(1)}, u32[]{:S(2)}, u32[]{:S(2)}) collective-permute-start(f32[128,256]{1,0:T(8,128)S(1)} %pair_sum.1.ready), channel_id=1, source_target_pairs={{4,0},{6,2},{12,8},{14,10},{20,16},{22,18},{28,24},{30,26},{5,1},{... | collective-permute-start | bytes 393224 | tf_op jit(solution)/shard_map/ppermute | solution.py:313
  98.0 17.3 %collective-permute-start.17 = (f32[128,256]{1,0:T(8,128)S(1)}, f32[128,256]{1,0:T(8,128)S(1)}, u32[]{:S(2)}, u32[]{:S(2)}) collective-permute-start(f32[128,256]{1,0:T(8,128)S(1)} %pair_sum.1.ready), channel_id=1, source_target_pairs={{4,12},{6,14},{12,4},{14,6},{20,28},{22,30},{28,20},{30,22},{5,13}... | collective-permute-start | bytes 393224 | tf_op jit(solution)/shard_map/ppermute | solution.py:313
  115.8 1.8 %collective-permute-start.21 = (f32[256,256]{1,0:T(8,128)S(1)}, f32[256,256]{1,0:T(8,128)S(1)}, u32[]{:S(2)}, u32[]{:S(2)}) collective-permute-start(f32[256,256]{1,0:T(8,128)S(1)} %chip_pick.1.refs_0_), channel_id=1, source_target_pairs={{0,2},{2,0},{4,6},{6,4},{8,10},{10,8},{12,14},{14,12},{16,18},{18,... | collective-permute-start | bytes 786440 | tf_op jit(solution)/shard_map/ppermute | solution.py:313

commit v4 on v3

--- a/solution.py
+++ b/solution.py
@@ -375,10 +375,11 @@
         flops=12 * rows // 2 * width * hidden,
     )[0]
     firsts = backward("back_here", who, t, [TWO, FAR, NEAR, OWN], after(g_here, last), [], 0)
-    last = next(steps)(firsts[0])
-    g_there = after(g_there, last)
+    g_there = after(g_there, firsts[0])
     last = backward("back_two", who, t, [TWO], g_there, [firsts[0]], 1)[0]
-    two = swapped(last, "dom")
+    two_out = last
+    last = next(steps)(last)
+    two = swapped(after(two_out, last), "dom")
     last = backward("back_far", who, t, [FAR], after(g_there, last), [firsts[1]], 1)[0]
     far = moved(last, "dom", -3, -1)
     last = backward("back_near", who, t, [NEAR], after(g_there, last), [firsts[2], two], 1)[0]

time: 120 us -> 121 us (level)
  waiting for transfers between devices: 38.4 us -> 32 us
  Pallas kernels: 46.3 us -> 52.3 us
    ppermute x18, waiting for transfers between devices: 36.7 us -> 30.3 us  [chosen(): lax.ppermute(value, axis, [pair for pair in pairs if pair[1] is not None])]
    pallas_call x1, Pallas kernels: 8.84 us -> 14.8 us  [lay_out(): pl.pallas_call(lay_out_kernel, grid_spec=pltpu.PrefetchScalarGridSpec(num...]
  transfers between devices with their start and end apart: 22 -> 22, of which waited for: 9 -> 9; matrix products, arithmetic and copies ran while one was open for 0% -> 0% of each run, Pallas kernels for 32% -> 38%
where the time goes in v4:
time: 121 us; the launch traced here: 120 us
  Pallas kernels  52.3 us (43%)
  waiting for transfers between devices  32 us (26%)
  starting transfers between devices  29.6 us (24%)
  local copies, waits for them, and re-layouts  4.63 us (4%)
    pallas_call x24, Pallas kernels, call(): pl.pallas_call(kernel, in_specs=[IN_SMEM] + [IN_VMEM] * len(operands), ou...  37.5 us
    ppermute x18, waiting for transfers between devices, chosen(): lax.ppermute(value, axis, [pair for pair in pairs if pair[1] is not None])  30.3 us
    ppermute x18, starting transfers between devices, chosen(): lax.ppermute(value, axis, [pair for pair in pairs if pair[1] is not None])  23.3 us
    pallas_call x1, Pallas kernels, lay_out(): pl.pallas_call(lay_out_kernel, grid_spec=pltpu.PrefetchScalarGridSpec(num...  14.8 us
    ppermute x4, starting transfers between devices, moved(): return lax.ppermute(value, axis, perm)  6.39 us
    unnamed x14, local copies, waits for them, and re-layouts  4.48 us
  transfers between devices with their start and end apart: 22, of which 9 were waited for; matrix products, arithmetic and copies ran while one was open for 0% of the time, Pallas kernels for 38%

profile of v4, /device:TPU:0, one launch (start us, length us, event | category | flops | bytes accessed | tf_op | source)
XLA Modules:
  0.0 119.6 jit_solution(5930932128713743814)
XLA Ops:
  0.6 2.4 %collective-permute-start.1 = (f32[1024,256]{1,0:T(8,128)}, f32[1024,256]{1,0:T(8,128)S(1)}, u32[]{:S(2)}, u32[]{:S(2)}) collective-permute-start(f32[1024,256]{1,0:T(8,128)} %refs_0_.1), channel_id=1, source_target_pairs={{0,6},{2,4},{4,10},{6,8},{8,14},{10,12},{12,18},{14,16},{16,22},{1... | collective-permute-start | bytes 3145736 | tf_op jit(solution)/shard_map/ppermute | solution.py:307
  3.1 0.1 stack.27.who
  3.1 1.2 %copy-done = f32[1024,256]{1,0:T(8,128)S(1)} copy-done((f32[1024,256]{1,0:T(8,128)S(1)}, f32[1024,256]{1,0:T(8,128)}, u32[]{:S(2)}) %copy-start) | copy-done | bytes 1048600
  4.4 0.6 cot_give.1
  5.0 1.6 %collective-permute-start.3 = (f32[512,256]{1,0:T(8,128)S(1)}, f32[512,256]{1,0:T(8,128)S(1)}, u32[]{:S(2)}, u32[]{:S(2)}) collective-permute-start(f32[512,256]{1,0:T(8,128)S(1)} %cot_give.1), channel_id=1, source_target_pairs={{0,1},{1,0},{2,3},{3,2},{4,5},{5,4},{6,7},{7,6},{8,9},{9,8},{10,11... | collective-permute-start | bytes 1572872 | tf_op jit(solution)/shard_map/ppermute | solution.py:313
  6.5 0.5 collective-permute-start.2
  7.1 0.1 collective-permute-start
  7.2 0.7 copy-done.4
  7.9 0.7 copy-done.5
  8.6 0.7 copy-done.6
  9.2 14.8 %lay_out.1 = (bf16[2,4,1024,1024]{3,2,1,0:T(8,128)(2,1)S(1)}, bf16[2,4,1024,1024]{3,2,1,0:T(8,128)(2,1)S(1)}) custom-call(s32[4,24]{1,0:T(4,128)S(1)} %bitcast.9, s32[4,24]{1,0:T(4,128)S(1)} %bitcast.10, s32[1,4]{1,0:T(1,128)S(1)} %copy-done.6, s32[8]{0:T(128)S(1)} %stack.27.who, f32[4,24,128,128]{3,2,1,0:T(8,128)} %bitcast.11), custom_call_target="tpu_custom_call" | custom-call | bytes 20000000 | tf_op jit(solution)/shard_map/lay_out/pallas_call | solution.py:75
  24.1 0.0 copy-start.2
  24.1 1.2 %copy-done.2 = f32[1024,256]{1,0:T(8,128)S(1)} copy-done((f32[1024,256]{1,0:T(8,128)S(1)}, f32[1024,256]{1,0:T(8,128)}, u32[]{:S(2)}) %copy-start.2) | copy-done | bytes 1048600
  25.3 3.0 %agg_own.1.refs_1_ = f32[1024,256]{1,0:T(8,128)S(1)} custom-call(s32[8]{0:T(128)S(1)} %stack.27.who, bf16[2,4,1024,1024]{3,2,1,0:T(8,128)(2,1)S(1)} %get-tuple-element.39.matrix, f32[1024,256]{1,0:T(8,128)S(1)} %copy-done.2), custom_call_target="tpu_custom_call" | custom-call | flops 1610612736 | bytes 17825792 | tf_op jit(solution)/shard_map/agg_own/pallas_call | solution.py:39
  28.4 2.4 %collective-permute-done.2.w_there = f32[512,256]{1,0:T(8,128)S(1)} collective-permute-done((f32[512,256]{1,0:T(8,128)}, f32[512,256]{1,0:T(8,128)S(1)}, u32[]{:S(2)}, u32[]{:S(2)}) %collective-permute-start.2) | collective-permute-done | bytes 524320 | tf_op jit(solution)/shard_map/ppermute | solution.py:313
  30.8 0.1 fusion
  30.8 0.1 collective-permute-start.5
  30.9 0.5 collective-permute-start.4
  31.4 3.0 %agg_near.1.refs_2_.refs_3_ = f32[1024,256]{1,0:T(8,128)S(1)} custom-call(s32[8]{0:T(128)S(1)} %stack.27.who, bf16[2,4,1024,1024]{3,2,1,0:T(8,128)(2,1)S(1)} %get-tuple-element.39.matrix, f32[1024,256]{1,0:T(8,128)S(1)} %collective-permute-done.1.refs_0_, f32[1024,256]{1,0:T(8,128)S(1)} %agg_own.1.refs_1_), custom_call_target="tpu_custom_call" | custom-call | flops 1610612736 | bytes 18874368 | tf_op jit(solution)/shard_map/agg_near/pallas_call | solution.py:39
  34.5 1.9 %agg_two.1.refs_1_ = f32[512,256]{1,0:T(8,128)S(1)} custom-call(s32[8]{0:T(128)S(1)} %stack.27.who, bf16[2,4,1024,1024]{3,2,1,0:T(8,128)(2,1)S(1)} %get-tuple-element.39.matrix, f32[512,256]{1,0:T(8,128)S(1)} %collective-permute-done.4.refs_0_.refs_1_, f32[512,256]{1,0:T(8,128)S(1)} %collective-permute-done.5.refs_1_.refs_2_, ...), custom_call_target="tpu_custom_call" | custom-call | flops 805306368 | bytes 18874368 | tf_op jit(solution)/shard_map/agg_two/pallas_call | solution.py:39
  36.4 1.9 %agg_give.1 = f32[512,256]{1,0:T(8,128)S(1)} custom-call(s32[8]{0:T(128)S(1)} %stack.27.who, bf16[2,4,1024,1024]{3,2,1,0:T(8,128)(2,1)S(1)} %get-tuple-element.39.matrix, f32[1024,256]{1,0:T(8,128)S(1)} %collective-permute-done.refs_0_, f32[512,256]{1,0:T(8,128)S(1)} %agg_two.1.refs_1_), custom_call_target="tpu_custom_call" | custom-call | flops 805306368 | bytes 18350080 | tf_op jit(solution)/shard_map/agg_give/pallas_call | solution.py:39
  38.3 1.6 %collective-permute-start.6 = (f32[512,256]{1,0:T(8,128)S(1)}, f32[512,256]{1,0:T(8,128)S(1)}, u32[]{:S(2)}, u32[]{:S(2)}) collective-permute-start(f32[512,256]{1,0:T(8,128)S(1)} %agg_give.1), channel_id=1, source_target_pairs={{0,1},{1,0},{2,3},{3,2},{4,5},{5,4},{6,7},{7,6},{8,9},{9,8},{10,11... | collective-permute-start | bytes 1572872 | tf_op jit(solution)/shard_map/ppermute | solution.py:313
  39.9 2.9 %agg_keep.1.own = f32[512,256]{1,0:T(8,128)S(1)} custom-call(s32[8]{0:T(128)S(1)} %stack.27.who, bf16[2,4,1024,1024]{3,2,1,0:T(8,128)(2,1)S(1)} %get-tuple-element.39.matrix, f32[1024,256]{1,0:T(8,128)S(1)} %collective-permute-done.refs_0_, f32[512,256]{1,0:T(8,128)S(1)} %collective-permute-done.4.refs_0_.refs_1_, ...), custom_call_target="tpu_custom_call" | custom-call | flops 1610612736 | bytes 19922944 | tf_op jit(solution)/shard_map/agg_keep/pallas_call | solution.py:39
  42.8 9.5 %collective-permute-done.6.far = f32[512,256]{1,0:T(8,128)S(1)} collective-permute-done((f32[512,256]{1,0:T(8,128)S(1)}, f32[512,256]{1,0:T(8,128)S(1)}, u32[]{:S(2)}, u32[]{:S(2)}) %collective-permute-start.6) | collective-permute-done | bytes 524320 | tf_op jit(solution)/shard_map/ppermute | solution.py:313
  52.3 2.3 %middle.1 = (f32[512,256]{1,0:T(8,128)S(1)}, f32[512,256]{1,0:T(8,128)S(1)}, f32[512,256]{1,0:T(8,128)S(1)}, f32[512,256]{1,0:T(8,128)S(1)}, f32[512,256]{1,0:T(8,128)S(1)}) custom-call(s32[8]{0:T(128)S(1)} %stack.27.who, f32[512,256]{1,0:T(8,128)S(1)} %agg_keep.1.own, f32[512,256]{1,0:T(8,128)S(1)} %collective-permute-done.6.far, f32[512,256]{1,0:T(8,128)S(1)} %copy-done.3, ...), custom_call_target="tpu_custom_call" | custom-call | flops 1207959552 | bytes 3670016 | tf_op jit(solution)/shard_map/middle/pallas_call | solution.py:39
  54.6 1.2 %weight_give.1 = f32[256,512]{1,0:T(8,128)S(1)} custom-call(s32[8]{0:T(128)S(1)} %stack.27.who, f32[512,256]{1,0:T(8,128)S(1)} %agg_keep.1.own, f32[512,256]{1,0:T(8,128)S(1)} %collective-permute-done.6.far, f32[512,256]{1,0:T(8,128)S(1)} %get-tuple-element.52.grad_here, f32[512,256]{1,0:T(8,128)S(1)} %get-tuple-element.45.grad_there), custom_call_target="tpu_custom_call" | custom-call | flops 402653184 | bytes 2097152 | tf_op jit(solution)/shard_map/weight_give/pallas_call | solution.py:39
  55.8 0.1 collective-permute-start.7
  55.9 1.6 %collective-permute-start.8 = (f32[512,256]{1,0:T(8,128)S(1)}, f32[512,256]{1,0:T(8,128)S(1)}, u32[]{:S(2)}, u32[]{:S(2)}) collective-permute-start(f32[512,256]{1,0:T(8,128)S(1)} %get-tuple-element.50), channel_id=1, source_target_pairs={{0,1},{1,0},{2,3},{3,2},{4,5},{5,4},{6,7},{7,6},{8,9},{9,8},{10,11... | collective-permute-start | bytes 1572872 | tf_op jit(solution)/shard_map/ppermute | solution.py:313
  57.5 1.2 %weight_keep.1.one = f32[256,512]{1,0:T(8,128)S(1)} custom-call(s32[8]{0:T(128)S(1)} %stack.27.who, f32[512,256]{1,0:T(8,128)S(1)} %agg_keep.1.own, f32[512,256]{1,0:T(8,128)S(1)} %collective-permute-done.6.far, f32[512,256]{1,0:T(8,128)S(1)} %get-tuple-element.52.grad_here, f32[512,256]{1,0:T(8,128)S(1)} %get-tuple-element.45.grad_there), custom_call_target="tpu_custom_call" | custom-call | flops 402653184 | bytes 2097152 | tf_op jit(solution)/shard_map/weight_keep/pallas_call | solution.py:39
  58.8 0.6 core_sum.1
  59.4 5.4 %collective-permute-start.9 = (f32[256,256]{1,0:T(8,128)S(1)}, f32[256,256]{1,0:T(8,128)S(1)}, u32[]{:S(2)}, u32[]{:S(2)}) collective-permute-start(f32[256,256]{1,0:T(8,128)S(1)} %get-tuple-element.56.refs_0_), channel_id=1, source_target_pairs={{0,4},{2,6},{8,12},{10,14},{16,20},{18,22},{24,28},{26,30},{1,5},{... | collective-permute-start | bytes 786440 | tf_op jit(solution)/shard_map/ppermute | solution.py:313
  64.8 1.2 keep.1.source
  66.0 3.9 %back_here.1 = (f32[1024,256]{1,0:T(8,128)S(1)}, f32[1024,256]{1,0:T(8,128)S(1)}, f32[1024,256]{1,0:T(8,128)S(1)}, f32[1024,256]{1,0:T(8,128)S(1)}) custom-call(s32[8]{0:T(128)S(1)} %stack.27.who, bf16[2,4,1024,1024]{3,2,1,0:T(8,128)(2,1)S(1)} %get-tuple-element.49.matrix, f32[512,256]{1,0:T(8,128)S(1)} %keep.1.source), custom_call_target="tpu_custom_call" | custom-call | flops 3221225472 | bytes 17301504 | tf_op jit(solution)/shard_map/back_here/pallas_call | solution.py:39
  69.9 0.3 collective-permute-done.8.source
  70.3 1.5 %back_two.1 = f32[1024,256]{1,0:T(8,128)S(1)} custom-call(s32[8]{0:T(128)S(1)} %stack.27.who, bf16[2,4,1024,1024]{3,2,1,0:T(8,128)(2,1)S(1)} %get-tuple-element.49.matrix, f32[512,256]{1,0:T(8,128)S(1)} %collective-permute-done.8.source, f32[1024,256]{1,0:T(8,128)S(1)} %get-tuple-element.54.refs_0_), custom_call_target="tpu_custom_call" | custom-call | flops 805306368 | bytes 18350080 | tf_op jit(solution)/shard_map/back_two/pallas_call | solution.py:39
  71.8 0.6 chip_there.1
  72.4 0.1 collective-permute-start.10
  72.5 1.5 %back_far.1 = f32[1024,256]{1,0:T(8,128)S(1)} custom-call(s32[8]{0:T(128)S(1)} %stack.27.who, bf16[2,4,1024,1024]{3,2,1,0:T(8,128)(2,1)S(1)} %get-tuple-element.49.matrix, f32[512,256]{1,0:T(8,128)S(1)} %collective-permute-done.8.source, f32[1024,256]{1,0:T(8,128)S(1)} %get-tuple-element.58.refs_0_), custom_call_target="tpu_custom_call" | custom-call | flops 805306368 | bytes 18350080 | tf_op jit(solution)/shard_map/back_far/pallas_call | solution.py:39
  74.0 3.8 %collective-permute-start.13 = (f32[1024,256]{1,0:T(8,128)S(1)}, f32[1024,256]{1,0:T(8,128)S(1)}, u32[]{:S(2)}, u32[]{:S(2)}) collective-permute-start(f32[1024,256]{1,0:T(8,128)S(1)} %back_far.1), channel_id=1, source_target_pairs={{0,26},{2,0},{4,30},{6,4},{8,2},{10,8},{12,6},{14,12},{16,10},{18,... | collective-permute-start | bytes 3145736 | tf_op jit(solution)/shard_map/ppermute | solution.py:307
  77.8 3.6 %collective-permute-start.11 = (f32[256,256]{1,0:T(8,128)S(1)}, f32[256,256]{1,0:T(8,128)S(1)}, u32[]{:S(2)}, u32[]{:S(2)}) collective-permute-start(f32[256,256]{1,0:T(8,128)S(1)} %get-tuple-element.62.one), channel_id=1, source_target_pairs={{0,4},{2,6},{8,12},{10,14},{16,20},{18,22},{24,28},{26,30},{1,5},{... | collective-permute-start | bytes 786440 | tf_op jit(solution)/shard_map/ppermute | solution.py:313
  81.4 1.8 %collective-permute-start.12 = (f32[256,256]{1,0:T(8,128)S(1)}, f32[256,256]{1,0:T(8,128)S(1)}, u32[]{:S(2)}, u32[]{:S(2)}) collective-permute-start(f32[256,256]{1,0:T(8,128)S(1)} %chip_there.1), channel_id=1, source_target_pairs={{0,1},{1,0},{2,3},{3,2},{4,5},{5,4},{6,7},{7,6},{8,9},{9,8},{10,11... | collective-permute-start | bytes 786440 | tf_op jit(solution)/shard_map/ppermute | solution.py:313
  83.2 1.5 %back_near.1 = f32[1024,256]{1,0:T(8,128)S(1)} custom-call(s32[8]{0:T(128)S(1)} %stack.27.who, bf16[2,4,1024,1024]{3,2,1,0:T(8,128)(2,1)S(1)} %get-tuple-element.49.matrix, f32[512,256]{1,0:T(8,128)S(1)} %collective-permute-done.8.source, f32[1024,256]{1,0:T(8,128)S(1)} %get-tuple-element.60.refs_0_, f32[1024,256]{1,0:T(8,128)S(1)} %collective-permute-done.10.refs_1_), custom_call_target="tpu_custom_call" | custom-call | flops 805306368 | bytes 19398656 | tf_op jit(solution)/shard_map/back_near/pallas_call | solution.py:39
  84.8 0.1 collective-permute-start.20
  84.8 0.7 collective-permute-done.11.two
  85.5 2.4 %collective-permute-done.12.three = f32[256,256]{1,0:T(8,128)S(1)} collective-permute-done((f32[256,256]{1,0:T(8,128)S(1)}, f32[256,256]{1,0:T(8,128)S(1)}, u32[]{:S(2)}, u32[]{:S(2)}) %collective-permute-start.12) | collective-permute-done | bytes 262176 | tf_op jit(solution)/shard_map/ppermute | solution.py:313
  87.9 0.6 side_sum.1
  88.5 1.8 %collective-permute-start.16 = (f32[512,256]{1,0:T(8,128)S(1)}, f32[512,256]{1,0:T(8,128)S(1)}, u32[]{:S(2)}, u32[]{:S(2)}) collective-permute-start(f32[512,256]{1,0:T(8,128)S(1)} %get-tuple-element.71), channel_id=1, source_target_pairs={{0,1},{1,0},{2,3},{3,2},{4,5},{5,4},{6,7},{7,6},{8,9},{9,8},{10,11... | collective-permute-start | bytes 1572872 | tf_op jit(solution)/shard_map/ppermute | solution.py:313
  90.3 0.7 collective-permute-start.14
  90.9 1.5 %back_own.1.refs_0_ = f32[1024,256]{1,0:T(8,128)S(1)} custom-call(s32[8]{0:T(128)S(1)} %stack.27.who, bf16[2,4,1024,1024]{3,2,1,0:T(8,128)(2,1)S(1)} %get-tuple-element.49.matrix, f32[512,256]{1,0:T(8,128)S(1)} %collective-permute-done.8.source, f32[1024,256]{1,0:T(8,128)S(1)} %get-tuple-element.66.refs_0_), custom_call_target="tpu_custom_call" | custom-call | flops 805306368 | bytes 18350080 | tf_op jit(solution)/shard_map/back_own/pallas_call | solution.py:39
  92.5 1.7 %collective-permute-done.13.refs_1_ = f32[1024,256]{1,0:T(8,128)S(1)} collective-permute-done((f32[1024,256]{1,0:T(8,128)S(1)}, f32[1024,256]{1,0:T(8,128)S(1)}, u32[]{:S(2)}, u32[]{:S(2)}) %collective-permute-start.13) | collective-permute-done | bytes 1048608 | tf_op jit(solution)/shard_map/ppermute | solution.py:307
  94.2 0.6 layer_sum.1.refs_0_
  94.7 0.7 collective-permute-start.15
  95.4 0.6 pair_sum.1.ready
  96.0 1.3 %collective-permute-start.19 = (f32[128,256]{1,0:T(8,128)S(1)}, f32[128,256]{1,0:T(8,128)S(1)}, u32[]{:S(2)}, u32[]{:S(2)}) collective-permute-start(f32[128,256]{1,0:T(8,128)S(1)} %pair_sum.1.ready), channel_id=1, source_target_pairs={{4,8},{6,10},{12,0},{14,2},{20,24},{22,26},{28,16},{30,18},{5,9},{... | collective-permute-start | bytes 393224 | tf_op jit(solution)/shard_map/ppermute | solution.py:313
  97.3 1.3 %collective-permute-start.18 = (f32[128,256]{1,0:T(8,128)S(1)}, f32[128,256]{1,0:T(8,128)S(1)}, u32[]{:S(2)}, u32[]{:S(2)}) collective-permute-start(f32[128,256]{1,0:T(8,128)S(1)} %pair_sum.1.ready), channel_id=1, source_target_pairs={{4,0},{6,2},{12,8},{14,10},{20,16},{22,18},{28,24},{30,26},{5,1},{... | collective-permute-start | bytes 393224 | tf_op jit(solution)/shard_map/ppermute | solution.py:313
  98.6 0.7 collective-permute-start.17
  99.3 0.8 collective-permute-done.16.refs_1_
  100.1 1.6 %activated.1 = f32[1024,256]{1,0:T(8,128)} custom-call(s32[8]{0:T(128)S(1)} %stack.27.who, f32[512,256]{1,0:T(8,128)S(1)} %get-tuple-element.69.refs_0_, f32[512,256]{1,0:T(8,128)S(1)} %collective-permute-done.16.refs_1_), custom_call_target="tpu_custom_call" | custom-call | bytes 1048576 | tf_op jit(solution)/shard_map/activated/pallas_call | solution.py:39
  101.6 13.4 %collective-permute-done.19.later_sent = f32[128,256]{1,0:T(8,128)S(1)} collective-permute-done((f32[128,256]{1,0:T(8,128)S(1)}, f32[128,256]{1,0:T(8,128)S(1)}, u32[]{:S(2)}, u32[]{:S(2)}) %collective-permute-start.19) | collective-permute-done | bytes 131104 | tf_op jit(solution)/shard_map/ppermute | solution.py:313
  115.1 0.8 collective-permute-done.18.ready_sent
  115.9 0.6 chip_pick.1.refs_0_
  116.5 0.1 collective-permute-start.21
  116.5 1.7 %feature_grad.1 = f32[1024,256]{1,0:T(8,128)} custom-call(s32[8]{0:T(128)S(1)} %stack.27.who, f32[1024,256]{1,0:T(8,128)S(1)} %back_own.1.refs_0_, f32[1024,256]{1,0:T(8,128)S(1)} %collective-permute-done.13.refs_1_, f32[1024,256]{1,0:T(8,128)S(1)} %collective-permute-done.20.refs_2_), custom_call_target="tpu_custom_call" | custom-call | bytes 3145728 | tf_op jit(solution)/shard_map/feature_grad/pallas_call | solution.py:39
  118.2 1.4 %weight_grad.1 = f32[512,256]{1,0:T(8,128)} custom-call(s32[8]{0:T(128)S(1)} %stack.27.who, f32[256,256]{1,0:T(8,128)S(1)} %chip_pick.1.refs_0_, f32[256,256]{1,0:T(8,128)S(1)} %collective-permute-done.21.refs_1_), custom_call_target="tpu_custom_call" | custom-call | bytes 524288 | tf_op jit(solution)/shard_map/weight_grad/pallas_call | solution.py:39
  (21 shorter events, 0.1 us)
Async XLA Ops:
  0.6 30.1 %collective-permute-start.1 = (f32[1024,256]{1,0:T(8,128)}, f32[1024,256]{1,0:T(8,128)S(1)}, u32[]{:S(2)}, u32[]{:S(2)}) collective-permute-start(f32[1024,256]{1,0:T(8,128)} %refs_0_.1), channel_id=1, source_target_pairs={{0,6},{2,4},{4,10},{6,8},{8,14},{10,12},{12,18},{14,16},{16,22},{1... | collective-permute-start | bytes 3145736 | tf_op jit(solution)/shard_map/ppermute | solution.py:307
  3.1 1.2 %copy-start = (f32[1024,256]{1,0:T(8,128)S(1)}, f32[1024,256]{1,0:T(8,128)}, u32[]{:S(2)}) copy-start(f32[1024,256]{1,0:T(8,128)} %cot.1) | copy-start | bytes 3145732
  5.0 23.4 %collective-permute-start.3 = (f32[512,256]{1,0:T(8,128)S(1)}, f32[512,256]{1,0:T(8,128)S(1)}, u32[]{:S(2)}, u32[]{:S(2)}) collective-permute-start(f32[512,256]{1,0:T(8,128)S(1)} %cot_give.1), channel_id=1, source_target_pairs={{0,1},{1,0},{2,3},{3,2},{4,5},{5,4},{6,7},{7,6},{8,9},{9,8},{10,11... | collective-permute-start | bytes 1572872 | tf_op jit(solution)/shard_map/ppermute | solution.py:313
  6.5 24.2 %collective-permute-start.2 = (f32[512,256]{1,0:T(8,128)}, f32[512,256]{1,0:T(8,128)S(1)}, u32[]{:S(2)}, u32[]{:S(2)}) collective-permute-start(f32[512,256]{1,0:T(8,128)} %w_here.3), channel_id=1, source_target_pairs={{0,1},{1,0},{2,3},{3,2},{4,5},{5,4},{6,7},{7,6},{8,9},{9,8},{10,11... | collective-permute-start | bytes 1572872 | tf_op jit(solution)/shard_map/ppermute | solution.py:313
  7.1 29.4 %collective-permute-start = (f32[1024,256]{1,0:T(8,128)}, f32[1024,256]{1,0:T(8,128)S(1)}, u32[]{:S(2)}, u32[]{:S(2)}) collective-permute-start(f32[1024,256]{1,0:T(8,128)} %refs_0_.1), channel_id=1, source_target_pairs={{0,2},{2,8},{4,6},{6,12},{8,10},{10,16},{12,14},{14,20},{16,18},{1... | collective-permute-start | bytes 3145736 | tf_op jit(solution)/shard_map/ppermute | solution.py:307
  7.2 0.7 copy-start.4
  7.9 0.7 copy-start.5
  8.6 0.7 copy-start.6
  24.1 1.2 %copy-start.2 = (f32[1024,256]{1,0:T(8,128)S(1)}, f32[1024,256]{1,0:T(8,128)}, u32[]{:S(2)}) copy-start(f32[1024,256]{1,0:T(8,128)} %refs_0_.1) | copy-start | bytes 3145732
  30.8 3.6 %collective-permute-start.5 = (f32[512,256]{1,0:T(8,128)S(1)}, f32[512,256]{1,0:T(8,128)S(1)}, u32[]{:S(2)}, u32[]{:S(2)}) collective-permute-start(f32[512,256]{1,0:T(8,128)S(1)} %get-tuple-element.75), channel_id=1, source_target_pairs={{0,2},{2,0},{4,6},{6,4},{8,10},{10,8},{12,14},{14,12},{16,18},{18,... | collective-permute-start | bytes 1572872 | tf_op jit(solution)/shard_map/ppermute | solution.py:313
  30.9 3.5 %collective-permute-start.4 = (f32[512,256]{1,0:T(8,128)S(1)}, f32[512,256]{1,0:T(8,128)S(1)}, u32[]{:S(2)}, u32[]{:S(2)}) collective-permute-start(f32[512,256]{1,0:T(8,128)S(1)} %get-tuple-element.76), channel_id=1, source_target_pairs={{0,2},{2,0},{4,6},{6,4},{8,10},{10,8},{12,14},{14,12},{16,18},{18,... | collective-permute-start | bytes 1572872 | tf_op jit(solution)/shard_map/ppermute | solution.py:313
  36.4 15.9 %copy-start.1 = (f32[1024,256]{1,0:T(8,128)S(1)}, f32[1024,256]{1,0:T(8,128)}, u32[]{:S(2)}) copy-start(f32[1024,256]{1,0:T(8,128)} %cot.1) | copy-start | bytes 3145732
  36.4 15.9 %copy-start.3 = (f32[512,256]{1,0:T(8,128)S(1)}, f32[512,256]{1,0:T(8,128)}, u32[]{:S(2)}) copy-start(f32[512,256]{1,0:T(8,128)} %w_here.3) | copy-start | bytes 1572868
  38.3 14.0 %collective-permute-start.6 = (f32[512,256]{1,0:T(8,128)S(1)}, f32[512,256]{1,0:T(8,128)S(1)}, u32[]{:S(2)}, u32[]{:S(2)}) collective-permute-start(f32[512,256]{1,0:T(8,128)S(1)} %agg_give.1), channel_id=1, source_target_pairs={{0,1},{1,0},{2,3},{3,2},{4,5},{5,4},{6,7},{7,6},{8,9},{9,8},{10,11... | collective-permute-start | bytes 1572872 | tf_op jit(solution)/shard_map/ppermute | solution.py:313
  55.8 2.9 %collective-permute-start.7 = (f32[256,512]{1,0:T(8,128)S(1)}, f32[256,512]{1,0:T(8,128)S(1)}, u32[]{:S(2)}, u32[]{:S(2)}) collective-permute-start(f32[256,512]{1,0:T(8,128)S(1)} %weight_give.1), channel_id=1, source_target_pairs={{0,2},{2,0},{4,6},{6,4},{8,10},{10,8},{12,14},{14,12},{16,18},{18,... | collective-permute-start | bytes 1572872 | tf_op jit(solution)/shard_map/ppermute | solution.py:313
  55.9 14.3 %collective-permute-start.8 = (f32[512,256]{1,0:T(8,128)S(1)}, f32[512,256]{1,0:T(8,128)S(1)}, u32[]{:S(2)}, u32[]{:S(2)}) collective-permute-start(f32[512,256]{1,0:T(8,128)S(1)} %get-tuple-element.50), channel_id=1, source_target_pairs={{0,1},{1,0},{2,3},{3,2},{4,5},{5,4},{6,7},{7,6},{8,9},{9,8},{10,11... | collective-permute-start | bytes 1572872 | tf_op jit(solution)/shard_map/ppermute | solution.py:313
  59.4 12.4 %collective-permute-start.9 = (f32[256,256]{1,0:T(8,128)S(1)}, f32[256,256]{1,0:T(8,128)S(1)}, u32[]{:S(2)}, u32[]{:S(2)}) collective-permute-start(f32[256,256]{1,0:T(8,128)S(1)} %get-tuple-element.56.refs_0_), channel_id=1, source_target_pairs={{0,4},{2,6},{8,12},{10,14},{16,20},{18,22},{24,28},{26,30},{1,5},{... | collective-permute-start | bytes 786440 | tf_op jit(solution)/shard_map/ppermute | solution.py:313
  72.4 10.8 %collective-permute-start.10 = (f32[1024,256]{1,0:T(8,128)S(1)}, f32[1024,256]{1,0:T(8,128)S(1)}, u32[]{:S(2)}, u32[]{:S(2)}) collective-permute-start(f32[1024,256]{1,0:T(8,128)S(1)} %back_two.1), channel_id=1, source_target_pairs={{0,2},{2,0},{4,6},{6,4},{8,10},{10,8},{12,14},{14,12},{16,18},{18,... | collective-permute-start | bytes 3145736 | tf_op jit(solution)/shard_map/ppermute | solution.py:313
  74.0 20.1 %collective-permute-start.13 = (f32[1024,256]{1,0:T(8,128)S(1)}, f32[1024,256]{1,0:T(8,128)S(1)}, u32[]{:S(2)}, u32[]{:S(2)}) collective-permute-start(f32[1024,256]{1,0:T(8,128)S(1)} %back_far.1), channel_id=1, source_target_pairs={{0,26},{2,0},{4,30},{6,4},{8,2},{10,8},{12,6},{14,12},{16,10},{18,... | collective-permute-start | bytes 3145736 | tf_op jit(solution)/shard_map/ppermute | solution.py:307
  77.8 7.7 %collective-permute-start.11 = (f32[256,256]{1,0:T(8,128)S(1)}, f32[256,256]{1,0:T(8,128)S(1)}, u32[]{:S(2)}, u32[]{:S(2)}) collective-permute-start(f32[256,256]{1,0:T(8,128)S(1)} %get-tuple-element.62.one), channel_id=1, source_target_pairs={{0,4},{2,6},{8,12},{10,14},{16,20},{18,22},{24,28},{26,30},{1,5},{... | collective-permute-start | bytes 786440 | tf_op jit(solution)/shard_map/ppermute | solution.py:313
  81.4 6.4 %collective-permute-start.12 = (f32[256,256]{1,0:T(8,128)S(1)}, f32[256,256]{1,0:T(8,128)S(1)}, u32[]{:S(2)}, u32[]{:S(2)}) collective-permute-start(f32[256,256]{1,0:T(8,128)S(1)} %chip_there.1), channel_id=1, source_target_pairs={{0,1},{1,0},{2,3},{3,2},{4,5},{5,4},{6,7},{7,6},{8,9},{9,8},{10,11... | collective-permute-start | bytes 786440 | tf_op jit(solution)/shard_map/ppermute | solution.py:313
  84.8 31.8 %collective-permute-start.20 = (f32[1024,256]{1,0:T(8,128)S(1)}, f32[1024,256]{1,0:T(8,128)S(1)}, u32[]{:S(2)}, u32[]{:S(2)}) collective-permute-start(f32[1024,256]{1,0:T(8,128)S(1)} %back_near.1), channel_id=1, source_target_pairs={{0,30},{2,28},{4,2},{6,0},{8,6},{10,4},{12,10},{14,8},{16,14},{18,... | collective-permute-start | bytes 3145736 | tf_op jit(solution)/shard_map/ppermute | solution.py:307
  88.5 11.6 %collective-permute-start.16 = (f32[512,256]{1,0:T(8,128)S(1)}, f32[512,256]{1,0:T(8,128)S(1)}, u32[]{:S(2)}, u32[]{:S(2)}) collective-permute-start(f32[512,256]{1,0:T(8,128)S(1)} %get-tuple-element.71), channel_id=1, source_target_pairs={{0,1},{1,0},{2,3},{3,2},{4,5},{5,4},{6,7},{7,6},{8,9},{9,8},{10,11... | collective-permute-start | bytes 1572872 | tf_op jit(solution)/shard_map/ppermute | solution.py:313
  90.3 3.9 %collective-permute-start.14 = (f32[128,256]{1,0:T(8,128)S(1)}, f32[128,256]{1,0:T(8,128)S(1)}, u32[]{:S(2)}, u32[]{:S(2)}) collective-permute-start(f32[128,256]{1,0:T(8,128)S(1)} %get-tuple-element.64), channel_id=1, source_target_pairs={{4,12},{6,14},{12,4},{14,6},{20,28},{22,30},{28,20},{30,22},{5,13}... | collective-permute-start | bytes 393224 | tf_op jit(solution)/shard_map/ppermute | solution.py:313
  94.7 0.7 collective-permute-start.15
  96.0 19.1 %collective-permute-start.19 = (f32[128,256]{1,0:T(8,128)S(1)}, f32[128,256]{1,0:T(8,128)S(1)}, u32[]{:S(2)}, u32[]{:S(2)}) collective-permute-start(f32[128,256]{1,0:T(8,128)S(1)} %pair_sum.1.ready), channel_id=1, source_target_pairs={{4,8},{6,10},{12,0},{14,2},{20,24},{22,26},{28,16},{30,18},{5,9},{... | collective-permute-start | bytes 393224 | tf_op jit(solution)/shard_map/ppermute | solution.py:313
  97.3 18.6 %collective-permute-start.18 = (f32[128,256]{1,0:T(8,128)S(1)}, f32[128,256]{1,0:T(8,128)S(1)}, u32[]{:S(2)}, u32[]{:S(2)}) collective-permute-start(f32[128,256]{1,0:T(8,128)S(1)} %pair_sum.1.ready), channel_id=1, source_target_pairs={{4,0},{6,2},{12,8},{14,10},{20,16},{22,18},{28,24},{30,26},{5,1},{... | collective-permute-start | bytes 393224 | tf_op jit(solution)/shard_map/ppermute | solution.py:313
  98.6 17.3 %collective-permute-start.17 = (f32[128,256]{1,0:T(8,128)S(1)}, f32[128,256]{1,0:T(8,128)S(1)}, u32[]{:S(2)}, u32[]{:S(2)}) collective-permute-start(f32[128,256]{1,0:T(8,128)S(1)} %pair_sum.1.ready), channel_id=1, source_target_pairs={{4,12},{6,14},{12,4},{14,6},{20,28},{22,30},{28,20},{30,22},{5,13}... | collective-permute-start | bytes 393224 | tf_op jit(solution)/shard_map/ppermute | solution.py:313
  116.5 1.8 %collective-permute-start.21 = (f32[256,256]{1,0:T(8,128)S(1)}, f32[256,256]{1,0:T(8,128)S(1)}, u32[]{:S(2)}, u32[]{:S(2)}) collective-permute-start(f32[256,256]{1,0:T(8,128)S(1)} %chip_pick.1.refs_0_), channel_id=1, source_target_pairs={{0,2},{2,0},{4,6},{6,4},{8,10},{10,8},{12,14},{14,12},{16,18},{18,... | collective-permute-start | bytes 786440 | tf_op jit(solution)/shard_map/ppermute | solution.py:313

commit v5 on v4

--- a/solution.py
+++ b/solution.py
@@ -376,12 +376,11 @@
     )[0]
     firsts = backward("back_here", who, t, [TWO, FAR, NEAR, OWN], after(g_here, last), [], 0)
     g_there = after(g_there, firsts[0])
-    last = backward("back_two", who, t, [TWO], g_there, [firsts[0]], 1)[0]
-    two_out = last
-    last = next(steps)(last)
+    two_out = backward("back_two", who, t, [TWO], g_there, [firsts[0]], 1)[0]
+    far_out = backward("back_far", who, t, [FAR], after(g_there, two_out), [firsts[1]], 1)[0]
+    last = next(steps)(far_out)
     two = swapped(after(two_out, last), "dom")
-    last = backward("back_far", who, t, [FAR], after(g_there, last), [firsts[1]], 1)[0]
-    far = moved(last, "dom", -3, -1)
+    far = moved(after(far_out, last), "dom", -3, -1)
     last = backward("back_near", who, t, [NEAR], after(g_there, last), [firsts[2], two], 1)[0]
     near = moved(last, "dom", -1, -3)
     last = next(steps)(last)

time: 121 us -> 120 us (level)
  Pallas kernels: 52.3 us -> 44.1 us
  waiting for transfers between devices: 32 us -> 39.4 us
    pallas_call x1, Pallas kernels: 14.8 us -> 6.62 us  [lay_out(): pl.pallas_call(lay_out_kernel, grid_spec=pltpu.PrefetchScalarGridSpec(num...]
    ppermute x18, waiting for transfers between devices: 30.3 us -> 37.7 us  [chosen(): lax.ppermute(value, axis, [pair for pair in pairs if pair[1] is not None])]
  transfers between devices with their start and end apart: 22 -> 22, of which waited for: 9 -> 9; matrix products, arithmetic and copies ran while one was open for 0% -> 0% of each run, Pallas kernels for 38% -> 31%
where the time goes in v5:
time: 120 us; the launch traced here: 119 us
  Pallas kernels  44.1 us (37%)
  waiting for transfers between devices  39.4 us (33%)
  starting transfers between devices  29.6 us (25%)
  local copies, waits for them, and re-layouts  4.63 us (4%)
    ppermute x18, waiting for transfers between devices, chosen(): lax.ppermute(value, axis, [pair for pair in pairs if pair[1] is not None])  37.7 us
    pallas_call x24, Pallas kernels, call(): pl.pallas_call(kernel, in_specs=[IN_SMEM] + [IN_VMEM] * len(operands), ou...  37.4 us
    ppermute x18, starting transfers between devices, chosen(): lax.ppermute(value, axis, [pair for pair in pairs if pair[1] is not None])  23.3 us
    pallas_call x1, Pallas kernels, lay_out(): pl.pallas_call(lay_out_kernel, grid_spec=pltpu.PrefetchScalarGridSpec(num...  6.62 us
    ppermute x4, starting transfers between devices, moved(): return lax.ppermute(value, axis, perm)  6.33 us
    unnamed x14, local copies, waits for them, and re-layouts  4.48 us
  transfers between devices with their start and end apart: 22, of which 9 were waited for; matrix products, arithmetic and copies ran while one was open for 0% of the time, Pallas kernels for 31%

profile of v5, /device:TPU:0, one launch (start us, length us, event | category | flops | bytes accessed | tf_op | source)
XLA Modules:
  0.0 118.7 jit_solution(3978690052502728955)
XLA Ops:
  0.6 2.4 %collective-permute-start.1 = (f32[1024,256]{1,0:T(8,128)}, f32[1024,256]{1,0:T(8,128)S(1)}, u32[]{:S(2)}, u32[]{:S(2)}) collective-permute-start(f32[1024,256]{1,0:T(8,128)} %refs_0_.1), channel_id=1, source_target_pairs={{0,6},{2,4},{4,10},{6,8},{8,14},{10,12},{12,18},{14,16},{16,22},{1... | collective-permute-start | bytes 3145736 | tf_op jit(solution)/shard_map/ppermute | solution.py:307
  3.1 0.1 stack.27.who
  3.1 1.2 %copy-done = f32[1024,256]{1,0:T(8,128)S(1)} copy-done((f32[1024,256]{1,0:T(8,128)S(1)}, f32[1024,256]{1,0:T(8,128)}, u32[]{:S(2)}) %copy-start) | copy-done | bytes 1048600
  4.4 0.6 cot_give.1
  5.0 1.6 %collective-permute-start.3 = (f32[512,256]{1,0:T(8,128)S(1)}, f32[512,256]{1,0:T(8,128)S(1)}, u32[]{:S(2)}, u32[]{:S(2)}) collective-permute-start(f32[512,256]{1,0:T(8,128)S(1)} %cot_give.1), channel_id=1, source_target_pairs={{0,1},{1,0},{2,3},{3,2},{4,5},{5,4},{6,7},{7,6},{8,9},{9,8},{10,11... | collective-permute-start | bytes 1572872 | tf_op jit(solution)/shard_map/ppermute | solution.py:313
  6.5 0.5 collective-permute-start.2
  7.1 0.1 collective-permute-start
  7.2 0.7 copy-done.4
  7.9 0.7 copy-done.5
  8.6 0.7 copy-done.6
  9.2 6.6 %lay_out.1 = (bf16[2,4,1024,1024]{3,2,1,0:T(8,128)(2,1)S(1)}, bf16[2,4,1024,1024]{3,2,1,0:T(8,128)(2,1)S(1)}) custom-call(s32[4,24]{1,0:T(4,128)S(1)} %bitcast.9, s32[4,24]{1,0:T(4,128)S(1)} %bitcast.10, s32[1,4]{1,0:T(1,128)S(1)} %copy-done.6, s32[8]{0:T(128)S(1)} %stack.27.who, f32[4,24,128,128]{3,2,1,0:T(8,128)} %bitcast.11), custom_call_target="tpu_custom_call" | custom-call | bytes 20000000 | tf_op jit(solution)/shard_map/lay_out/pallas_call | solution.py:75
  15.8 0.0 copy-start.2
  15.9 1.2 %copy-done.2 = f32[1024,256]{1,0:T(8,128)S(1)} copy-done((f32[1024,256]{1,0:T(8,128)S(1)}, f32[1024,256]{1,0:T(8,128)}, u32[]{:S(2)}) %copy-start.2) | copy-done | bytes 1048600
  17.1 3.0 %agg_own.1.refs_1_ = f32[1024,256]{1,0:T(8,128)S(1)} custom-call(s32[8]{0:T(128)S(1)} %stack.27.who, bf16[2,4,1024,1024]{3,2,1,0:T(8,128)(2,1)S(1)} %get-tuple-element.40.matrix, f32[1024,256]{1,0:T(8,128)S(1)} %copy-done.2), custom_call_target="tpu_custom_call" | custom-call | flops 1610612736 | bytes 17825792 | tf_op jit(solution)/shard_map/agg_own/pallas_call | solution.py:39
  20.1 10.6 %collective-permute-done.2.w_there = f32[512,256]{1,0:T(8,128)S(1)} collective-permute-done((f32[512,256]{1,0:T(8,128)}, f32[512,256]{1,0:T(8,128)S(1)}, u32[]{:S(2)}, u32[]{:S(2)}) %collective-permute-start.2) | collective-permute-done | bytes 524320 | tf_op jit(solution)/shard_map/ppermute | solution.py:313
  30.8 0.1 fusion
  30.8 0.1 collective-permute-start.5
  30.9 0.5 collective-permute-start.4
  31.4 3.0 %agg_near.1.refs_2_.refs_3_ = f32[1024,256]{1,0:T(8,128)S(1)} custom-call(s32[8]{0:T(128)S(1)} %stack.27.who, bf16[2,4,1024,1024]{3,2,1,0:T(8,128)(2,1)S(1)} %get-tuple-element.40.matrix, f32[1024,256]{1,0:T(8,128)S(1)} %collective-permute-done.1.refs_0_, f32[1024,256]{1,0:T(8,128)S(1)} %agg_own.1.refs_1_), custom_call_target="tpu_custom_call" | custom-call | flops 1610612736 | bytes 18874368 | tf_op jit(solution)/shard_map/agg_near/pallas_call | solution.py:39
  34.5 1.9 %agg_two.1.refs_1_ = f32[512,256]{1,0:T(8,128)S(1)} custom-call(s32[8]{0:T(128)S(1)} %stack.27.who, bf16[2,4,1024,1024]{3,2,1,0:T(8,128)(2,1)S(1)} %get-tuple-element.40.matrix, f32[512,256]{1,0:T(8,128)S(1)} %collective-permute-done.4.refs_0_.refs_1_, f32[512,256]{1,0:T(8,128)S(1)} %collective-permute-done.5.refs_1_.refs_2_, ...), custom_call_target="tpu_custom_call" | custom-call | flops 805306368 | bytes 18874368 | tf_op jit(solution)/shard_map/agg_two/pallas_call | solution.py:39
  36.4 1.9 %agg_give.1 = f32[512,256]{1,0:T(8,128)S(1)} custom-call(s32[8]{0:T(128)S(1)} %stack.27.who, bf16[2,4,1024,1024]{3,2,1,0:T(8,128)(2,1)S(1)} %get-tuple-element.40.matrix, f32[1024,256]{1,0:T(8,128)S(1)} %collective-permute-done.refs_0_, f32[512,256]{1,0:T(8,128)S(1)} %agg_two.1.refs_1_), custom_call_target="tpu_custom_call" | custom-call | flops 805306368 | bytes 18350080 | tf_op jit(solution)/shard_map/agg_give/pallas_call | solution.py:39
  38.3 1.6 %collective-permute-start.6 = (f32[512,256]{1,0:T(8,128)S(1)}, f32[512,256]{1,0:T(8,128)S(1)}, u32[]{:S(2)}, u32[]{:S(2)}) collective-permute-start(f32[512,256]{1,0:T(8,128)S(1)} %agg_give.1), channel_id=1, source_target_pairs={{0,1},{1,0},{2,3},{3,2},{4,5},{5,4},{6,7},{7,6},{8,9},{9,8},{10,11... | collective-permute-start | bytes 1572872 | tf_op jit(solution)/shard_map/ppermute | solution.py:313
  39.9 2.9 %agg_keep.1.own = f32[512,256]{1,0:T(8,128)S(1)} custom-call(s32[8]{0:T(128)S(1)} %stack.27.who, bf16[2,4,1024,1024]{3,2,1,0:T(8,128)(2,1)S(1)} %get-tuple-element.40.matrix, f32[1024,256]{1,0:T(8,128)S(1)} %collective-permute-done.refs_0_, f32[512,256]{1,0:T(8,128)S(1)} %collective-permute-done.4.refs_0_.refs_1_, ...), custom_call_target="tpu_custom_call" | custom-call | flops 1610612736 | bytes 19922944 | tf_op jit(solution)/shard_map/agg_keep/pallas_call | solution.py:39
  42.8 9.5 %collective-permute-done.6.far = f32[512,256]{1,0:T(8,128)S(1)} collective-permute-done((f32[512,256]{1,0:T(8,128)S(1)}, f32[512,256]{1,0:T(8,128)S(1)}, u32[]{:S(2)}, u32[]{:S(2)}) %collective-permute-start.6) | collective-permute-done | bytes 524320 | tf_op jit(solution)/shard_map/ppermute | solution.py:313
  52.3 2.3 %middle.1 = (f32[512,256]{1,0:T(8,128)S(1)}, f32[512,256]{1,0:T(8,128)S(1)}, f32[512,256]{1,0:T(8,128)S(1)}, f32[512,256]{1,0:T(8,128)S(1)}, f32[512,256]{1,0:T(8,128)S(1)}) custom-call(s32[8]{0:T(128)S(1)} %stack.27.who, f32[512,256]{1,0:T(8,128)S(1)} %agg_keep.1.own, f32[512,256]{1,0:T(8,128)S(1)} %collective-permute-done.6.far, f32[512,256]{1,0:T(8,128)S(1)} %copy-done.3, ...), custom_call_target="tpu_custom_call" | custom-call | flops 1207959552 | bytes 3670016 | tf_op jit(solution)/shard_map/middle/pallas_call | solution.py:39
  54.6 1.2 %weight_give.1 = f32[256,512]{1,0:T(8,128)S(1)} custom-call(s32[8]{0:T(128)S(1)} %stack.27.who, f32[512,256]{1,0:T(8,128)S(1)} %agg_keep.1.own, f32[512,256]{1,0:T(8,128)S(1)} %collective-permute-done.6.far, f32[512,256]{1,0:T(8,128)S(1)} %get-tuple-element.53.grad_here, f32[512,256]{1,0:T(8,128)S(1)} %get-tuple-element.46.grad_there), custom_call_target="tpu_custom_call" | custom-call | flops 402653184 | bytes 2097152 | tf_op jit(solution)/shard_map/weight_give/pallas_call | solution.py:39
  55.8 0.1 collective-permute-start.7
  55.9 1.6 %collective-permute-start.8 = (f32[512,256]{1,0:T(8,128)S(1)}, f32[512,256]{1,0:T(8,128)S(1)}, u32[]{:S(2)}, u32[]{:S(2)}) collective-permute-start(f32[512,256]{1,0:T(8,128)S(1)} %get-tuple-element.51), channel_id=1, source_target_pairs={{0,1},{1,0},{2,3},{3,2},{4,5},{5,4},{6,7},{7,6},{8,9},{9,8},{10,11... | collective-permute-start | bytes 1572872 | tf_op jit(solution)/shard_map/ppermute | solution.py:313
  57.5 1.2 %weight_keep.1.one = f32[256,512]{1,0:T(8,128)S(1)} custom-call(s32[8]{0:T(128)S(1)} %stack.27.who, f32[512,256]{1,0:T(8,128)S(1)} %agg_keep.1.own, f32[512,256]{1,0:T(8,128)S(1)} %collective-permute-done.6.far, f32[512,256]{1,0:T(8,128)S(1)} %get-tuple-element.53.grad_here, f32[512,256]{1,0:T(8,128)S(1)} %get-tuple-element.46.grad_there), custom_call_target="tpu_custom_call" | custom-call | flops 402653184 | bytes 2097152 | tf_op jit(solution)/shard_map/weight_keep/pallas_call | solution.py:39
  58.8 0.6 core_sum.1
  59.4 5.4 %collective-permute-start.9 = (f32[256,256]{1,0:T(8,128)S(1)}, f32[256,256]{1,0:T(8,128)S(1)}, u32[]{:S(2)}, u32[]{:S(2)}) collective-permute-start(f32[256,256]{1,0:T(8,128)S(1)} %get-tuple-element.59.refs_0_), channel_id=1, source_target_pairs={{0,4},{2,6},{8,12},{10,14},{16,20},{18,22},{24,28},{26,30},{1,5},{... | collective-permute-start | bytes 786440 | tf_op jit(solution)/shard_map/ppermute | solution.py:313
  64.8 1.2 %keep.1.source = f32[512,256]{1,0:T(8,128)S(1)} custom-call(s32[8]{0:T(128)S(1)} %stack.27.who, f32[512,256]{1,0:T(8,128)S(1)} %copy-done.3, f32[512,256]{1,0:T(8,128)S(1)} %collective-permute-done.2.w_there, f32[512,256]{1,0:T(8,128)S(1)} %get-tuple-element.53.grad_here, f32[512,256]{1,0:T(8,128)S(1)} %get-tuple-element.46.grad_there), custom_call_target="tpu_custom_call" | custom-call | flops 402653184 | bytes 2097152 | tf_op jit(solution)/shard_map/keep/pallas_call | solution.py:39
  66.0 3.9 %back_here.1 = (f32[1024,256]{1,0:T(8,128)S(1)}, f32[1024,256]{1,0:T(8,128)S(1)}, f32[1024,256]{1,0:T(8,128)S(1)}, f32[1024,256]{1,0:T(8,128)S(1)}) custom-call(s32[8]{0:T(128)S(1)} %stack.27.who, bf16[2,4,1024,1024]{3,2,1,0:T(8,128)(2,1)S(1)} %get-tuple-element.50.matrix, f32[512,256]{1,0:T(8,128)S(1)} %keep.1.source), custom_call_target="tpu_custom_call" | custom-call | flops 3221225472 | bytes 17301504 | tf_op jit(solution)/shard_map/back_here/pallas_call | solution.py:39
  69.9 0.3 collective-permute-done.8.source
  70.3 1.5 %back_two.1 = f32[1024,256]{1,0:T(8,128)S(1)} custom-call(s32[8]{0:T(128)S(1)} %stack.27.who, bf16[2,4,1024,1024]{3,2,1,0:T(8,128)(2,1)S(1)} %get-tuple-element.50.matrix, f32[512,256]{1,0:T(8,128)S(1)} %collective-permute-done.8.source, f32[1024,256]{1,0:T(8,128)S(1)} %get-tuple-element.55.refs_0_), custom_call_target="tpu_custom_call" | custom-call | flops 805306368 | bytes 18350080 | tf_op jit(solution)/shard_map/back_two/pallas_call | solution.py:39
  71.8 1.5 %back_far.1 = f32[1024,256]{1,0:T(8,128)S(1)} custom-call(s32[8]{0:T(128)S(1)} %stack.27.who, bf16[2,4,1024,1024]{3,2,1,0:T(8,128)(2,1)S(1)} %get-tuple-element.50.matrix, f32[512,256]{1,0:T(8,128)S(1)} %collective-permute-done.8.source, f32[1024,256]{1,0:T(8,128)S(1)} %get-tuple-element.58.refs_0_), custom_call_target="tpu_custom_call" | custom-call | flops 805306368 | bytes 18350080 | tf_op jit(solution)/shard_map/back_far/pallas_call | solution.py:39
  73.4 0.6 chip_there.1
  73.9 0.1 collective-permute-start.10
  74.0 3.7 %collective-permute-start.13 = (f32[1024,256]{1,0:T(8,128)S(1)}, f32[1024,256]{1,0:T(8,128)S(1)}, u32[]{:S(2)}, u32[]{:S(2)}) collective-permute-start(f32[1024,256]{1,0:T(8,128)S(1)} %back_far.1), channel_id=1, source_target_pairs={{0,26},{2,0},{4,30},{6,4},{8,2},{10,8},{12,6},{14,12},{16,10},{18,... | collective-permute-start | bytes 3145736 | tf_op jit(solution)/shard_map/ppermute | solution.py:307
  77.7 3.7 %collective-permute-start.11 = (f32[256,256]{1,0:T(8,128)S(1)}, f32[256,256]{1,0:T(8,128)S(1)}, u32[]{:S(2)}, u32[]{:S(2)}) collective-permute-start(f32[256,256]{1,0:T(8,128)S(1)} %get-tuple-element.63.one), channel_id=1, source_target_pairs={{0,4},{2,6},{8,12},{10,14},{16,20},{18,22},{24,28},{26,30},{1,5},{... | collective-permute-start | bytes 786440 | tf_op jit(solution)/shard_map/ppermute | solution.py:313
  81.4 1.8 %collective-permute-start.12 = (f32[256,256]{1,0:T(8,128)S(1)}, f32[256,256]{1,0:T(8,128)S(1)}, u32[]{:S(2)}, u32[]{:S(2)}) collective-permute-start(f32[256,256]{1,0:T(8,128)S(1)} %chip_there.1), channel_id=1, source_target_pairs={{0,1},{1,0},{2,3},{3,2},{4,5},{5,4},{6,7},{7,6},{8,9},{9,8},{10,11... | collective-permute-start | bytes 786440 | tf_op jit(solution)/shard_map/ppermute | solution.py:313
  83.2 1.5 %back_near.1 = f32[1024,256]{1,0:T(8,128)S(1)} custom-call(s32[8]{0:T(128)S(1)} %stack.27.who, bf16[2,4,1024,1024]{3,2,1,0:T(8,128)(2,1)S(1)} %get-tuple-element.50.matrix, f32[512,256]{1,0:T(8,128)S(1)} %collective-permute-done.8.source, f32[1024,256]{1,0:T(8,128)S(1)} %get-tuple-element.61.refs_0_, f32[1024,256]{1,0:T(8,128)S(1)} %collective-permute-done.10.refs_1_), custom_call_target="tpu_custom_call" | custom-call | flops 805306368 | bytes 19398656 | tf_op jit(solution)/shard_map/back_near/pallas_call | solution.py:39
  84.7 0.1 collective-permute-start.20
  84.8 0.7 collective-permute-done.11.two
  85.5 2.3 %collective-permute-done.12.three = f32[256,256]{1,0:T(8,128)S(1)} collective-permute-done((f32[256,256]{1,0:T(8,128)S(1)}, f32[256,256]{1,0:T(8,128)S(1)}, u32[]{:S(2)}, u32[]{:S(2)}) %collective-permute-start.12) | collective-permute-done | bytes 262176 | tf_op jit(solution)/shard_map/ppermute | solution.py:313
  87.8 0.6 side_sum.1
  88.4 1.8 %collective-permute-start.16 = (f32[512,256]{1,0:T(8,128)S(1)}, f32[512,256]{1,0:T(8,128)S(1)}, u32[]{:S(2)}, u32[]{:S(2)}) collective-permute-start(f32[512,256]{1,0:T(8,128)S(1)} %get-tuple-element.73), channel_id=1, source_target_pairs={{0,1},{1,0},{2,3},{3,2},{4,5},{5,4},{6,7},{7,6},{8,9},{9,8},{10,11... | collective-permute-start | bytes 1572872 | tf_op jit(solution)/shard_map/ppermute | solution.py:313
  90.2 0.7 collective-permute-start.14
  90.9 1.5 %back_own.1.refs_0_ = f32[1024,256]{1,0:T(8,128)S(1)} custom-call(s32[8]{0:T(128)S(1)} %stack.27.who, bf16[2,4,1024,1024]{3,2,1,0:T(8,128)(2,1)S(1)} %get-tuple-element.50.matrix, f32[512,256]{1,0:T(8,128)S(1)} %collective-permute-done.8.source, f32[1024,256]{1,0:T(8,128)S(1)} %get-tuple-element.67.refs_0_), custom_call_target="tpu_custom_call" | custom-call | flops 805306368 | bytes 18350080 | tf_op jit(solution)/shard_map/back_own/pallas_call | solution.py:39
  92.4 1.7 %collective-permute-done.13.refs_1_ = f32[1024,256]{1,0:T(8,128)S(1)} collective-permute-done((f32[1024,256]{1,0:T(8,128)S(1)}, f32[1024,256]{1,0:T(8,128)S(1)}, u32[]{:S(2)}, u32[]{:S(2)}) %collective-permute-start.13) | collective-permute-done | bytes 1048608 | tf_op jit(solution)/shard_map/ppermute | solution.py:307
  94.1 0.6 layer_sum.1.refs_0_
  94.7 0.7 collective-permute-start.15
  95.4 0.6 pair_sum.1.ready
  95.9 1.3 %collective-permute-start.19 = (f32[128,256]{1,0:T(8,128)S(1)}, f32[128,256]{1,0:T(8,128)S(1)}, u32[]{:S(2)}, u32[]{:S(2)}) collective-permute-start(f32[128,256]{1,0:T(8,128)S(1)} %pair_sum.1.ready), channel_id=1, source_target_pairs={{4,8},{6,10},{12,0},{14,2},{20,24},{22,26},{28,16},{30,18},{5,9},{... | collective-permute-start | bytes 393224 | tf_op jit(solution)/shard_map/ppermute | solution.py:313
  97.2 1.3 %collective-permute-start.18 = (f32[128,256]{1,0:T(8,128)S(1)}, f32[128,256]{1,0:T(8,128)S(1)}, u32[]{:S(2)}, u32[]{:S(2)}) collective-permute-start(f32[128,256]{1,0:T(8,128)S(1)} %pair_sum.1.ready), channel_id=1, source_target_pairs={{4,0},{6,2},{12,8},{14,10},{20,16},{22,18},{28,24},{30,26},{5,1},{... | collective-permute-start | bytes 393224 | tf_op jit(solution)/shard_map/ppermute | solution.py:313
  98.5 0.7 collective-permute-start.17
  99.2 0.8 collective-permute-done.16.refs_1_
  100.0 1.6 %activated.1 = f32[1024,256]{1,0:T(8,128)} custom-call(s32[8]{0:T(128)S(1)} %stack.27.who, f32[512,256]{1,0:T(8,128)S(1)} %get-tuple-element.71.refs_0_, f32[512,256]{1,0:T(8,128)S(1)} %collective-permute-done.16.refs_1_), custom_call_target="tpu_custom_call" | custom-call | bytes 1048576 | tf_op jit(solution)/shard_map/activated/pallas_call | solution.py:39
  101.6 13.3 %collective-permute-done.19.later_sent = f32[128,256]{1,0:T(8,128)S(1)} collective-permute-done((f32[128,256]{1,0:T(8,128)S(1)}, f32[128,256]{1,0:T(8,128)S(1)}, u32[]{:S(2)}, u32[]{:S(2)}) %collective-permute-start.19) | collective-permute-done | bytes 131104 | tf_op jit(solution)/shard_map/ppermute | solution.py:313
  114.9 0.1 collective-permute-done.18.ready_sent
  115.0 0.6 chip_pick.1.refs_0_
  115.6 0.1 collective-permute-start.21
  115.6 1.7 %feature_grad.1 = f32[1024,256]{1,0:T(8,128)} custom-call(s32[8]{0:T(128)S(1)} %stack.27.who, f32[1024,256]{1,0:T(8,128)S(1)} %back_own.1.refs_0_, f32[1024,256]{1,0:T(8,128)S(1)} %collective-permute-done.13.refs_1_, f32[1024,256]{1,0:T(8,128)S(1)} %collective-permute-done.20.refs_2_), custom_call_target="tpu_custom_call" | custom-call | bytes 3145728 | tf_op jit(solution)/shard_map/feature_grad/pallas_call | solution.py:39
  117.3 1.4 %weight_grad.1 = f32[512,256]{1,0:T(8,128)} custom-call(s32[8]{0:T(128)S(1)} %stack.27.who, f32[256,256]{1,0:T(8,128)S(1)} %chip_pick.1.refs_0_, f32[256,256]{1,0:T(8,128)S(1)} %collective-permute-done.21.refs_1_), custom_call_target="tpu_custom_call" | custom-call | bytes 524288 | tf_op jit(solution)/shard_map/weight_grad/pallas_call | solution.py:39
  (21 shorter events, 0.1 us)
Async XLA Ops:
  0.6 30.1 %collective-permute-start.1 = (f32[1024,256]{1,0:T(8,128)}, f32[1024,256]{1,0:T(8,128)S(1)}, u32[]{:S(2)}, u32[]{:S(2)}) collective-permute-start(f32[1024,256]{1,0:T(8,128)} %refs_0_.1), channel_id=1, source_target_pairs={{0,6},{2,4},{4,10},{6,8},{8,14},{10,12},{12,18},{14,16},{16,22},{1... | collective-permute-start | bytes 3145736 | tf_op jit(solution)/shard_map/ppermute | solution.py:307
  3.1 1.2 %copy-start = (f32[1024,256]{1,0:T(8,128)S(1)}, f32[1024,256]{1,0:T(8,128)}, u32[]{:S(2)}) copy-start(f32[1024,256]{1,0:T(8,128)} %cot.1) | copy-start | bytes 3145732
  5.0 15.2 %collective-permute-start.3 = (f32[512,256]{1,0:T(8,128)S(1)}, f32[512,256]{1,0:T(8,128)S(1)}, u32[]{:S(2)}, u32[]{:S(2)}) collective-permute-start(f32[512,256]{1,0:T(8,128)S(1)} %cot_give.1), channel_id=1, source_target_pairs={{0,1},{1,0},{2,3},{3,2},{4,5},{5,4},{6,7},{7,6},{8,9},{9,8},{10,11... | collective-permute-start | bytes 1572872 | tf_op jit(solution)/shard_map/ppermute | solution.py:313
  6.5 24.2 %collective-permute-start.2 = (f32[512,256]{1,0:T(8,128)}, f32[512,256]{1,0:T(8,128)S(1)}, u32[]{:S(2)}, u32[]{:S(2)}) collective-permute-start(f32[512,256]{1,0:T(8,128)} %w_here.3), channel_id=1, source_target_pairs={{0,1},{1,0},{2,3},{3,2},{4,5},{5,4},{6,7},{7,6},{8,9},{9,8},{10,11... | collective-permute-start | bytes 1572872 | tf_op jit(solution)/shard_map/ppermute | solution.py:313
  7.1 29.4 %collective-permute-start = (f32[1024,256]{1,0:T(8,128)}, f32[1024,256]{1,0:T(8,128)S(1)}, u32[]{:S(2)}, u32[]{:S(2)}) collective-permute-start(f32[1024,256]{1,0:T(8,128)} %refs_0_.1), channel_id=1, source_target_pairs={{0,2},{2,8},{4,6},{6,12},{8,10},{10,16},{12,14},{14,20},{16,18},{1... | collective-permute-start | bytes 3145736 | tf_op jit(solution)/shard_map/ppermute | solution.py:307
  7.2 0.7 copy-start.4
  7.9 0.7 copy-start.5
  8.6 0.7 copy-start.6
  15.8 1.2 %copy-start.2 = (f32[1024,256]{1,0:T(8,128)S(1)}, f32[1024,256]{1,0:T(8,128)}, u32[]{:S(2)}) copy-start(f32[1024,256]{1,0:T(8,128)} %refs_0_.1) | copy-start | bytes 3145732
  30.8 3.6 %collective-permute-start.5 = (f32[512,256]{1,0:T(8,128)S(1)}, f32[512,256]{1,0:T(8,128)S(1)}, u32[]{:S(2)}, u32[]{:S(2)}) collective-permute-start(f32[512,256]{1,0:T(8,128)S(1)} %get-tuple-element.77), channel_id=1, source_target_pairs={{0,2},{2,0},{4,6},{6,4},{8,10},{10,8},{12,14},{14,12},{16,18},{18,... | collective-permute-start | bytes 1572872 | tf_op jit(solution)/shard_map/ppermute | solution.py:313
  30.9 3.5 %collective-permute-start.4 = (f32[512,256]{1,0:T(8,128)S(1)}, f32[512,256]{1,0:T(8,128)S(1)}, u32[]{:S(2)}, u32[]{:S(2)}) collective-permute-start(f32[512,256]{1,0:T(8,128)S(1)} %get-tuple-element.78), channel_id=1, source_target_pairs={{0,2},{2,0},{4,6},{6,4},{8,10},{10,8},{12,14},{14,12},{16,18},{18,... | collective-permute-start | bytes 1572872 | tf_op jit(solution)/shard_map/ppermute | solution.py:313
  36.4 15.9 %copy-start.1 = (f32[1024,256]{1,0:T(8,128)S(1)}, f32[1024,256]{1,0:T(8,128)}, u32[]{:S(2)}) copy-start(f32[1024,256]{1,0:T(8,128)} %cot.1) | copy-start | bytes 3145732
  36.4 15.9 %copy-start.3 = (f32[512,256]{1,0:T(8,128)S(1)}, f32[512,256]{1,0:T(8,128)}, u32[]{:S(2)}) copy-start(f32[512,256]{1,0:T(8,128)} %w_here.3) | copy-start | bytes 1572868
  38.3 14.0 %collective-permute-start.6 = (f32[512,256]{1,0:T(8,128)S(1)}, f32[512,256]{1,0:T(8,128)S(1)}, u32[]{:S(2)}, u32[]{:S(2)}) collective-permute-start(f32[512,256]{1,0:T(8,128)S(1)} %agg_give.1), channel_id=1, source_target_pairs={{0,1},{1,0},{2,3},{3,2},{4,5},{5,4},{6,7},{7,6},{8,9},{9,8},{10,11... | collective-permute-start | bytes 1572872 | tf_op jit(solution)/shard_map/ppermute | solution.py:313
  55.8 2.9 %collective-permute-start.7 = (f32[256,512]{1,0:T(8,128)S(1)}, f32[256,512]{1,0:T(8,128)S(1)}, u32[]{:S(2)}, u32[]{:S(2)}) collective-permute-start(f32[256,512]{1,0:T(8,128)S(1)} %weight_give.1), channel_id=1, source_target_pairs={{0,2},{2,0},{4,6},{6,4},{8,10},{10,8},{12,14},{14,12},{16,18},{18,... | collective-permute-start | bytes 1572872 | tf_op jit(solution)/shard_map/ppermute | solution.py:313
  55.9 14.3 %collective-permute-start.8 = (f32[512,256]{1,0:T(8,128)S(1)}, f32[512,256]{1,0:T(8,128)S(1)}, u32[]{:S(2)}, u32[]{:S(2)}) collective-permute-start(f32[512,256]{1,0:T(8,128)S(1)} %get-tuple-element.51), channel_id=1, source_target_pairs={{0,1},{1,0},{2,3},{3,2},{4,5},{5,4},{6,7},{7,6},{8,9},{9,8},{10,11... | collective-permute-start | bytes 1572872 | tf_op jit(solution)/shard_map/ppermute | solution.py:313
  59.4 14.0 %collective-permute-start.9 = (f32[256,256]{1,0:T(8,128)S(1)}, f32[256,256]{1,0:T(8,128)S(1)}, u32[]{:S(2)}, u32[]{:S(2)}) collective-permute-start(f32[256,256]{1,0:T(8,128)S(1)} %get-tuple-element.59.refs_0_), channel_id=1, source_target_pairs={{0,4},{2,6},{8,12},{10,14},{16,20},{18,22},{24,28},{26,30},{1,5},{... | collective-permute-start | bytes 786440 | tf_op jit(solution)/shard_map/ppermute | solution.py:313
  73.9 9.2 %collective-permute-start.10 = (f32[1024,256]{1,0:T(8,128)S(1)}, f32[1024,256]{1,0:T(8,128)S(1)}, u32[]{:S(2)}, u32[]{:S(2)}) collective-permute-start(f32[1024,256]{1,0:T(8,128)S(1)} %back_two.1), channel_id=1, source_target_pairs={{0,2},{2,0},{4,6},{6,4},{8,10},{10,8},{12,14},{14,12},{16,18},{18,... | collective-permute-start | bytes 3145736 | tf_op jit(solution)/shard_map/ppermute | solution.py:313
  74.0 20.1 %collective-permute-start.13 = (f32[1024,256]{1,0:T(8,128)S(1)}, f32[1024,256]{1,0:T(8,128)S(1)}, u32[]{:S(2)}, u32[]{:S(2)}) collective-permute-start(f32[1024,256]{1,0:T(8,128)S(1)} %back_far.1), channel_id=1, source_target_pairs={{0,26},{2,0},{4,30},{6,4},{8,2},{10,8},{12,6},{14,12},{16,10},{18,... | collective-permute-start | bytes 3145736 | tf_op jit(solution)/shard_map/ppermute | solution.py:307
  77.7 7.8 %collective-permute-start.11 = (f32[256,256]{1,0:T(8,128)S(1)}, f32[256,256]{1,0:T(8,128)S(1)}, u32[]{:S(2)}, u32[]{:S(2)}) collective-permute-start(f32[256,256]{1,0:T(8,128)S(1)} %get-tuple-element.63.one), channel_id=1, source_target_pairs={{0,4},{2,6},{8,12},{10,14},{16,20},{18,22},{24,28},{26,30},{1,5},{... | collective-permute-start | bytes 786440 | tf_op jit(solution)/shard_map/ppermute | solution.py:313
  81.4 6.4 %collective-permute-start.12 = (f32[256,256]{1,0:T(8,128)S(1)}, f32[256,256]{1,0:T(8,128)S(1)}, u32[]{:S(2)}, u32[]{:S(2)}) collective-permute-start(f32[256,256]{1,0:T(8,128)S(1)} %chip_there.1), channel_id=1, source_target_pairs={{0,1},{1,0},{2,3},{3,2},{4,5},{5,4},{6,7},{7,6},{8,9},{9,8},{10,11... | collective-permute-start | bytes 786440 | tf_op jit(solution)/shard_map/ppermute | solution.py:313
  84.7 30.9 %collective-permute-start.20 = (f32[1024,256]{1,0:T(8,128)S(1)}, f32[1024,256]{1,0:T(8,128)S(1)}, u32[]{:S(2)}, u32[]{:S(2)}) collective-permute-start(f32[1024,256]{1,0:T(8,128)S(1)} %back_near.1), channel_id=1, source_target_pairs={{0,30},{2,28},{4,2},{6,0},{8,6},{10,4},{12,10},{14,8},{16,14},{18,... | collective-permute-start | bytes 3145736 | tf_op jit(solution)/shard_map/ppermute | solution.py:307
  88.4 11.6 %collective-permute-start.16 = (f32[512,256]{1,0:T(8,128)S(1)}, f32[512,256]{1,0:T(8,128)S(1)}, u32[]{:S(2)}, u32[]{:S(2)}) collective-permute-start(f32[512,256]{1,0:T(8,128)S(1)} %get-tuple-element.73), channel_id=1, source_target_pairs={{0,1},{1,0},{2,3},{3,2},{4,5},{5,4},{6,7},{7,6},{8,9},{9,8},{10,11... | collective-permute-start | bytes 1572872 | tf_op jit(solution)/shard_map/ppermute | solution.py:313
  90.2 3.9 %collective-permute-start.14 = (f32[128,256]{1,0:T(8,128)S(1)}, f32[128,256]{1,0:T(8,128)S(1)}, u32[]{:S(2)}, u32[]{:S(2)}) collective-permute-start(f32[128,256]{1,0:T(8,128)S(1)} %get-tuple-element.65), channel_id=1, source_target_pairs={{4,12},{6,14},{12,4},{14,6},{20,28},{22,30},{28,20},{30,22},{5,13}... | collective-permute-start | bytes 393224 | tf_op jit(solution)/shard_map/ppermute | solution.py:313
  94.7 0.7 collective-permute-start.15
  95.9 18.9 %collective-permute-start.19 = (f32[128,256]{1,0:T(8,128)S(1)}, f32[128,256]{1,0:T(8,128)S(1)}, u32[]{:S(2)}, u32[]{:S(2)}) collective-permute-start(f32[128,256]{1,0:T(8,128)S(1)} %pair_sum.1.ready), channel_id=1, source_target_pairs={{4,8},{6,10},{12,0},{14,2},{20,24},{22,26},{28,16},{30,18},{5,9},{... | collective-permute-start | bytes 393224 | tf_op jit(solution)/shard_map/ppermute | solution.py:313
  97.2 17.7 %collective-permute-start.18 = (f32[128,256]{1,0:T(8,128)S(1)}, f32[128,256]{1,0:T(8,128)S(1)}, u32[]{:S(2)}, u32[]{:S(2)}) collective-permute-start(f32[128,256]{1,0:T(8,128)S(1)} %pair_sum.1.ready), channel_id=1, source_target_pairs={{4,0},{6,2},{12,8},{14,10},{20,16},{22,18},{28,24},{30,26},{5,1},{... | collective-permute-start | bytes 393224 | tf_op jit(solution)/shard_map/ppermute | solution.py:313
  98.5 16.5 %collective-permute-start.17 = (f32[128,256]{1,0:T(8,128)S(1)}, f32[128,256]{1,0:T(8,128)S(1)}, u32[]{:S(2)}, u32[]{:S(2)}) collective-permute-start(f32[128,256]{1,0:T(8,128)S(1)} %pair_sum.1.ready), channel_id=1, source_target_pairs={{4,12},{6,14},{12,4},{14,6},{20,28},{22,30},{28,20},{30,22},{5,13}... | collective-permute-start | bytes 393224 | tf_op jit(solution)/shard_map/ppermute | solution.py:313
  115.6 1.8 %collective-permute-start.21 = (f32[256,256]{1,0:T(8,128)S(1)}, f32[256,256]{1,0:T(8,128)S(1)}, u32[]{:S(2)}, u32[]{:S(2)}) collective-permute-start(f32[256,256]{1,0:T(8,128)S(1)} %chip_pick.1.refs_0_), channel_id=1, source_target_pairs={{0,2},{2,0},{4,6},{6,4},{8,10},{10,8},{12,14},{14,12},{16,18},{18,... | collective-permute-start | bytes 786440 | tf_op jit(solution)/shard_map/ppermute | solution.py:313

commit v6 on v5

--- a/solution.py
+++ b/solution.py
@@ -376,11 +376,11 @@
     )[0]
     firsts = backward("back_here", who, t, [TWO, FAR, NEAR, OWN], after(g_here, last), [], 0)
     g_there = after(g_there, firsts[0])
-    two_out = backward("back_two", who, t, [TWO], g_there, [firsts[0]], 1)[0]
-    far_out = backward("back_far", who, t, [FAR], after(g_there, two_out), [firsts[1]], 1)[0]
-    last = next(steps)(far_out)
+    far_out = backward("back_far", who, t, [FAR], g_there, [firsts[1]], 1)[0]
+    two_out = backward("back_two", who, t, [TWO], after(g_there, far_out), [firsts[0]], 1)[0]
+    last = next(steps)(two_out)
+    far = moved(after(far_out, last), "dom", -3, -1)
     two = swapped(after(two_out, last), "dom")
-    far = moved(after(far_out, last), "dom", -3, -1)
     last = backward("back_near", who, t, [NEAR], after(g_there, last), [firsts[2], two], 1)[0]
     near = moved(last, "dom", -1, -3)
     last = next(steps)(last)

time: 120 us -> 120 us (level)
  Pallas kernels: 44.1 us -> 46 us
  waiting for transfers between devices: 39.4 us -> 37.5 us
    ppermute x18, waiting for transfers between devices: 37.7 us -> 35.8 us  [chosen(): lax.ppermute(value, axis, [pair for pair in pairs if pair[1] is not None])]
    pallas_call x1, Pallas kernels: 6.62 us -> 8.51 us  [lay_out(): pl.pallas_call(lay_out_kernel, grid_spec=pltpu.PrefetchScalarGridSpec(num...]
  transfers between devices with their start and end apart: 22 -> 22, of which waited for: 9 -> 9; matrix products, arithmetic and copies ran while one was open for 0% -> 0% of each run, Pallas kernels for 31% -> 33%
where the time goes in v6:
time: 120 us; the launch traced here: 119 us
  Pallas kernels  46 us (38%)
  waiting for transfers between devices  37.5 us (31%)
  starting transfers between devices  29.6 us (25%)
  local copies, waits for them, and re-layouts  4.63 us (4%)
    pallas_call x24, Pallas kernels, call(): pl.pallas_call(kernel, in_specs=[IN_SMEM] + [IN_VMEM] * len(operands), ou...  37.4 us
    ppermute x18, waiting for transfers between devices, chosen(): lax.ppermute(value, axis, [pair for pair in pairs if pair[1] is not None])  35.8 us
    ppermute x18, starting transfers between devices, chosen(): lax.ppermute(value, axis, [pair for pair in pairs if pair[1] is not None])  23.3 us
    pallas_call x1, Pallas kernels, lay_out(): pl.pallas_call(lay_out_kernel, grid_spec=pltpu.PrefetchScalarGridSpec(num...  8.51 us
    ppermute x4, starting transfers between devices, moved(): return lax.ppermute(value, axis, perm)  6.33 us
    unnamed x14, local copies, waits for them, and re-layouts  4.48 us
  transfers between devices with their start and end apart: 22, of which 9 were waited for; matrix products, arithmetic and copies ran while one was open for 0% of the time, Pallas kernels for 33%

profile of v6, /device:TPU:0, one launch (start us, length us, event | category | flops | bytes accessed | tf_op | source)
XLA Modules:
  0.0 118.7 jit_solution(15441698540430576135)
XLA Ops:
  0.6 2.4 %collective-permute-start.1 = (f32[1024,256]{1,0:T(8,128)}, f32[1024,256]{1,0:T(8,128)S(1)}, u32[]{:S(2)}, u32[]{:S(2)}) collective-permute-start(f32[1024,256]{1,0:T(8,128)} %refs_0_.1), channel_id=1, source_target_pairs={{0,6},{2,4},{4,10},{6,8},{8,14},{10,12},{12,18},{14,16},{16,22},{1... | collective-permute-start | bytes 3145736 | tf_op jit(solution)/shard_map/ppermute | solution.py:307
  3.1 0.1 stack.27.who
  3.1 1.2 %copy-done = f32[1024,256]{1,0:T(8,128)S(1)} copy-done((f32[1024,256]{1,0:T(8,128)S(1)}, f32[1024,256]{1,0:T(8,128)}, u32[]{:S(2)}) %copy-start) | copy-done | bytes 1048600
  4.4 0.6 cot_give.1
  5.0 1.6 %collective-permute-start.3 = (f32[512,256]{1,0:T(8,128)S(1)}, f32[512,256]{1,0:T(8,128)S(1)}, u32[]{:S(2)}, u32[]{:S(2)}) collective-permute-start(f32[512,256]{1,0:T(8,128)S(1)} %cot_give.1), channel_id=1, source_target_pairs={{0,1},{1,0},{2,3},{3,2},{4,5},{5,4},{6,7},{7,6},{8,9},{9,8},{10,11... | collective-permute-start | bytes 1572872 | tf_op jit(solution)/shard_map/ppermute | solution.py:313
  6.5 0.5 collective-permute-start.2
  7.1 0.1 collective-permute-start
  7.2 0.7 copy-done.4
  7.9 0.7 copy-done.5
  8.6 0.7 copy-done.6
  9.2 8.5 %lay_out.1 = (bf16[2,4,1024,1024]{3,2,1,0:T(8,128)(2,1)S(1)}, bf16[2,4,1024,1024]{3,2,1,0:T(8,128)(2,1)S(1)}) custom-call(s32[4,24]{1,0:T(4,128)S(1)} %bitcast.9, s32[4,24]{1,0:T(4,128)S(1)} %bitcast.10, s32[1,4]{1,0:T(1,128)S(1)} %copy-done.6, s32[8]{0:T(128)S(1)} %stack.27.who, f32[4,24,128,128]{3,2,1,0:T(8,128)} %bitcast.11), custom_call_target="tpu_custom_call" | custom-call | bytes 20000000 | tf_op jit(solution)/shard_map/lay_out/pallas_call | solution.py:75
  17.7 0.0 copy-start.2
  17.7 1.2 %copy-done.2 = f32[1024,256]{1,0:T(8,128)S(1)} copy-done((f32[1024,256]{1,0:T(8,128)S(1)}, f32[1024,256]{1,0:T(8,128)}, u32[]{:S(2)}) %copy-start.2) | copy-done | bytes 1048600
  19.0 3.0 %agg_own.1.refs_1_ = f32[1024,256]{1,0:T(8,128)S(1)} custom-call(s32[8]{0:T(128)S(1)} %stack.27.who, bf16[2,4,1024,1024]{3,2,1,0:T(8,128)(2,1)S(1)} %get-tuple-element.40.matrix, f32[1024,256]{1,0:T(8,128)S(1)} %copy-done.2), custom_call_target="tpu_custom_call" | custom-call | flops 1610612736 | bytes 17825792 | tf_op jit(solution)/shard_map/agg_own/pallas_call | solution.py:39
  22.0 8.7 %collective-permute-done.2.w_there = f32[512,256]{1,0:T(8,128)S(1)} collective-permute-done((f32[512,256]{1,0:T(8,128)}, f32[512,256]{1,0:T(8,128)S(1)}, u32[]{:S(2)}, u32[]{:S(2)}) %collective-permute-start.2) | collective-permute-done | bytes 524320 | tf_op jit(solution)/shard_map/ppermute | solution.py:313
  30.8 0.1 fusion
  30.8 0.1 collective-permute-start.5
  30.9 0.5 collective-permute-start.4
  31.4 3.0 %agg_near.1.refs_2_.refs_3_ = f32[1024,256]{1,0:T(8,128)S(1)} custom-call(s32[8]{0:T(128)S(1)} %stack.27.who, bf16[2,4,1024,1024]{3,2,1,0:T(8,128)(2,1)S(1)} %get-tuple-element.40.matrix, f32[1024,256]{1,0:T(8,128)S(1)} %collective-permute-done.1.refs_0_, f32[1024,256]{1,0:T(8,128)S(1)} %agg_own.1.refs_1_), custom_call_target="tpu_custom_call" | custom-call | flops 1610612736 | bytes 18874368 | tf_op jit(solution)/shard_map/agg_near/pallas_call | solution.py:39
  34.5 1.9 %agg_two.1.refs_1_ = f32[512,256]{1,0:T(8,128)S(1)} custom-call(s32[8]{0:T(128)S(1)} %stack.27.who, bf16[2,4,1024,1024]{3,2,1,0:T(8,128)(2,1)S(1)} %get-tuple-element.40.matrix, f32[512,256]{1,0:T(8,128)S(1)} %collective-permute-done.4.refs_0_.refs_1_, f32[512,256]{1,0:T(8,128)S(1)} %collective-permute-done.5.refs_1_.refs_2_, ...), custom_call_target="tpu_custom_call" | custom-call | flops 805306368 | bytes 18874368 | tf_op jit(solution)/shard_map/agg_two/pallas_call | solution.py:39
  36.4 1.9 %agg_give.1 = f32[512,256]{1,0:T(8,128)S(1)} custom-call(s32[8]{0:T(128)S(1)} %stack.27.who, bf16[2,4,1024,1024]{3,2,1,0:T(8,128)(2,1)S(1)} %get-tuple-element.40.matrix, f32[1024,256]{1,0:T(8,128)S(1)} %collective-permute-done.refs_0_, f32[512,256]{1,0:T(8,128)S(1)} %agg_two.1.refs_1_), custom_call_target="tpu_custom_call" | custom-call | flops 805306368 | bytes 18350080 | tf_op jit(solution)/shard_map/agg_give/pallas_call | solution.py:39
  38.3 1.6 %collective-permute-start.6 = (f32[512,256]{1,0:T(8,128)S(1)}, f32[512,256]{1,0:T(8,128)S(1)}, u32[]{:S(2)}, u32[]{:S(2)}) collective-permute-start(f32[512,256]{1,0:T(8,128)S(1)} %agg_give.1), channel_id=1, source_target_pairs={{0,1},{1,0},{2,3},{3,2},{4,5},{5,4},{6,7},{7,6},{8,9},{9,8},{10,11... | collective-permute-start | bytes 1572872 | tf_op jit(solution)/shard_map/ppermute | solution.py:313
  39.9 2.9 %agg_keep.1.own = f32[512,256]{1,0:T(8,128)S(1)} custom-call(s32[8]{0:T(128)S(1)} %stack.27.who, bf16[2,4,1024,1024]{3,2,1,0:T(8,128)(2,1)S(1)} %get-tuple-element.40.matrix, f32[1024,256]{1,0:T(8,128)S(1)} %collective-permute-done.refs_0_, f32[512,256]{1,0:T(8,128)S(1)} %collective-permute-done.4.refs_0_.refs_1_, ...), custom_call_target="tpu_custom_call" | custom-call | flops 1610612736 | bytes 19922944 | tf_op jit(solution)/shard_map/agg_keep/pallas_call | solution.py:39
  42.8 9.5 %collective-permute-done.6.far = f32[512,256]{1,0:T(8,128)S(1)} collective-permute-done((f32[512,256]{1,0:T(8,128)S(1)}, f32[512,256]{1,0:T(8,128)S(1)}, u32[]{:S(2)}, u32[]{:S(2)}) %collective-permute-start.6) | collective-permute-done | bytes 524320 | tf_op jit(solution)/shard_map/ppermute | solution.py:313
  52.3 2.3 %middle.1 = (f32[512,256]{1,0:T(8,128)S(1)}, f32[512,256]{1,0:T(8,128)S(1)}, f32[512,256]{1,0:T(8,128)S(1)}, f32[512,256]{1,0:T(8,128)S(1)}, f32[512,256]{1,0:T(8,128)S(1)}) custom-call(s32[8]{0:T(128)S(1)} %stack.27.who, f32[512,256]{1,0:T(8,128)S(1)} %agg_keep.1.own, f32[512,256]{1,0:T(8,128)S(1)} %collective-permute-done.6.far, f32[512,256]{1,0:T(8,128)S(1)} %copy-done.3, ...), custom_call_target="tpu_custom_call" | custom-call | flops 1207959552 | bytes 3670016 | tf_op jit(solution)/shard_map/middle/pallas_call | solution.py:39
  54.6 1.2 %weight_give.1 = f32[256,512]{1,0:T(8,128)S(1)} custom-call(s32[8]{0:T(128)S(1)} %stack.27.who, f32[512,256]{1,0:T(8,128)S(1)} %agg_keep.1.own, f32[512,256]{1,0:T(8,128)S(1)} %collective-permute-done.6.far, f32[512,256]{1,0:T(8,128)S(1)} %get-tuple-element.53.grad_here, f32[512,256]{1,0:T(8,128)S(1)} %get-tuple-element.46.grad_there), custom_call_target="tpu_custom_call" | custom-call | flops 402653184 | bytes 2097152 | tf_op jit(solution)/shard_map/weight_give/pallas_call | solution.py:39
  55.8 0.1 collective-permute-start.7
  55.9 1.6 %collective-permute-start.8 = (f32[512,256]{1,0:T(8,128)S(1)}, f32[512,256]{1,0:T(8,128)S(1)}, u32[]{:S(2)}, u32[]{:S(2)}) collective-permute-start(f32[512,256]{1,0:T(8,128)S(1)} %get-tuple-element.51), channel_id=1, source_target_pairs={{0,1},{1,0},{2,3},{3,2},{4,5},{5,4},{6,7},{7,6},{8,9},{9,8},{10,11... | collective-permute-start | bytes 1572872 | tf_op jit(solution)/shard_map/ppermute | solution.py:313
  57.5 1.2 %weight_keep.1.one = f32[256,512]{1,0:T(8,128)S(1)} custom-call(s32[8]{0:T(128)S(1)} %stack.27.who, f32[512,256]{1,0:T(8,128)S(1)} %agg_keep.1.own, f32[512,256]{1,0:T(8,128)S(1)} %collective-permute-done.6.far, f32[512,256]{1,0:T(8,128)S(1)} %get-tuple-element.53.grad_here, f32[512,256]{1,0:T(8,128)S(1)} %get-tuple-element.46.grad_there), custom_call_target="tpu_custom_call" | custom-call | flops 402653184 | bytes 2097152 | tf_op jit(solution)/shard_map/weight_keep/pallas_call | solution.py:39
  58.8 0.6 core_sum.1
  59.4 5.4 %collective-permute-start.9 = (f32[256,256]{1,0:T(8,128)S(1)}, f32[256,256]{1,0:T(8,128)S(1)}, u32[]{:S(2)}, u32[]{:S(2)}) collective-permute-start(f32[256,256]{1,0:T(8,128)S(1)} %get-tuple-element.59.refs_0_), channel_id=1, source_target_pairs={{0,4},{2,6},{8,12},{10,14},{16,20},{18,22},{24,28},{26,30},{1,5},{... | collective-permute-start | bytes 786440 | tf_op jit(solution)/shard_map/ppermute | solution.py:313
  64.8 1.2 %keep.1.source = f32[512,256]{1,0:T(8,128)S(1)} custom-call(s32[8]{0:T(128)S(1)} %stack.27.who, f32[512,256]{1,0:T(8,128)S(1)} %copy-done.3, f32[512,256]{1,0:T(8,128)S(1)} %collective-permute-done.2.w_there, f32[512,256]{1,0:T(8,128)S(1)} %get-tuple-element.53.grad_here, f32[512,256]{1,0:T(8,128)S(1)} %get-tuple-element.46.grad_there), custom_call_target="tpu_custom_call" | custom-call | flops 402653184 | bytes 2097152 | tf_op jit(solution)/shard_map/keep/pallas_call | solution.py:39
  66.0 3.9 %back_here.1 = (f32[1024,256]{1,0:T(8,128)S(1)}, f32[1024,256]{1,0:T(8,128)S(1)}, f32[1024,256]{1,0:T(8,128)S(1)}, f32[1024,256]{1,0:T(8,128)S(1)}) custom-call(s32[8]{0:T(128)S(1)} %stack.27.who, bf16[2,4,1024,1024]{3,2,1,0:T(8,128)(2,1)S(1)} %get-tuple-element.50.matrix, f32[512,256]{1,0:T(8,128)S(1)} %keep.1.source), custom_call_target="tpu_custom_call" | custom-call | flops 3221225472 | bytes 17301504 | tf_op jit(solution)/shard_map/back_here/pallas_call | solution.py:39
  69.9 0.3 collective-permute-done.8.source
  70.3 1.5 %back_far.1 = f32[1024,256]{1,0:T(8,128)S(1)} custom-call(s32[8]{0:T(128)S(1)} %stack.27.who, bf16[2,4,1024,1024]{3,2,1,0:T(8,128)(2,1)S(1)} %get-tuple-element.50.matrix, f32[512,256]{1,0:T(8,128)S(1)} %collective-permute-done.8.source, f32[1024,256]{1,0:T(8,128)S(1)} %get-tuple-element.57.refs_0_), custom_call_target="tpu_custom_call" | custom-call | flops 805306368 | bytes 18350080 | tf_op jit(solution)/shard_map/back_far/pallas_call | solution.py:39
  71.8 1.5 %back_two.1 = f32[1024,256]{1,0:T(8,128)S(1)} custom-call(s32[8]{0:T(128)S(1)} %stack.27.who, bf16[2,4,1024,1024]{3,2,1,0:T(8,128)(2,1)S(1)} %get-tuple-element.50.matrix, f32[512,256]{1,0:T(8,128)S(1)} %collective-permute-done.8.source, f32[1024,256]{1,0:T(8,128)S(1)} %get-tuple-element.55.refs_0_), custom_call_target="tpu_custom_call" | custom-call | flops 805306368 | bytes 18350080 | tf_op jit(solution)/shard_map/back_two/pallas_call | solution.py:39
  73.4 0.6 chip_there.1
  73.9 0.1 collective-permute-start.10
  74.0 3.7 %collective-permute-start.13 = (f32[1024,256]{1,0:T(8,128)S(1)}, f32[1024,256]{1,0:T(8,128)S(1)}, u32[]{:S(2)}, u32[]{:S(2)}) collective-permute-start(f32[1024,256]{1,0:T(8,128)S(1)} %back_far.1), channel_id=1, source_target_pairs={{0,26},{2,0},{4,30},{6,4},{8,2},{10,8},{12,6},{14,12},{16,10},{18,... | collective-permute-start | bytes 3145736 | tf_op jit(solution)/shard_map/ppermute | solution.py:307
  77.7 3.7 %collective-permute-start.11 = (f32[256,256]{1,0:T(8,128)S(1)}, f32[256,256]{1,0:T(8,128)S(1)}, u32[]{:S(2)}, u32[]{:S(2)}) collective-permute-start(f32[256,256]{1,0:T(8,128)S(1)} %get-tuple-element.63.one), channel_id=1, source_target_pairs={{0,4},{2,6},{8,12},{10,14},{16,20},{18,22},{24,28},{26,30},{1,5},{... | collective-permute-start | bytes 786440 | tf_op jit(solution)/shard_map/ppermute | solution.py:313
  81.4 1.8 %collective-permute-start.12 = (f32[256,256]{1,0:T(8,128)S(1)}, f32[256,256]{1,0:T(8,128)S(1)}, u32[]{:S(2)}, u32[]{:S(2)}) collective-permute-start(f32[256,256]{1,0:T(8,128)S(1)} %chip_there.1), channel_id=1, source_target_pairs={{0,1},{1,0},{2,3},{3,2},{4,5},{5,4},{6,7},{7,6},{8,9},{9,8},{10,11... | collective-permute-start | bytes 786440 | tf_op jit(solution)/shard_map/ppermute | solution.py:313
  83.2 1.5 %back_near.1 = f32[1024,256]{1,0:T(8,128)S(1)} custom-call(s32[8]{0:T(128)S(1)} %stack.27.who, bf16[2,4,1024,1024]{3,2,1,0:T(8,128)(2,1)S(1)} %get-tuple-element.50.matrix, f32[512,256]{1,0:T(8,128)S(1)} %collective-permute-done.8.source, f32[1024,256]{1,0:T(8,128)S(1)} %get-tuple-element.61.refs_0_, f32[1024,256]{1,0:T(8,128)S(1)} %collective-permute-done.10.refs_1_), custom_call_target="tpu_custom_call" | custom-call | flops 805306368 | bytes 19398656 | tf_op jit(solution)/shard_map/back_near/pallas_call | solution.py:39
  84.7 0.1 collective-permute-start.20
  84.8 0.7 collective-permute-done.11.two
  85.5 2.3 %collective-permute-done.12.three = f32[256,256]{1,0:T(8,128)S(1)} collective-permute-done((f32[256,256]{1,0:T(8,128)S(1)}, f32[256,256]{1,0:T(8,128)S(1)}, u32[]{:S(2)}, u32[]{:S(2)}) %collective-permute-start.12) | collective-permute-done | bytes 262176 | tf_op jit(solution)/shard_map/ppermute | solution.py:313
  87.8 0.6 side_sum.1
  88.4 1.8 %collective-permute-start.16 = (f32[512,256]{1,0:T(8,128)S(1)}, f32[512,256]{1,0:T(8,128)S(1)}, u32[]{:S(2)}, u32[]{:S(2)}) collective-permute-start(f32[512,256]{1,0:T(8,128)S(1)} %get-tuple-element.73), channel_id=1, source_target_pairs={{0,1},{1,0},{2,3},{3,2},{4,5},{5,4},{6,7},{7,6},{8,9},{9,8},{10,11... | collective-permute-start | bytes 1572872 | tf_op jit(solution)/shard_map/ppermute | solution.py:313
  90.2 0.7 collective-permute-start.14
  90.9 1.5 %back_own.1.refs_0_ = f32[1024,256]{1,0:T(8,128)S(1)} custom-call(s32[8]{0:T(128)S(1)} %stack.27.who, bf16[2,4,1024,1024]{3,2,1,0:T(8,128)(2,1)S(1)} %get-tuple-element.50.matrix, f32[512,256]{1,0:T(8,128)S(1)} %collective-permute-done.8.source, f32[1024,256]{1,0:T(8,128)S(1)} %get-tuple-element.67.refs_0_), custom_call_target="tpu_custom_call" | custom-call | flops 805306368 | bytes 18350080 | tf_op jit(solution)/shard_map/back_own/pallas_call | solution.py:39
  92.4 1.7 %collective-permute-done.13.refs_1_ = f32[1024,256]{1,0:T(8,128)S(1)} collective-permute-done((f32[1024,256]{1,0:T(8,128)S(1)}, f32[1024,256]{1,0:T(8,128)S(1)}, u32[]{:S(2)}, u32[]{:S(2)}) %collective-permute-start.13) | collective-permute-done | bytes 1048608 | tf_op jit(solution)/shard_map/ppermute | solution.py:307
  94.1 0.6 layer_sum.1.refs_0_
  94.7 0.7 collective-permute-start.15
  95.4 0.6 pair_sum.1.ready
  95.9 1.3 %collective-permute-start.19 = (f32[128,256]{1,0:T(8,128)S(1)}, f32[128,256]{1,0:T(8,128)S(1)}, u32[]{:S(2)}, u32[]{:S(2)}) collective-permute-start(f32[128,256]{1,0:T(8,128)S(1)} %pair_sum.1.ready), channel_id=1, source_target_pairs={{4,8},{6,10},{12,0},{14,2},{20,24},{22,26},{28,16},{30,18},{5,9},{... | collective-permute-start | bytes 393224 | tf_op jit(solution)/shard_map/ppermute | solution.py:313
  97.2 1.3 %collective-permute-start.18 = (f32[128,256]{1,0:T(8,128)S(1)}, f32[128,256]{1,0:T(8,128)S(1)}, u32[]{:S(2)}, u32[]{:S(2)}) collective-permute-start(f32[128,256]{1,0:T(8,128)S(1)} %pair_sum.1.ready), channel_id=1, source_target_pairs={{4,0},{6,2},{12,8},{14,10},{20,16},{22,18},{28,24},{30,26},{5,1},{... | collective-permute-start | bytes 393224 | tf_op jit(solution)/shard_map/ppermute | solution.py:313
  98.5 0.7 collective-permute-start.17
  99.2 0.8 collective-permute-done.16.refs_1_
  100.0 1.6 %activated.1 = f32[1024,256]{1,0:T(8,128)} custom-call(s32[8]{0:T(128)S(1)} %stack.27.who, f32[512,256]{1,0:T(8,128)S(1)} %get-tuple-element.71.refs_0_, f32[512,256]{1,0:T(8,128)S(1)} %collective-permute-done.16.refs_1_), custom_call_target="tpu_custom_call" | custom-call | bytes 1048576 | tf_op jit(solution)/shard_map/activated/pallas_call | solution.py:39
  101.6 13.3 %collective-permute-done.19.later_sent = f32[128,256]{1,0:T(8,128)S(1)} collective-permute-done((f32[128,256]{1,0:T(8,128)S(1)}, f32[128,256]{1,0:T(8,128)S(1)}, u32[]{:S(2)}, u32[]{:S(2)}) %collective-permute-start.19) | collective-permute-done | bytes 131104 | tf_op jit(solution)/shard_map/ppermute | solution.py:313
  114.9 0.1 collective-permute-done.18.ready_sent
  115.0 0.6 chip_pick.1.refs_0_
  115.6 0.1 collective-permute-start.21
  115.6 1.7 %feature_grad.1 = f32[1024,256]{1,0:T(8,128)} custom-call(s32[8]{0:T(128)S(1)} %stack.27.who, f32[1024,256]{1,0:T(8,128)S(1)} %back_own.1.refs_0_, f32[1024,256]{1,0:T(8,128)S(1)} %collective-permute-done.13.refs_1_, f32[1024,256]{1,0:T(8,128)S(1)} %collective-permute-done.20.refs_2_), custom_call_target="tpu_custom_call" | custom-call | bytes 3145728 | tf_op jit(solution)/shard_map/feature_grad/pallas_call | solution.py:39
  117.3 1.4 %weight_grad.1 = f32[512,256]{1,0:T(8,128)} custom-call(s32[8]{0:T(128)S(1)} %stack.27.who, f32[256,256]{1,0:T(8,128)S(1)} %chip_pick.1.refs_0_, f32[256,256]{1,0:T(8,128)S(1)} %collective-permute-done.21.refs_1_), custom_call_target="tpu_custom_call" | custom-call | bytes 524288 | tf_op jit(solution)/shard_map/weight_grad/pallas_call | solution.py:39
  (21 shorter events, 0.1 us)
Async XLA Ops:
  0.6 30.1 %collective-permute-start.1 = (f32[1024,256]{1,0:T(8,128)}, f32[1024,256]{1,0:T(8,128)S(1)}, u32[]{:S(2)}, u32[]{:S(2)}) collective-permute-start(f32[1024,256]{1,0:T(8,128)} %refs_0_.1), channel_id=1, source_target_pairs={{0,6},{2,4},{4,10},{6,8},{8,14},{10,12},{12,18},{14,16},{16,22},{1... | collective-permute-start | bytes 3145736 | tf_op jit(solution)/shard_map/ppermute | solution.py:307
  3.1 1.2 %copy-start = (f32[1024,256]{1,0:T(8,128)S(1)}, f32[1024,256]{1,0:T(8,128)}, u32[]{:S(2)}) copy-start(f32[1024,256]{1,0:T(8,128)} %cot.1) | copy-start | bytes 3145732
  5.0 17.0 %collective-permute-start.3 = (f32[512,256]{1,0:T(8,128)S(1)}, f32[512,256]{1,0:T(8,128)S(1)}, u32[]{:S(2)}, u32[]{:S(2)}) collective-permute-start(f32[512,256]{1,0:T(8,128)S(1)} %cot_give.1), channel_id=1, source_target_pairs={{0,1},{1,0},{2,3},{3,2},{4,5},{5,4},{6,7},{7,6},{8,9},{9,8},{10,11... | collective-permute-start | bytes 1572872 | tf_op jit(solution)/shard_map/ppermute | solution.py:313
  6.5 24.2 %collective-permute-start.2 = (f32[512,256]{1,0:T(8,128)}, f32[512,256]{1,0:T(8,128)S(1)}, u32[]{:S(2)}, u32[]{:S(2)}) collective-permute-start(f32[512,256]{1,0:T(8,128)} %w_here.3), channel_id=1, source_target_pairs={{0,1},{1,0},{2,3},{3,2},{4,5},{5,4},{6,7},{7,6},{8,9},{9,8},{10,11... | collective-permute-start | bytes 1572872 | tf_op jit(solution)/shard_map/ppermute | solution.py:313
  7.1 29.4 %collective-permute-start = (f32[1024,256]{1,0:T(8,128)}, f32[1024,256]{1,0:T(8,128)S(1)}, u32[]{:S(2)}, u32[]{:S(2)}) collective-permute-start(f32[1024,256]{1,0:T(8,128)} %refs_0_.1), channel_id=1, source_target_pairs={{0,2},{2,8},{4,6},{6,12},{8,10},{10,16},{12,14},{14,20},{16,18},{1... | collective-permute-start | bytes 3145736 | tf_op jit(solution)/shard_map/ppermute | solution.py:307
  7.2 0.7 copy-start.4
  7.9 0.7 copy-start.5
  8.6 0.7 copy-start.6
  17.7 1.2 %copy-start.2 = (f32[1024,256]{1,0:T(8,128)S(1)}, f32[1024,256]{1,0:T(8,128)}, u32[]{:S(2)}) copy-start(f32[1024,256]{1,0:T(8,128)} %refs_0_.1) | copy-start | bytes 3145732
  30.8 3.6 %collective-permute-start.5 = (f32[512,256]{1,0:T(8,128)S(1)}, f32[512,256]{1,0:T(8,128)S(1)}, u32[]{:S(2)}, u32[]{:S(2)}) collective-permute-start(f32[512,256]{1,0:T(8,128)S(1)} %get-tuple-element.77), channel_id=1, source_target_pairs={{0,2},{2,0},{4,6},{6,4},{8,10},{10,8},{12,14},{14,12},{16,18},{18,... | collective-permute-start | bytes 1572872 | tf_op jit(solution)/shard_map/ppermute | solution.py:313
  30.9 3.5 %collective-permute-start.4 = (f32[512,256]{1,0:T(8,128)S(1)}, f32[512,256]{1,0:T(8,128)S(1)}, u32[]{:S(2)}, u32[]{:S(2)}) collective-permute-start(f32[512,256]{1,0:T(8,128)S(1)} %get-tuple-element.78), channel_id=1, source_target_pairs={{0,2},{2,0},{4,6},{6,4},{8,10},{10,8},{12,14},{14,12},{16,18},{18,... | collective-permute-start | bytes 1572872 | tf_op jit(solution)/shard_map/ppermute | solution.py:313
  36.4 15.9 %copy-start.1 = (f32[1024,256]{1,0:T(8,128)S(1)}, f32[1024,256]{1,0:T(8,128)}, u32[]{:S(2)}) copy-start(f32[1024,256]{1,0:T(8,128)} %cot.1) | copy-start | bytes 3145732
  36.4 15.9 %copy-start.3 = (f32[512,256]{1,0:T(8,128)S(1)}, f32[512,256]{1,0:T(8,128)}, u32[]{:S(2)}) copy-start(f32[512,256]{1,0:T(8,128)} %w_here.3) | copy-start | bytes 1572868
  38.3 14.0 %collective-permute-start.6 = (f32[512,256]{1,0:T(8,128)S(1)}, f32[512,256]{1,0:T(8,128)S(1)}, u32[]{:S(2)}, u32[]{:S(2)}) collective-permute-start(f32[512,256]{1,0:T(8,128)S(1)} %agg_give.1), channel_id=1, source_target_pairs={{0,1},{1,0},{2,3},{3,2},{4,5},{5,4},{6,7},{7,6},{8,9},{9,8},{10,11... | collective-permute-start | bytes 1572872 | tf_op jit(solution)/shard_map/ppermute | solution.py:313
  55.8 2.9 %collective-permute-start.7 = (f32[256,512]{1,0:T(8,128)S(1)}, f32[256,512]{1,0:T(8,128)S(1)}, u32[]{:S(2)}, u32[]{:S(2)}) collective-permute-start(f32[256,512]{1,0:T(8,128)S(1)} %weight_give.1), channel_id=1, source_target_pairs={{0,2},{2,0},{4,6},{6,4},{8,10},{10,8},{12,14},{14,12},{16,18},{18,... | collective-permute-start | bytes 1572872 | tf_op jit(solution)/shard_map/ppermute | solution.py:313
  55.9 14.3 %collective-permute-start.8 = (f32[512,256]{1,0:T(8,128)S(1)}, f32[512,256]{1,0:T(8,128)S(1)}, u32[]{:S(2)}, u32[]{:S(2)}) collective-permute-start(f32[512,256]{1,0:T(8,128)S(1)} %get-tuple-element.51), channel_id=1, source_target_pairs={{0,1},{1,0},{2,3},{3,2},{4,5},{5,4},{6,7},{7,6},{8,9},{9,8},{10,11... | collective-permute-start | bytes 1572872 | tf_op jit(solution)/shard_map/ppermute | solution.py:313
  59.4 14.0 %collective-permute-start.9 = (f32[256,256]{1,0:T(8,128)S(1)}, f32[256,256]{1,0:T(8,128)S(1)}, u32[]{:S(2)}, u32[]{:S(2)}) collective-permute-start(f32[256,256]{1,0:T(8,128)S(1)} %get-tuple-element.59.refs_0_), channel_id=1, source_target_pairs={{0,4},{2,6},{8,12},{10,14},{16,20},{18,22},{24,28},{26,30},{1,5},{... | collective-permute-start | bytes 786440 | tf_op jit(solution)/shard_map/ppermute | solution.py:313
  73.9 9.2 %collective-permute-start.10 = (f32[1024,256]{1,0:T(8,128)S(1)}, f32[1024,256]{1,0:T(8,128)S(1)}, u32[]{:S(2)}, u32[]{:S(2)}) collective-permute-start(f32[1024,256]{1,0:T(8,128)S(1)} %back_two.1), channel_id=1, source_target_pairs={{0,2},{2,0},{4,6},{6,4},{8,10},{10,8},{12,14},{14,12},{16,18},{18,... | collective-permute-start | bytes 3145736 | tf_op jit(solution)/shard_map/ppermute | solution.py:313
  74.0 20.1 %collective-permute-start.13 = (f32[1024,256]{1,0:T(8,128)S(1)}, f32[1024,256]{1,0:T(8,128)S(1)}, u32[]{:S(2)}, u32[]{:S(2)}) collective-permute-start(f32[1024,256]{1,0:T(8,128)S(1)} %back_far.1), channel_id=1, source_target_pairs={{0,26},{2,0},{4,30},{6,4},{8,2},{10,8},{12,6},{14,12},{16,10},{18,... | collective-permute-start | bytes 3145736 | tf_op jit(solution)/shard_map/ppermute | solution.py:307
  77.7 7.8 %collective-permute-start.11 = (f32[256,256]{1,0:T(8,128)S(1)}, f32[256,256]{1,0:T(8,128)S(1)}, u32[]{:S(2)}, u32[]{:S(2)}) collective-permute-start(f32[256,256]{1,0:T(8,128)S(1)} %get-tuple-element.63.one), channel_id=1, source_target_pairs={{0,4},{2,6},{8,12},{10,14},{16,20},{18,22},{24,28},{26,30},{1,5},{... | collective-permute-start | bytes 786440 | tf_op jit(solution)/shard_map/ppermute | solution.py:313
  81.4 6.4 %collective-permute-start.12 = (f32[256,256]{1,0:T(8,128)S(1)}, f32[256,256]{1,0:T(8,128)S(1)}, u32[]{:S(2)}, u32[]{:S(2)}) collective-permute-start(f32[256,256]{1,0:T(8,128)S(1)} %chip_there.1), channel_id=1, source_target_pairs={{0,1},{1,0},{2,3},{3,2},{4,5},{5,4},{6,7},{7,6},{8,9},{9,8},{10,11... | collective-permute-start | bytes 786440 | tf_op jit(solution)/shard_map/ppermute | solution.py:313
  84.7 30.9 %collective-permute-start.20 = (f32[1024,256]{1,0:T(8,128)S(1)}, f32[1024,256]{1,0:T(8,128)S(1)}, u32[]{:S(2)}, u32[]{:S(2)}) collective-permute-start(f32[1024,256]{1,0:T(8,128)S(1)} %back_near.1), channel_id=1, source_target_pairs={{0,30},{2,28},{4,2},{6,0},{8,6},{10,4},{12,10},{14,8},{16,14},{18,... | collective-permute-start | bytes 3145736 | tf_op jit(solution)/shard_map/ppermute | solution.py:307
  88.4 11.6 %collective-permute-start.16 = (f32[512,256]{1,0:T(8,128)S(1)}, f32[512,256]{1,0:T(8,128)S(1)}, u32[]{:S(2)}, u32[]{:S(2)}) collective-permute-start(f32[512,256]{1,0:T(8,128)S(1)} %get-tuple-element.73), channel_id=1, source_target_pairs={{0,1},{1,0},{2,3},{3,2},{4,5},{5,4},{6,7},{7,6},{8,9},{9,8},{10,11... | collective-permute-start | bytes 1572872 | tf_op jit(solution)/shard_map/ppermute | solution.py:313
  90.2 3.9 %collective-permute-start.14 = (f32[128,256]{1,0:T(8,128)S(1)}, f32[128,256]{1,0:T(8,128)S(1)}, u32[]{:S(2)}, u32[]{:S(2)}) collective-permute-start(f32[128,256]{1,0:T(8,128)S(1)} %get-tuple-element.65), channel_id=1, source_target_pairs={{4,12},{6,14},{12,4},{14,6},{20,28},{22,30},{28,20},{30,22},{5,13}... | collective-permute-start | bytes 393224 | tf_op jit(solution)/shard_map/ppermute | solution.py:313
  94.7 0.7 collective-permute-start.15
  95.9 18.9 %collective-permute-start.19 = (f32[128,256]{1,0:T(8,128)S(1)}, f32[128,256]{1,0:T(8,128)S(1)}, u32[]{:S(2)}, u32[]{:S(2)}) collective-permute-start(f32[128,256]{1,0:T(8,128)S(1)} %pair_sum.1.ready), channel_id=1, source_target_pairs={{4,8},{6,10},{12,0},{14,2},{20,24},{22,26},{28,16},{30,18},{5,9},{... | collective-permute-start | bytes 393224 | tf_op jit(solution)/shard_map/ppermute | solution.py:313
  97.2 17.7 %collective-permute-start.18 = (f32[128,256]{1,0:T(8,128)S(1)}, f32[128,256]{1,0:T(8,128)S(1)}, u32[]{:S(2)}, u32[]{:S(2)}) collective-permute-start(f32[128,256]{1,0:T(8,128)S(1)} %pair_sum.1.ready), channel_id=1, source_target_pairs={{4,0},{6,2},{12,8},{14,10},{20,16},{22,18},{28,24},{30,26},{5,1},{... | collective-permute-start | bytes 393224 | tf_op jit(solution)/shard_map/ppermute | solution.py:313
  98.5 16.5 %collective-permute-start.17 = (f32[128,256]{1,0:T(8,128)S(1)}, f32[128,256]{1,0:T(8,128)S(1)}, u32[]{:S(2)}, u32[]{:S(2)}) collective-permute-start(f32[128,256]{1,0:T(8,128)S(1)} %pair_sum.1.ready), channel_id=1, source_target_pairs={{4,12},{6,14},{12,4},{14,6},{20,28},{22,30},{28,20},{30,22},{5,13}... | collective-permute-start | bytes 393224 | tf_op jit(solution)/shard_map/ppermute | solution.py:313
  115.6 1.8 %collective-permute-start.21 = (f32[256,256]{1,0:T(8,128)S(1)}, f32[256,256]{1,0:T(8,128)S(1)}, u32[]{:S(2)}, u32[]{:S(2)}) collective-permute-start(f32[256,256]{1,0:T(8,128)S(1)} %chip_pick.1.refs_0_), channel_id=1, source_target_pairs={{0,2},{2,0},{4,6},{6,4},{8,10},{10,8},{12,14},{14,12},{16,18},{18,... | collective-permute-start | bytes 786440 | tf_op jit(solution)/shard_map/ppermute | solution.py:313
